TPU v7x, 32 devices: a whole 2x2x4 slice. The times are simulated.
32 devices in a mesh: group: 2 (over y), node: 4 (over z), local: 4 (over x, core).
Axes of the slice: x: 2, y: 2, z: 4, core: 2. Of those that a mesh axis runs over, the one named last changes fastest.
Arguments:
- attended: bfloat16 [256, 5120], P(('group', 'node'), 'local'), parts along dimension 0, may hold values from -6 to 6
- norm_gain: float32 [5120], replicated, may hold values from 0.5 to 1.5
- node_ids: int32 [256, 2], P(('group', 'node', 'local')), parts along dimension 0, may hold values from 0 to 3, as said below
- gates: bfloat16 [256, 2, 2], P(('group', 'node', 'local')), parts along dimension 0, may hold values from 0.099609375 to 0.796875
- w_gate: bfloat16 [8, 5120, 2048], P('node', None, 'local'), may hold values from -0.078125 to 0.078125
- w_up: bfloat16 [8, 5120, 2048], P('node', None, 'local'), may hold values from -0.078125 to 0.078125
- w_down: bfloat16 [8, 2048, 5120], P('node', 'local'), may hold values from -0.25 to 0.25
- s_gate: bfloat16 [5120, 1024], P(None, 'local'), may hold values from -0.078125 to 0.078125
- s_up: bfloat16 [5120, 1024], P(None, 'local'), may hold values from -0.078125 to 0.078125
- s_down: bfloat16 [1024, 5120], P('local'), may hold values from -0.375 to 0.375
Outputs:
- mixed: bfloat16 [256, 5120], P(('group', 'node', 'local')), parts along dimension 0
There are 2 independent parts, one for each index of `group`. A program takes and returns all parts, laid end to end along the dimension named above; an argument that names none is the same for every part. Nothing has to cross between parts.
Inputs may be any that keep to these rules, and one draw needn't show every extreme that they name: `node_ids`: each token's 2 node ids are distinct. Among the 8 tokens of one device no node is named by more than 6 tokens, and in every draw some node is named by exactly 6 tokens of every device.
All inputs are finite; a program needn't handle non-finite values.
Results may differ from a plain program's by a relative error of at most 0.0085.
Values may be sent and summed in bfloat16 or wider, within the bound.
No kernel may reach another device: no remote copies, remote signals or barrier semaphores. Data moves between devices by JAX's collectives and lax.ppermute only.
A program may use at most 128 MiB of HBM per device.

v0:
```python
import jax
import jax.numpy as jnp
from jax import lax
from jax.sharding import PartitionSpec as P


def selection(node_rows, nodes, capacity):
    tok_count, pick_count = node_rows.shape
    node_hits = (node_rows[:, :, None] == jnp.arange(nodes, dtype=jnp.int32)).astype(jnp.int32)
    flat_hits = node_hits.reshape(tok_count * pick_count, nodes)
    earlier = jnp.cumsum(flat_hits, axis=0) - flat_hits
    slot_index = jnp.sum(earlier * flat_hits, axis=1).reshape(tok_count, pick_count)
    slot_key = node_rows * capacity + slot_index
    slots = jnp.arange(nodes * capacity, dtype=jnp.int32)
    return (slot_key[None, :, :] == slots[:, None, None]).astype(jnp.float32)


def expert_term(token_rows, row_gates, w_gate, w_up, w_down):
    running = jnp.zeros((token_rows.shape[0], w_down.shape[2]), jnp.float32)
    for expert in range(w_gate.shape[0]):
        gate_proj = jnp.dot(token_rows, w_gate[expert], preferred_element_type=jnp.float32)
        up_proj = jnp.dot(token_rows, w_up[expert], preferred_element_type=jnp.float32)
        hidden = (jax.nn.silu(gate_proj) * up_proj).astype(jnp.bfloat16)
        weight = row_gates[:, expert : expert + 1].astype(jnp.float32)
        running = running + weight * jnp.dot(
            hidden, w_down[expert], preferred_element_type=jnp.float32
        )
    return running


def on_device(attended, norm_gain, node_ids, gates, w_gate, w_up, w_down, s_gate, s_up, s_down):
    node_count = lax.axis_size("node")
    local_count = lax.axis_size("local")
    token_rows = lax.all_to_all(attended, "local", split_axis=0, concat_axis=1, tiled=True)
    tok_count, width = token_rows.shape
    pick_count = node_ids.shape[1]
    experts_here = w_gate.shape[0]
    capacity = tok_count * pick_count // node_count + 2
    residual = token_rows.astype(jnp.float32)
    inv_scale = lax.rsqrt(jnp.mean(residual * residual, axis=1, keepdims=True) + 1e-06)
    normed = (residual * inv_scale * norm_gain).astype(jnp.bfloat16)
    node_tokens = lax.all_gather(normed, "local", axis=0, tiled=True)
    shared_gate = jnp.dot(node_tokens, s_gate, preferred_element_type=jnp.float32)
    shared_up = jnp.dot(node_tokens, s_up, preferred_element_type=jnp.float32)
    shared_hidden = (jax.nn.silu(shared_gate) * shared_up).astype(jnp.bfloat16)
    shared = lax.psum_scatter(
        jnp.dot(shared_hidden, s_down, preferred_element_type=jnp.float32).astype(jnp.bfloat16),
        "local",
        scatter_dimension=0,
        tiled=True,
    ).astype(jnp.float32)
    matches = selection(node_ids, node_count, capacity)
    selector = matches.sum(axis=2)
    send_rows = jnp.dot(
        selector.astype(jnp.bfloat16), normed, preferred_element_type=jnp.float32
    ).astype(jnp.bfloat16)
    send_gates = jnp.einsum(
        "stk,tkj->sj", matches, gates.astype(jnp.float32), precision=lax.Precision.HIGHEST
    ).astype(jnp.bfloat16)
    slot_total = node_count * capacity
    fan_rows = jnp.broadcast_to(
        send_rows.reshape(node_count, 1, capacity, width),
        (node_count, local_count, capacity, width),
    )
    fan_gates = jnp.broadcast_to(
        send_gates.reshape(node_count, 1, capacity, experts_here),
        (node_count, local_count, capacity, experts_here),
    )
    got_rows, got_gates = (
        lax.all_to_all(
            fan_rows.reshape(node_count * local_count, capacity, width),
            ("node", "local"),
            split_axis=0,
            concat_axis=0,
            tiled=True,
        ),
        lax.all_to_all(
            fan_gates.reshape(node_count * local_count, capacity, experts_here),
            ("node", "local"),
            split_axis=0,
            concat_axis=0,
            tiled=True,
        ),
    )
    partial_term = expert_term(
        got_rows.reshape(-1, width), got_gates.reshape(-1, experts_here), w_gate, w_up, w_down
    ).astype(jnp.bfloat16)
    partials = lax.all_to_all(
        partial_term.reshape(node_count * local_count, capacity, width),
        ("node", "local"),
        split_axis=0,
        concat_axis=0,
        tiled=True,
    )
    returned = (
        partials.reshape(node_count, local_count, capacity, width).astype(jnp.float32).sum(axis=1)
    )
    returned = returned.reshape(slot_total, width)
    routed = jnp.dot(
        selector.T, returned, precision=lax.Precision.HIGHEST, preferred_element_type=jnp.float32
    )
    return (residual + routed + shared).astype(jnp.bfloat16)


def solution(mesh):
    in_specs = (
        P(("group", "node"), "local"),
        P(),
        P(("group", "node", "local"), None),
        P(("group", "node", "local"), None, None),
        P("node", None, "local"),
        P("node", None, "local"),
        P("node", "local", None),
        P(None, "local"),
        P(None, "local"),
        P("local", None),
    )
    out_specs = P(("group", "node", "local"), None)
    return jax.shard_map(
        on_device, mesh=mesh, in_specs=in_specs, out_specs=out_specs, check_vma=False
    )
```

profile of v0, /device:TPU:0, one launch (start us, length us, event | category | flops | bytes accessed | tf_op | source)
XLA Modules:
  0.0 146.0 jit_solution(880478850347103910)
XLA Ops:
  6.5 4.5 %all-to-all-start = ((bf16[4,8,1280]{2,1,0:T(8,128)(2,1)}), bf16[4,8,1280]{2,1,0:T(8,128)(2,1)S(1)}, u32[]{:S(2)}, u32[]{:S(2)}) async-start(bf16[4,8,1280]{2,1,0:T(8,128)(2,1)} %bitcast.69), calls=%async_computation | async-start | bytes 163840 | tf_op jit(solution)/shard_map/all_to_all | solution.py:34
  11.0 0.8 copy.17
  12.0 0.2 select_reduce_fusion
  12.3 0.9 fusion.33
  13.2 0.1 broadcast_in_dim.8
  13.4 1.9 %all-to-all-done = bf16[4,8,1280]{2,1,0:T(8,128)(2,1)S(1)} async-done(((bf16[4,8,1280]{2,1,0:T(8,128)(2,1)}), bf16[4,8,1280]{2,1,0:T(8,128)(2,1)S(1)}, u32[]{:S(2)}, u32[]{:S(2)}) %all-to-all-start) | async-done | bytes 81952 | tf_op jit(solution)/shard_map/all_to_all | solution.py:34
  15.2 0.6 broadcast_in_dim.9
  15.8 5.5 %all-to-all-start.1 = ((bf16[16,6,2]{1,2,0:T(2,128)(2,1)}), bf16[16,6,2]{1,2,0:T(2,128)(2,1)S(1)}, u32[]{:S(2)}, u32[]{:S(2)}) async-start(bf16[16,6,2]{1,2,0:T(2,128)(2,1)} %bitcast.4), calls=%async_computation.1 | async-start | bytes 16384 | tf_op jit(solution)/shard_map/all_to_all | solution.py:77
  21.3 0.2 multiply_reduce_fusion
  21.5 0.8 multiply_convert_fusion
  22.3 0.3 convolution_convert_fusion.1
  22.6 0.1 broadcast_in_dim.10
  22.7 5.0 %all-to-all-done.1 = bf16[16,6,2]{1,2,0:T(2,128)(2,1)S(1)} async-done(((bf16[16,6,2]{1,2,0:T(2,128)(2,1)}), bf16[16,6,2]{1,2,0:T(2,128)(2,1)S(1)}, u32[]{:S(2)}, u32[]{:S(2)}) %all-to-all-start.1) | async-done | bytes 416 | tf_op jit(solution)/shard_map/all_to_all | solution.py:77
  27.7 1.2 broadcast_in_dim.11
  28.9 4.4 %all-to-all-start.2 = ((bf16[16,6,5120]{2,1,0:T(8,128)(2,1)}), bf16[16,6,5120]{2,1,0:T(8,128)(2,1)}, u32[]{:S(2)}, u32[]{:S(2)}) async-start(bf16[16,6,5120]{2,1,0:T(8,128)(2,1)} %bitcast.66), calls=%async_computation.2 | async-start | bytes 2621440 | tf_op jit(solution)/shard_map/all_to_all | solution.py:70
  33.3 0.1 reshape.49
  33.4 27.3 %all-to-all-done.2 = bf16[16,6,5120]{2,1,0:T(8,128)(2,1)} async-done(((bf16[16,6,5120]{2,1,0:T(8,128)(2,1)}), bf16[16,6,5120]{2,1,0:T(8,128)(2,1)}, u32[]{:S(2)}, u32[]{:S(2)}) %all-to-all-start.2) | async-done | bytes 983072 | tf_op jit(solution)/shard_map/all_to_all | solution.py:70
  60.6 2.2 %reshape.51 = bf16[96,5120]{1,0:T(8,128)(2,1)} reshape(bf16[16,6,5120]{2,1,0:T(8,128)(2,1)} %all-to-all-done.2) | data formatting | bytes 1966080 | tf_op jit(solution)/shard_map/reshape | solution.py:86
  62.9 3.8 %fusion.7 = f32[96,512]{1,0:T(8,128)S(1)} fusion(bf16[96,5120]{1,0:T(8,128)(2,1)} %reshape.51, bf16[2,5120,512]{2,1,0:T(8,128)(2,1)} %param.14), kind=kOutput, calls=%fused_computation.12 | convolution fusion | flops 503316480 | bytes 6422528 | tf_op jit(solution)/shard_map/dot_general | solution.py:21
  66.7 3.4 %fusion.12 = f32[96,512]{1,0:T(8,128)S(1)} fusion(bf16[96,5120]{1,0:T(8,128)(2,1)S(1)} %copy-done.1, bf16[2,5120,512]{2,1,0:T(8,128)(2,1)} %param.14), kind=kOutput, calls=%fused_computation.17 | convolution fusion | flops 503316480 | bytes 6422528 | tf_op jit(solution)/shard_map/dot_general | solution.py:21
  70.2 7.5 %convolution_multiply_fusion.1 = f32[96,5120]{1,0:T(8,128)} fusion(bf16[2,512,5120]{2,1,0:T(8,128)(2,1)} %param.16, f32[96]{0:T(128)S(1)} %get-tuple-element.6, bf16[96,5120]{1,0:T(8,128)(2,1)} %reshape.51, bf16[2,5120,512]{2,1,0:T(8,128)(2,1)} %param.15, f32[96,512]{1,0:T(8,128)S(1)} %fusion.12), kind=kOutput, calls=%fused_computation.2 | convolution fusion | flops 1007419392 | bytes 13631872 | tf_op jit(solution)/shard_map/dot_general | solution.py:25
  77.7 7.7 %fusion.1 = bf16[96,5120]{1,0:T(8,128)(2,1)} fusion(f32[96,5120]{1,0:T(8,128)} %convolution_multiply_fusion.1, bf16[2,512,5120]{2,1,0:T(8,128)(2,1)} %param.16, f32[96]{0:T(128)S(1)} %get-tuple-element.5, bf16[96,5120]{1,0:T(8,128)(2,1)} %reshape.51, bf16[2,5120,512]{2,1,0:T(8,128)(2,1)} %param.15, f32[96,512]{1,0:T(8,128)S(1)} %fusion.7), kind=kOutput, calls=%fused_computation.3 | convolution fusion | flops 1008402432 | bytes 14614912 | tf_op jit(solution)/shard_map/dot_general | solution.py:25
  85.4 2.3 %reshape.52 = bf16[16,6,5120]{2,1,0:T(8,128)(2,1)} reshape(bf16[96,5120]{1,0:T(8,128)(2,1)} %fusion.1) | data formatting | bytes 1966080 | tf_op jit(solution)/shard_map/reshape | solution.py:89
  87.7 8.0 %all-to-all-start.3 = ((bf16[16,6,5120]{2,1,0:T(8,128)(2,1)}), bf16[16,6,5120]{2,1,0:T(8,128)(2,1)}, u32[]{:S(2)}, u32[]{:S(2)}) async-start(bf16[16,6,5120]{2,1,0:T(8,128)(2,1)} %reshape.52), calls=%async_computation.3 | async-start | bytes 2621440 | tf_op jit(solution)/shard_map/all_to_all | solution.py:88
  95.8 13.7 %all_gather.3 = bf16[32,5120]{1,0:T(8,128)(2,1)S(1)} all-gather(bf16[8,5120]{1,0:T(8,128)(2,1)S(1)} %multiply_convert_fusion), channel_id=1, replica_groups=mesh['group'=2,'node'=4,'local'=4] {'local'}, dimensions={0}, use_global_device_ids=true | all-gather | bytes 409600 | tf_op jit(solution)/shard_map/all_gather | solution.py:42
  109.5 2.3 %fusion.62 = f32[32,256]{1,0:T(8,128)S(1)} fusion(bf16[32,5120]{1,0:T(8,128)(2,1)S(1)} %all_gather.3, bf16[5120,256]{1,0:T(8,128)(2,1)} %param.17), kind=kOutput, calls=%fused_computation.68 | convolution fusion | flops 83886080 | bytes 2981888 | tf_op jit(solution)/shard_map/dot_general | solution.py:43
  111.8 4.0 %convolution_convert_fusion = bf16[32,5120]{1,0:T(8,128)(2,1)} fusion(bf16[256,5120]{1,0:T(8,128)(2,1)S(1)} %copy-done, bf16[32,5120]{1,0:T(8,128)(2,1)S(1)} %all_gather.3, bf16[5120,256]{1,0:T(8,128)(2,1)} %param.18, f32[32,256]{1,0:T(8,128)S(1)} %fusion.62), kind=kOutput, calls=%fused_computation.4 | convolution fusion | flops 167985152 | bytes 5931008 | tf_op jit(solution)/shard_map/dot_general | solution.py:47
  115.8 7.4 %all-to-all-done.3 = bf16[16,6,5120]{2,1,0:T(8,128)(2,1)} async-done(((bf16[16,6,5120]{2,1,0:T(8,128)(2,1)}), bf16[16,6,5120]{2,1,0:T(8,128)(2,1)}, u32[]{:S(2)}, u32[]{:S(2)}) %all-to-all-start.3) | async-done | bytes 983072 | tf_op jit(solution)/shard_map/all_to_all | solution.py:88
  123.2 1.7 %convert_reduce_fusion = f32[4,6,5120]{2,1,0:T(8,128)S(1)} fusion(bf16[16,6,5120]{2,1,0:T(8,128)(2,1)} %all-to-all-done.3), kind=kLoop, calls=%fused_computation.25 | loop fusion | flops 860160 | bytes 1474560 | tf_op jit(solution)/shard_map/reduce_sum | solution.py:96
  124.9 0.8 reshape.53
  125.7 11.4 %reduce-scatter.2.cloned.1.call-done = bf16[8,5120]{1,0:T(8,128)(2,1)} async-done(((bf16[32,5120]{1,0:T(8,128)(2,1)}), bf16[8,5120]{1,0:T(8,128)(2,1)}) %reduce-scatter.2.cloned.1.call-update) | async-done | bytes 81936 | tf_op jit(solution)/shard_map/reduce_scatter | solution.py:46
  137.1 2.0 %fusion.3 = bf16[8,5120]{1,0:T(8,128)(2,1)} fusion(f32[8,5120]{1,0:T(8,128)S(1)} %bitcast.68, f32[24,8]{0,1:T(8,128)S(1)} %convert_reduce_fusion.1, f32[24,5120]{1,0:T(8,128)} %reshape.53, bf16[8,5120]{1,0:T(8,128)(2,1)} %reduce-scatter.2.cloned.1.call-done), kind=kOutput, calls=%fused_computation.8 | convolution fusion | flops 11960320 | bytes 819968 | tf_op jit(solution)/shard_map/dot_general | solution.py:99
  (18 shorter events, 0.6 us)
Async XLA Ops:
  6.5 105.2 %copy-start = (bf16[256,5120]{1,0:T(8,128)(2,1)S(1)}, bf16[256,5120]{1,0:T(8,128)(2,1)}, u32[]{:S(2)}) copy-start(bf16[256,5120]{1,0:T(8,128)(2,1)} %param.19) | copy-start | bytes 7864324
  6.5 8.7 %all-to-all-start = ((bf16[4,8,1280]{2,1,0:T(8,128)(2,1)}), bf16[4,8,1280]{2,1,0:T(8,128)(2,1)S(1)}, u32[]{:S(2)}, u32[]{:S(2)}) async-start(bf16[4,8,1280]{2,1,0:T(8,128)(2,1)} %bitcast.69), calls=%async_computation | async-start | bytes 163840 | tf_op jit(solution)/shard_map/all_to_all | solution.py:34
  15.8 11.8 %all-to-all-start.1 = ((bf16[16,6,2]{1,2,0:T(2,128)(2,1)}), bf16[16,6,2]{1,2,0:T(2,128)(2,1)S(1)}, u32[]{:S(2)}, u32[]{:S(2)}) async-start(bf16[16,6,2]{1,2,0:T(2,128)(2,1)} %bitcast.4), calls=%async_computation.1 | async-start | bytes 16384 | tf_op jit(solution)/shard_map/all_to_all | solution.py:77
  28.9 31.8 %all-to-all-start.2 = ((bf16[16,6,5120]{2,1,0:T(8,128)(2,1)}), bf16[16,6,5120]{2,1,0:T(8,128)(2,1)}, u32[]{:S(2)}, u32[]{:S(2)}) async-start(bf16[16,6,5120]{2,1,0:T(8,128)(2,1)} %bitcast.66), calls=%async_computation.2 | async-start | bytes 2621440 | tf_op jit(solution)/shard_map/all_to_all | solution.py:70
  62.9 3.8 %copy-start.1 = (bf16[96,5120]{1,0:T(8,128)(2,1)S(1)}, bf16[96,5120]{1,0:T(8,128)(2,1)}, u32[]{:S(2)}) copy-start(bf16[96,5120]{1,0:T(8,128)(2,1)} %reshape.51) | copy-start | bytes 2949124
  87.7 35.5 %all-to-all-start.3 = ((bf16[16,6,5120]{2,1,0:T(8,128)(2,1)}), bf16[16,6,5120]{2,1,0:T(8,128)(2,1)}, u32[]{:S(2)}, u32[]{:S(2)}) async-start(bf16[16,6,5120]{2,1,0:T(8,128)(2,1)} %reshape.52), calls=%async_computation.3 | async-start | bytes 2621440 | tf_op jit(solution)/shard_map/all_to_all | solution.py:88
  95.7 41.4 %reduce-scatter.2.cloned.1.call-start = ((), (), s32[]{:S(2)}) async-start(), calls=%async_computation.5 | async-start | bytes 409600 | tf_op jit(solution)/shard_map/reduce_scatter | solution.py:46
Sparse Core Ops, SparseCore 0:
  115.9 21.1 reduce-scatter.1
where the time goes:
time: 147 us; the launch traced here: 146 us
  waiting for transfers between devices  52.9 us (36%)
  matrix products  32 us (22%)
  starting transfers between devices  22.4 us (15%)
  blocking collectives  13.7 us (9%)
  between operations  13.5 us (9%)
  local copies, waits for them, and re-layouts  8.45 us (6%)
  other arithmetic  3.06 us (2%)
    all_to_all x1, waiting for transfers between devices, on_device(): lax.all_to_all(fan_rows.reshape(node_count * local_count, capacity, width...  27.3 us
    dot_general x2, matrix products, expert_term(): jnp.dot(hidden, w_down[expert], preferred_element_type=jnp.float32)  15.3 us
    all_gather x1, blocking collectives, on_device(): node_tokens = lax.all_gather(normed, 'local', axis=0, tiled=True)  13.7 us
    reduce_scatter x1, waiting for transfers between devices, on_device(): lax.psum_scatter(jnp.dot(shared_hidden, s_down, preferred_element_type=jn...  11.4 us
    all_to_all x1, starting transfers between devices, on_device(): lax.all_to_all(partial_term.reshape(node_count * local_count, capacity, w...  8.03 us
    all_to_all x1, waiting for transfers between devices, on_device(): lax.all_to_all(partial_term.reshape(node_count * local_count, capacity, w...  7.37 us
    dot_general x2, matrix products, expert_term(): jnp.dot(token_rows, w_gate[expert], preferred_element_type=jnp.float32)  7.25 us
    all_to_all x1, starting transfers between devices, on_device(): lax.all_to_all(fan_gates.reshape(node_count * local_count, capacity, expe...  5.49 us
  transfers between devices with their start and end apart: 5, of which 5 were waited for; matrix products, arithmetic and copies ran while one was open for 9% of the time, Pallas kernels for 0%

commit v1 on v0

v1 whole, which is shorter than its diff:
```python
import functools

import jax
import jax.numpy as jnp
from jax import lax
from jax.experimental import pallas as pl
from jax.experimental.pallas import tpu as pltpu
from jax.sharding import PartitionSpec as P

ROWS = 128
CORES = 2
VMEM_BYTES = 14 * 2**20


def swap(x, axis, offset):
    size = lax.axis_size(axis)
    return lax.ppermute(x, axis, [(i, i ^ offset) for i in range(size)])


def resident(x):
    return pltpu.with_memory_space_constraint(x, pltpu.VMEM)


def row_loop(total, body):
    block = min(ROWS, total)
    if total == block:
        body(pl.ds(0, block))
        return

    @pl.loop(0, total // block)
    def _(index):
        body(pl.ds(pl.multiple_of(index * block, block), block))


def project(chunk_ref, gain_ref, weights, shared_weights, sums_in, sums, part):
    total, depth = chunk_ref.shape
    acc_ref, shared_ref, square_ref = sums
    start = pl.multiple_of(part * depth, depth)
    gain = gain_ref[part]
    inner = weights[0].shape[2]
    shared_inner = shared_weights[0].shape[1]

    def scaled(rows):
        values = chunk_ref[rows, :].astype(jnp.float32)
        return values, (values * gain).astype(jnp.bfloat16)

    def body(rows):
        values, lhs = scaled(rows)
        square = jnp.sum(values * values, axis=1, keepdims=True)
        square = jnp.broadcast_to(square, (square.shape[0], square_ref.shape[1]))
        if sums_in is not None:
            square = square + sums_in[2][rows, :]
        square_ref[rows, :] = square
        for expert in range(weights[0].shape[0]):
            for which, weight in enumerate(weights):
                column = (expert * 2 + which) * inner
                term = jnp.dot(
                    lhs,
                    weight[expert, pl.ds(start, depth), :],
                    preferred_element_type=jnp.float32,
                )
                if sums_in is not None:
                    term = term + sums_in[0][rows, column : column + inner]
                acc_ref[rows, column : column + inner] = term

    row_loop(total, body)
    own = shared_ref.shape[0]
    _, lhs = scaled(pl.ds(0, own))
    for which, weight in enumerate(shared_weights):
        column = which * shared_inner
        term = jnp.dot(
            lhs, weight[pl.ds(start, depth), :], preferred_element_type=jnp.float32
        )
        if sums_in is not None:
            term = term + sums_in[1][:, column : column + shared_inner]
        shared_ref[:, column : column + shared_inner] = term


def project_kernel(first, part_ref, chunk_ref, gain_ref, gate, up, s_gate, s_up, *refs):
    sums_in, sums = (None, refs) if first else (refs[:3], refs[3:])
    project(chunk_ref, gain_ref, (gate, up), (s_gate, s_up), sums_in, sums, part_ref[0])


def act(gate, up):
    return gate / (1.0 + jnp.exp(-gate)) * up


def hidden_kernel(
    width, pick, place_ref, chunk_ref, gain_ref, gate, up, s_gate, s_up,
    acc_in, shared_in, square_in, *refs
):
    *tags, hidden_ref, shared_hidden_ref, acc_ref, shared_ref, square_ref, weight_ref = refs
    part, me, node = place_ref[0], place_ref[1], place_ref[2]
    project(
        chunk_ref, gain_ref, (gate, up), (s_gate, s_up), (acc_in, shared_in, square_in),
        (acc_ref, shared_ref, square_ref), part,
    )
    experts, inner = gate.shape[0], gate.shape[2]
    total = chunk_ref.shape[0]
    own = shared_ref.shape[0]
    nodes, tokens = tags[0].shape[0], tags[0].shape[1]
    for offset, tag_ref in enumerate(tags):
        place = lax.bitwise_xor(me, offset) * tokens
        for other in range(nodes):
            tag = tag_ref[other].astype(jnp.float32)
            for expert in range(experts):
                weight = jnp.zeros((tokens, 1), jnp.float32)
                for k in range(pick):
                    column = pick + k * experts + expert
                    weight = weight + jnp.where(
                        tag[:, k : k + 1] == node.astype(jnp.float32),
                        tag[:, column : column + 1],
                        0.0,
                    )
                rows = pl.ds(pl.multiple_of(other * own + place, tokens), tokens)
                weight_ref[expert, rows, :] = jnp.broadcast_to(weight, (tokens, weight_ref.shape[2]))

    def body(rows):
        scale = lax.rsqrt(square_ref[rows, :][:, :1] / width + 1e-06)
        for expert in range(experts):
            column = expert * 2 * inner
            gate_proj = acc_ref[rows, column : column + inner] * scale
            up_proj = acc_ref[rows, column + inner : column + 2 * inner] * scale
            weight = weight_ref[expert, rows, :][:, :1]
            hidden_ref[rows, expert * inner : (expert + 1) * inner] = (
                act(gate_proj, up_proj) * weight
            ).astype(jnp.bfloat16)

    row_loop(total, body)
    shared_inner = s_gate.shape[1]
    scale = lax.rsqrt(square_ref[:own, :][:, :1] / width + 1e-06)
    gate_proj = shared_ref[:, :shared_inner] * scale
    up_proj = shared_ref[:, shared_inner:] * scale
    shared_hidden_ref[...] = act(gate_proj, up_proj).astype(jnp.bfloat16)


def down_kernel(
    columns, place_ref, hidden_ref, shared_hidden_ref, down, s_down, keep_ref, send_ref, out_ref
):
    me = place_ref[1]
    experts, inner = down.shape[0], down.shape[1]
    total, own = hidden_ref.shape[0], shared_hidden_ref.shape[0]

    def body(rows):
        term = None
        for expert in range(experts):
            more = jnp.dot(
                hidden_ref[rows, expert * inner : (expert + 1) * inner],
                down[expert, :, columns],
                preferred_element_type=jnp.float32,
            )
            term = more if term is None else term + more
        out_ref[rows, :] = term

    row_loop(total, body)
    out_ref[:own, :] += jnp.dot(
        shared_hidden_ref[...], s_down[:, columns], preferred_element_type=jnp.float32
    )
    pairs, nodes, tokens = keep_ref.shape[:3]
    for pair in range(pairs):
        for side, to_ref in enumerate((keep_ref, send_ref)):
            place = lax.bitwise_xor(me, pair * CORES + side) * tokens
            for other in range(nodes):
                rows = pl.ds(pl.multiple_of(other * own + place, tokens), tokens)
                to_ref[pair, other] = out_ref[rows, :].astype(to_ref.dtype)


def call(kernel, name, flops, read, out_shape, in_specs, scratch=(), aliases=None):
    return pl.pallas_call(
        kernel,
        out_shape=out_shape,
        in_specs=in_specs,
        out_specs=jax.tree.map(lambda _: pl.BlockSpec(memory_space=pltpu.VMEM), out_shape),
        scratch_shapes=list(scratch),
        input_output_aliases=aliases or {},
        compiler_params=pltpu.CompilerParams(vmem_limit_bytes=VMEM_BYTES),
        cost_estimate=pl.CostEstimate(flops=flops, bytes_accessed=read, transcendentals=0),
        name=name,
    )


def on_device(attended, norm_gain, node_ids, gates, w_gate, w_up, w_down, s_gate, s_up, s_down):
    node_count = lax.axis_size("node")
    local_count = lax.axis_size("local")
    pairs = local_count // CORES
    node, me = lax.axis_index("node"), lax.axis_index("local")
    own, depth = attended.shape
    tokens, pick = node_ids.shape
    experts, width, inner = w_gate.shape
    shared_inner = s_gate.shape[1]
    total = node_count * own
    smem = pl.BlockSpec(memory_space=pltpu.SMEM)
    vmem = pl.BlockSpec(memory_space=pltpu.VMEM)

    tag = jnp.concatenate(
        [node_ids.astype(jnp.bfloat16), gates.reshape(tokens, pick * experts)], axis=1
    )
    tag = jnp.pad(tag, ((0, 0), (0, 128 - tag.shape[1])))

    def gather_nodes(x):
        return jnp.concatenate([x] + [swap(x, "node", k) for k in range(1, node_count)], axis=0)

    def gather_local(x):
        columns = [x] + [swap(x, "local", k * CORES) for k in range(1, pairs)]
        return [y for column in columns for y in (column, swap(column, "local", 1))]

    chunks = gather_local(gather_nodes(attended))
    tags = gather_local(gather_nodes(tag[None]))

    gain = norm_gain.reshape(local_count, 1, depth)
    up_weights = tuple(resident(w) for w in (w_gate, w_up, s_gate, s_up))
    down_weights = tuple(resident(w) for w in (w_down, s_down))
    sums_shape = [
        jax.ShapeDtypeStruct((total, experts * 2 * inner), jnp.float32),
        jax.ShapeDtypeStruct((own, 2 * shared_inner), jnp.float32),
        jax.ShapeDtypeStruct((total, 128), jnp.float32),
    ]
    flops = 2 * depth * (total * experts * 2 * inner + own * 2 * shared_inner)
    read = 2 * depth * (experts * 2 * inner + 2 * shared_inner)
    sums = None
    for offset, chunk in enumerate(chunks[:-1]):
        part = lax.bitwise_xor(me, offset)[None]
        first = sums is None
        sums = call(
            functools.partial(project_kernel, first),
            "project",
            flops,
            read,
            sums_shape,
            [smem] + [vmem] * (6 if first else 9),
            aliases={} if first else {7: 0, 8: 1, 9: 2},
        )(part, chunk, gain, *up_weights, *(() if first else sums))
    place = jnp.stack([lax.bitwise_xor(me, local_count - 1), me, node])
    hidden, shared_hidden = call(
        functools.partial(hidden_kernel, width, pick),
        "hidden",
        flops,
        read,
        [
            jax.ShapeDtypeStruct((total, experts * inner), jnp.bfloat16),
            jax.ShapeDtypeStruct((own, shared_inner), jnp.bfloat16),
        ],
        [smem] + [vmem] * (9 + local_count),
        scratch=[pltpu.VMEM(s.shape, s.dtype) for s in sums_shape]
        + [pltpu.VMEM((experts, total, 128), jnp.float32)],
    )(place, chunks[-1], gain, *up_weights, *sums, *tags)

    slices = max(1, total // ROWS)
    step = width // slices
    results = []
    for index in range(slices):
        shape = (pairs, node_count, tokens, step)
        keep, send = call(
            functools.partial(down_kernel, slice(index * step, (index + 1) * step)),
            "down",
            2 * step * (total * experts * inner + own * shared_inner),
            2 * step * (experts * inner + shared_inner),
            [jax.ShapeDtypeStruct(shape, jnp.float32), jax.ShapeDtypeStruct(shape, jnp.bfloat16)],
            [smem] + [vmem] * 4,
            scratch=[pltpu.VMEM((total, step), jnp.float32)],
        )(place, hidden, shared_hidden, *down_weights)
        mine = keep + swap(send, "local", 1).astype(jnp.float32)
        result = mine[0]
        for k in range(1, pairs):
            result = result + swap(mine[k].astype(jnp.bfloat16), "local", k * CORES).astype(jnp.float32)
        total_here = result[0]
        for k in range(1, node_count):
            total_here = total_here + swap(result[k].astype(jnp.bfloat16), "node", k).astype(jnp.float32)
        results.append(total_here)
    mixed = jnp.concatenate(results, axis=1)

    rows = jnp.stack([lax.dynamic_slice_in_dim(c, me * tokens, tokens, 0) for c in chunks])
    bit = 1
    while bit < local_count:
        flipped = rows.reshape(local_count // (2 * bit), 2, bit, tokens, depth)[:, ::-1]
        rows = jnp.where((me & bit) != 0, flipped.reshape(rows.shape), rows)
        bit *= 2
    residual = rows.transpose(1, 0, 2).reshape(tokens, width).astype(jnp.float32)
    return (residual + mixed).astype(jnp.bfloat16)


def solution(mesh):
    in_specs = (
        P(("group", "node"), "local"),
        P(),
        P(("group", "node", "local"), None),
        P(("group", "node", "local"), None, None),
        P("node", None, "local"),
        P("node", None, "local"),
        P("node", "local", None),
        P(None, "local"),
        P(None, "local"),
        P("local", None),
    )
    out_specs = P(("group", "node", "local"), None)
    return jax.shard_map(
        on_device, mesh=mesh, in_specs=in_specs, out_specs=out_specs, check_vma=False
    )
```

time: 147 us -> 79.4 us (0.54)
  waiting for transfers between devices: 52.9 us -> 19.3 us
  matrix products: 32 us -> 0 us
  local copies, waits for them, and re-layouts: 8.45 us -> 28.1 us
  blocking collectives: 13.7 us -> 0 us
  between operations: 13.5 us -> 0.2 us
  Pallas kernels: 0 us -> 9.79 us
  starting transfers between devices: 22.4 us -> 19.7 us
    all_to_all x4 -> x0, waiting for transfers between devices: 41.5 us -> none  [the longest x1 27.3 us: on_device(): lax.all_to_all(fan_rows.reshape(node_count * local_count, capacity, width...]
    dot_general x9 -> x0, matrix products: 32 us -> none  [the longest x2 15.3 us: expert_term(): jnp.dot(hidden, w_down[expert], preferred_element_type=jnp.float32)]
    unnamed x5 -> x35, local copies, waits for them, and re-layouts: 0.77 us -> 25.7 us
    all_to_all x4 -> x0, starting transfers between devices: 22.4 us -> none  [the longest x1 8.03 us: on_device(): lax.all_to_all(partial_term.reshape(node_count * local_count, capacity, w...]
    ppermute x0 -> x17, starting transfers between devices: none -> 19.7 us  [swap(): return lax.ppermute(x, axis, [(i, i ^ offset) for i in range(size)])]
    ppermute x0 -> x17, waiting for transfers between devices: none -> 19.3 us  [swap(): return lax.ppermute(x, axis, [(i, i ^ offset) for i in range(size)])]
    all_gather x1 -> x0, blocking collectives: 13.7 us -> none  [on_device(): node_tokens = lax.all_gather(normed, 'local', axis=0, tiled=True)]
    reduce_scatter x1 -> x0, waiting for transfers between devices: 11.4 us -> none  [on_device(): lax.psum_scatter(jnp.dot(shared_hidden, s_down, preferred_element_type=jn...]
  transfers between devices with their start and end apart: 5 -> 17, of which waited for: 5 -> 7; matrix products, arithmetic and copies ran while one was open for 9% -> 5% of each run, Pallas kernels for 0% -> 7%
where the time goes in v1:
time: 79.4 us; the launch traced here: 78.8 us
  local copies, waits for them, and re-layouts  28.1 us (35%)
  starting transfers between devices  19.7 us (25%)
  waiting for transfers between devices  19.3 us (24%)
  Pallas kernels  9.79 us (12%)
  other arithmetic  1.79 us (2%)
    unnamed x35, local copies, waits for them, and re-layouts  25.7 us
    ppermute x17, starting transfers between devices, swap(): return lax.ppermute(x, axis, [(i, i ^ offset) for i in range(size)])  19.7 us
    ppermute x17, waiting for transfers between devices, swap(): return lax.ppermute(x, axis, [(i, i ^ offset) for i in range(size)])  19.3 us
    pallas_call x3, Pallas kernels, on_device(): call(functools.partial(project_kernel, first), 'project', flops, read, su...  5.44 us
    pallas_call x1, Pallas kernels, on_device(): call(functools.partial(down_kernel, slice(index * step, (index + 1) * ste...  2.64 us
    pallas_call x1, Pallas kernels, on_device(): call(functools.partial(hidden_kernel, width, pick), 'hidden', flops, read...  1.72 us
  transfers between devices with their start and end apart: 17, of which 7 were waited for; matrix products, arithmetic and copies ran while one was open for 5% of the time, Pallas kernels for 7%

profile of v1, /device:TPU:0, one launch (start us, length us, event | category | flops | bytes accessed | tf_op | source)
XLA Modules:
  0.0 78.8 jit_solution(12789012091196800990)
XLA Ops:
  0.0 3.0 %collective-permute-start = (bf16[32,1280]{1,0:T(8,128)(2,1)}, bf16[32,1280]{1,0:T(8,128)(2,1)S(1)}, u32[]{:S(2)}, u32[]{:S(2)}) collective-permute-start(bf16[32,1280]{1,0:T(8,128)(2,1)} %param.10), channel_id=1, source_target_pairs={{0,4},{4,0},{8,12},{12,8},{1,5},{5,1},{9,13},{13,9},{2,6},{6,2},{1... | collective-permute-start | bytes 245768 | tf_op jit(solution)/shard_map/ppermute | solution.py:17
  3.0 2.6 %collective-permute-start.1 = (bf16[32,1280]{1,0:T(8,128)(2,1)}, bf16[32,1280]{1,0:T(8,128)(2,1)S(1)}, u32[]{:S(2)}, u32[]{:S(2)}) collective-permute-start(bf16[32,1280]{1,0:T(8,128)(2,1)} %param.10), channel_id=1, source_target_pairs={{0,8},{4,12},{8,0},{12,4},{1,9},{5,13},{9,1},{13,5},{2,10},{6,14},... | collective-permute-start | bytes 245768 | tf_op jit(solution)/shard_map/ppermute | solution.py:17
  5.6 0.8 copy.20
  7.3 1.9 %collective-permute-start.7 = (bf16[1,8,128]{2,1,0:T(8,128)(2,1)S(1)}, bf16[1,8,128]{2,1,0:T(8,128)(2,1)S(1)}, u32[]{:S(2)}, u32[]{:S(2)}) collective-permute-start(bf16[1,8,128]{2,1,0:T(8,128)(2,1)S(1)} %fusion.12), channel_id=1, source_target_pairs={{0,8},{4,12},{8,0},{12,4},{1,9},{5,13},{9,1},{13,5},{2,10},{6,14},... | collective-permute-start | bytes 6152 | tf_op jit(solution)/shard_map/ppermute | solution.py:17
  9.2 2.5 %collective-permute-start.6 = (bf16[1,8,128]{2,1,0:T(8,128)(2,1)S(1)}, bf16[1,8,128]{2,1,0:T(8,128)(2,1)S(1)}, u32[]{:S(2)}, u32[]{:S(2)}) collective-permute-start(bf16[1,8,128]{2,1,0:T(8,128)(2,1)S(1)} %fusion.12), channel_id=1, source_target_pairs={{0,4},{4,0},{8,12},{12,8},{1,5},{5,1},{9,13},{13,9},{2,6},{6,2},{1... | collective-permute-start | bytes 6152 | tf_op jit(solution)/shard_map/ppermute | solution.py:17
  11.6 0.9 %constant_dynamic-update-slice_fusion.3 = bf16[128,1280]{1,0:T(8,128)(2,1)S(1)} fusion(bf16[32,1280]{1,0:T(8,128)(2,1)} %param.10), kind=kLoop, calls=%fused_computation.26 | loop fusion | bytes 163840
  13.2 1.6 %collective-permute-start.10 = (bf16[4,8,128]{2,1,0:T(8,128)(2,1)S(1)}, bf16[4,8,128]{2,1,0:T(8,128)(2,1)S(1)}, u32[]{:S(2)}, u32[]{:S(2)}) collective-permute-start(bf16[4,8,128]{2,1,0:T(8,128)(2,1)S(1)} %pad_maximum_fusion.1.refs_0_), channel_id=1, source_target_pairs={{0,2},{1,3},{2,0},{3,1},{4,6},{5,7},{6,4},{7,5},{8,10},{9,11},{10,... | collective-permute-start | bytes 24584 | tf_op jit(solution)/shard_map/ppermute | solution.py:17
  14.8 4.3 %collective-permute-done.2 = bf16[32,1280]{1,0:T(8,128)(2,1)S(1)} collective-permute-done((bf16[32,1280]{1,0:T(8,128)(2,1)}, bf16[32,1280]{1,0:T(8,128)(2,1)S(1)}, u32[]{:S(2)}, u32[]{:S(2)}) %collective-permute-start.2) | collective-permute-done | bytes 81952 | tf_op jit(solution)/shard_map/ppermute | solution.py:17
  19.1 1.5 %collective-permute-start.4 = (bf16[128,1280]{1,0:T(8,128)(2,1)S(1)}, bf16[128,1280]{1,0:T(8,128)(2,1)}, u32[]{:S(2)}, u32[]{:S(2)}) collective-permute-start(bf16[128,1280]{1,0:T(8,128)(2,1)S(1)} %constant_dynamic-update-slice_fusion.chunk_ref), channel_id=1, source_target_pairs={{0,2},{1,3},{2,0},{3,1},{4,6},{5,7},{6,4},{7,5},{8,10},{9,11},{10,... | collective-permute-start | bytes 983048 | tf_op jit(solution)/shard_map/ppermute | solution.py:17
  21.3 4.0 %copy-done = bf16[2,5120,512]{2,1,0:T(8,128)(2,1)S(1)} copy-done((bf16[2,5120,512]{2,1,0:T(8,128)(2,1)S(1)}, bf16[2,5120,512]{2,1,0:T(8,128)(2,1)}, u32[]{:S(2)}) %copy-start) | copy-done | bytes 10485784
  25.2 4.0 %copy-done.2 = bf16[2,5120,512]{2,1,0:T(8,128)(2,1)S(1)} copy-done((bf16[2,5120,512]{2,1,0:T(8,128)(2,1)S(1)}, bf16[2,5120,512]{2,1,0:T(8,128)(2,1)}, u32[]{:S(2)}) %copy-start.2) | copy-done | bytes 10485784
  29.2 1.7 %copy-done.4 = bf16[5120,256]{1,0:T(8,128)(2,1)S(1)} copy-done((bf16[5120,256]{1,0:T(8,128)(2,1)S(1)}, bf16[5120,256]{1,0:T(8,128)(2,1)}, u32[]{:S(2)}) %copy-start.4) | copy-done | bytes 2621464
  31.0 1.7 %copy-done.6 = bf16[5120,256]{1,0:T(8,128)(2,1)S(1)} copy-done((bf16[5120,256]{1,0:T(8,128)(2,1)S(1)}, bf16[5120,256]{1,0:T(8,128)(2,1)}, u32[]{:S(2)}) %copy-start.6) | copy-done | bytes 2621464
  33.4 1.1 %project.3 = (f32[128,2048]{1,0:T(8,128)S(1)}, f32[32,512]{1,0:T(8,128)S(1)}, f32[128,128]{1,0:T(8,128)S(1)}) custom-call(s32[1]{0:T(128)} %bitcast.12.part_ref, bf16[128,1280]{1,0:T(8,128)(2,1)S(1)} %constant_dynamic-update-slice_fusion.chunk_ref, f32[4,1,1280]{2,1,0:T(1,128)S(1)} %bitcast.59, bf16[2,5120,512]{2,1,0:T(8,128)(2,1)S(1)} %copy-done, ...), custom_call_target="tpu_custom_call" | custom-call | flops 713031680 | bytes 6553600 | tf_op jit(solution)/shard_map/project/pallas_call | solution.py:224
  34.5 1.0 %copy-done.8 = f32[128,2048]{1,0:T(8,128)} copy-done((f32[128,2048]{1,0:T(8,128)}, f32[128,2048]{1,0:T(8,128)S(1)}, u32[]{:S(2)}) %copy-start.8) | copy-done | bytes 1048600
  35.9 1.8 %copy-done.1 = bf16[2,5120,512]{2,1,0:T(8,128)(2,1)S(1)} copy-done((bf16[2,5120,512]{2,1,0:T(8,128)(2,1)S(1)}, bf16[2,5120,512]{2,1,0:T(8,128)(2,1)}, u32[]{:S(2)}) %copy-start.1) | copy-done | bytes 10485784
  37.8 3.0 %copy-done.3 = bf16[2,5120,512]{2,1,0:T(8,128)(2,1)S(1)} copy-done((bf16[2,5120,512]{2,1,0:T(8,128)(2,1)S(1)}, bf16[2,5120,512]{2,1,0:T(8,128)(2,1)}, u32[]{:S(2)}) %copy-start.3) | copy-done | bytes 10485784
  40.8 0.7 copy-done.5
  41.5 1.7 %copy-done.7 = bf16[5120,256]{1,0:T(8,128)(2,1)S(1)} copy-done((bf16[5120,256]{1,0:T(8,128)(2,1)S(1)}, bf16[5120,256]{1,0:T(8,128)(2,1)}, u32[]{:S(2)}) %copy-start.7) | copy-done | bytes 2621464
  43.3 1.2 %copy-done.9 = f32[128,2048]{1,0:T(8,128)S(1)} copy-done((f32[128,2048]{1,0:T(8,128)S(1)}, f32[128,2048]{1,0:T(8,128)}, u32[]{:S(2)}) %copy-start.9) | copy-done | bytes 1048600
  44.5 2.2 %project.4 = (f32[128,2048]{1,0:T(8,128)S(1)}, f32[32,512]{1,0:T(8,128)S(1)}, f32[128,128]{1,0:T(8,128)S(1)}) custom-call(s32[1]{0:T(128)} %bitcast.16.part_ref, bf16[128,1280]{1,0:T(8,128)(2,1)} %collective-permute-done.3.chunk_ref, f32[4,1,1280]{2,1,0:T(1,128)S(1)} %bitcast.60, ...), custom_call_target="tpu_custom_call", output_to_operand_aliasing={{0}: (7, {}), {1}: (8, {}), {2}: (9, {})} | custom-call | flops 713031680 | bytes 6553600 | tf_op jit(solution)/shard_map/project/pallas_call | solution.py:224
  46.7 0.7 dynamic-slice_bitcast_fusion.1
  47.4 2.2 %project.5 = (f32[128,2048]{1,0:T(8,128)S(1)}, f32[32,512]{1,0:T(8,128)S(1)}, f32[128,128]{1,0:T(8,128)S(1)}) custom-call(s32[1]{0:T(128)} %bitcast.15.part_ref, bf16[128,1280]{1,0:T(8,128)(2,1)} %collective-permute-done.4.chunk_ref, f32[4,1,1280]{2,1,0:T(1,128)S(1)} %bitcast.61, ...), custom_call_target="tpu_custom_call", output_to_operand_aliasing={{0}: (7, {}), {1}: (8, {}), {2}: (9, {})} | custom-call | flops 713031680 | bytes 6553600 | tf_op jit(solution)/shard_map/project/pallas_call | solution.py:224
  49.7 1.7 %hidden.1 = (bf16[128,1024]{1,0:T(8,128)(2,1)S(1)}, bf16[32,256]{1,0:T(8,128)(2,1)S(1)}) custom-call(s32[3]{0:T(128)S(1)} %pad_add_fusion.place_ref, bf16[128,1280]{1,0:T(8,128)(2,1)S(1)} %collective-permute-done.5.chunk_ref, f32[4,1,1280]{2,1,0:T(1,128)S(1)} %bitcast.62, bf16[2,5120,512]{2,1,0:T(8,128)(2,1)S(1)} %copy-done.1, ...), custom_call_target="tpu_custom_call" | custom-call | flops 713031680 | bytes 6553600 | tf_op jit(solution)/shard_map/hidden/pallas_call | solution.py:234
  51.8 1.3 %slice-done.1 = s8[4194304]{0:T(1024)(128)(4,1)S(1)} async-done(((s8[10485760]{0:T(1024)(128)(4,1)}), s8[4194304]{0:T(1024)(128)(4,1)S(1)}, s32[]{:S(2)}) %slice-start.1) | async-done | bytes 4194328
  53.7 0.7 copy-done.10
  54.5 2.6 %down.2 = (f32[2,4,8,5120]{3,2,1,0:T(8,128)S(1)}, bf16[2,4,8,5120]{3,2,1,0:T(8,128)(2,1)S(1)}) custom-call(s32[3]{0:T(128)S(1)} %pad_add_fusion.place_ref, bf16[128,1024]{1,0:T(8,128)(2,1)S(1)} %get-tuple-element.27.hidden_ref, bf16[32,256]{1,0:T(8,128)(2,1)S(1)} %get-tuple-element.28.shared_hidden_ref, bf16[2,512,5120]{2,1,0:T(8,128)(2,1)S(1)} %bitcast.58, ...), custom_call_target="tpu_custom_call" | custom-call | flops 1426063360 | bytes 13107200 | tf_op jit(solution)/shard_map/down/pallas_call | solution.py:253
  58.4 1.0 %collective-permute-done.12 = bf16[2,4,8,5120]{3,2,1,0:T(8,128)(2,1)S(1)} collective-permute-done((bf16[2,4,8,5120]{3,2,1,0:T(8,128)(2,1)S(1)}, bf16[2,4,8,5120]{3,2,1,0:T(8,128)(2,1)S(1)}, u32[]{:S(2)}, u32[]{:S(2)}) %collective-permute-start.12) | collective-permute-done | bytes 655392 | tf_op jit(solution)/shard_map/ppermute | solution.py:17
  60.1 9.4 %collective-permute-done.13 = bf16[4,8,5120]{2,1,0:T(8,128)(2,1)S(1)} collective-permute-done((bf16[4,8,5120]{2,1,0:T(8,128)(2,1)S(1)}, bf16[4,8,5120]{2,1,0:T(8,128)(2,1)S(1)}, u32[]{:S(2)}, u32[]{:S(2)}) %collective-permute-start.13) | collective-permute-done | bytes 327712 | tf_op jit(solution)/shard_map/ppermute | solution.py:17
  70.0 4.0 %collective-permute-start.14 = (bf16[8,5120]{1,0:T(8,128)(2,1)S(1)}, bf16[8,5120]{1,0:T(8,128)(2,1)S(1)}, u32[]{:S(2)}, u32[]{:S(2)}) collective-permute-start(bf16[8,5120]{1,0:T(8,128)(2,1)S(1)} %get-tuple-element.33), channel_id=1, source_target_pairs={{0,4},{4,0},{8,12},{12,8},{1,5},{5,1},{9,13},{13,9},{2,6},{6,2},{1... | collective-permute-start | bytes 245768 | tf_op jit(solution)/shard_map/ppermute | solution.py:17
  74.1 2.8 %collective-permute-done.16 = bf16[8,5120]{1,0:T(8,128)(2,1)S(1)} collective-permute-done((bf16[8,5120]{1,0:T(8,128)(2,1)S(1)}, bf16[8,5120]{1,0:T(8,128)(2,1)S(1)}, u32[]{:S(2)}, u32[]{:S(2)}) %collective-permute-start.16) | collective-permute-done | bytes 81952 | tf_op jit(solution)/shard_map/ppermute | solution.py:17
  77.0 1.1 %collective-permute-done.15 = bf16[8,5120]{1,0:T(8,128)(2,1)S(1)} collective-permute-done((bf16[8,5120]{1,0:T(8,128)(2,1)S(1)}, bf16[8,5120]{1,0:T(8,128)(2,1)S(1)}, u32[]{:S(2)}, u32[]{:S(2)}) %collective-permute-start.15) | collective-permute-done | bytes 81952 | tf_op jit(solution)/shard_map/ppermute | solution.py:17
  (64 shorter events, 7.7 us)
Async XLA Ops:
  0.0 14.8 %collective-permute-start = (bf16[32,1280]{1,0:T(8,128)(2,1)}, bf16[32,1280]{1,0:T(8,128)(2,1)S(1)}, u32[]{:S(2)}, u32[]{:S(2)}) collective-permute-start(bf16[32,1280]{1,0:T(8,128)(2,1)} %param.10), channel_id=1, source_target_pairs={{0,4},{4,0},{8,12},{12,8},{1,5},{5,1},{9,13},{13,9},{2,6},{6,2},{1... | collective-permute-start | bytes 245768 | tf_op jit(solution)/shard_map/ppermute | solution.py:17
  3.0 11.7 %collective-permute-start.1 = (bf16[32,1280]{1,0:T(8,128)(2,1)}, bf16[32,1280]{1,0:T(8,128)(2,1)S(1)}, u32[]{:S(2)}, u32[]{:S(2)}) collective-permute-start(bf16[32,1280]{1,0:T(8,128)(2,1)} %param.10), channel_id=1, source_target_pairs={{0,8},{4,12},{8,0},{12,4},{1,9},{5,13},{9,1},{13,5},{2,10},{6,14},... | collective-permute-start | bytes 245768 | tf_op jit(solution)/shard_map/ppermute | solution.py:17
  7.2 5.4 %collective-permute-start.8 = (bf16[1,8,128]{2,1,0:T(8,128)(2,1)S(1)}, bf16[1,8,128]{2,1,0:T(8,128)(2,1)S(1)}, u32[]{:S(2)}, u32[]{:S(2)}) collective-permute-start(bf16[1,8,128]{2,1,0:T(8,128)(2,1)S(1)} %fusion.12), channel_id=1, source_target_pairs={{0,12},{4,8},{8,4},{12,0},{1,13},{5,9},{9,5},{13,1},{2,14},{6,10},... | collective-permute-start | bytes 6152 | tf_op jit(solution)/shard_map/ppermute | solution.py:17
  7.3 5.4 %collective-permute-start.7 = (bf16[1,8,128]{2,1,0:T(8,128)(2,1)S(1)}, bf16[1,8,128]{2,1,0:T(8,128)(2,1)S(1)}, u32[]{:S(2)}, u32[]{:S(2)}) collective-permute-start(bf16[1,8,128]{2,1,0:T(8,128)(2,1)S(1)} %fusion.12), channel_id=1, source_target_pairs={{0,8},{4,12},{8,0},{12,4},{1,9},{5,13},{9,1},{13,5},{2,10},{6,14},... | collective-permute-start | bytes 6152 | tf_op jit(solution)/shard_map/ppermute | solution.py:17
  9.2 4.0 %collective-permute-start.6 = (bf16[1,8,128]{2,1,0:T(8,128)(2,1)S(1)}, bf16[1,8,128]{2,1,0:T(8,128)(2,1)S(1)}, u32[]{:S(2)}, u32[]{:S(2)}) collective-permute-start(bf16[1,8,128]{2,1,0:T(8,128)(2,1)S(1)} %fusion.12), channel_id=1, source_target_pairs={{0,4},{4,0},{8,12},{12,8},{1,5},{5,1},{9,13},{13,9},{2,6},{6,2},{1... | collective-permute-start | bytes 6152 | tf_op jit(solution)/shard_map/ppermute | solution.py:17
  12.6 6.4 %collective-permute-start.2 = (bf16[32,1280]{1,0:T(8,128)(2,1)}, bf16[32,1280]{1,0:T(8,128)(2,1)S(1)}, u32[]{:S(2)}, u32[]{:S(2)}) collective-permute-start(bf16[32,1280]{1,0:T(8,128)(2,1)} %param.10), channel_id=1, source_target_pairs={{0,12},{4,8},{8,4},{12,0},{1,13},{5,9},{9,5},{13,1},{2,14},{6,10},... | collective-permute-start | bytes 245768 | tf_op jit(solution)/shard_map/ppermute | solution.py:17
  13.2 8.0 %collective-permute-start.10 = (bf16[4,8,128]{2,1,0:T(8,128)(2,1)S(1)}, bf16[4,8,128]{2,1,0:T(8,128)(2,1)S(1)}, u32[]{:S(2)}, u32[]{:S(2)}) collective-permute-start(bf16[4,8,128]{2,1,0:T(8,128)(2,1)S(1)} %pad_maximum_fusion.1.refs_0_), channel_id=1, source_target_pairs={{0,2},{1,3},{2,0},{3,1},{4,6},{5,7},{6,4},{7,5},{8,10},{9,11},{10,... | collective-permute-start | bytes 24584 | tf_op jit(solution)/shard_map/ppermute | solution.py:17
  19.1 16.4 %collective-permute-start.4 = (bf16[128,1280]{1,0:T(8,128)(2,1)S(1)}, bf16[128,1280]{1,0:T(8,128)(2,1)}, u32[]{:S(2)}, u32[]{:S(2)}) collective-permute-start(bf16[128,1280]{1,0:T(8,128)(2,1)S(1)} %constant_dynamic-update-slice_fusion.chunk_ref), channel_id=1, source_target_pairs={{0,2},{1,3},{2,0},{3,1},{4,6},{5,7},{6,4},{7,5},{8,10},{9,11},{10,... | collective-permute-start | bytes 983048 | tf_op jit(solution)/shard_map/ppermute | solution.py:17
  20.6 15.4 %collective-permute-start.3 = (bf16[128,1280]{1,0:T(8,128)(2,1)S(1)}, bf16[128,1280]{1,0:T(8,128)(2,1)}, u32[]{:S(2)}, u32[]{:S(2)}) collective-permute-start(bf16[128,1280]{1,0:T(8,128)(2,1)S(1)} %constant_dynamic-update-slice_fusion.chunk_ref), channel_id=1, source_target_pairs={{0,1},{1,0},{2,3},{3,2},{4,5},{5,4},{6,7},{7,6},{8,9},{9,8},{10,11... | collective-permute-start | bytes 983048 | tf_op jit(solution)/shard_map/ppermute | solution.py:17
  20.7 29.0 %collective-permute-start.9 = (bf16[4,8,128]{2,1,0:T(8,128)(2,1)S(1)}, bf16[4,8,128]{2,1,0:T(8,128)(2,1)S(1)}, u32[]{:S(2)}, u32[]{:S(2)}) collective-permute-start(bf16[4,8,128]{2,1,0:T(8,128)(2,1)S(1)} %pad_maximum_fusion.1.refs_0_), channel_id=1, source_target_pairs={{0,1},{1,0},{2,3},{3,2},{4,5},{5,4},{6,7},{7,6},{8,9},{9,8},{10,11... | collective-permute-start | bytes 24584 | tf_op jit(solution)/shard_map/ppermute | solution.py:17
  21.2 28.5 %collective-permute-start.11 = (bf16[4,8,128]{2,1,0:T(8,128)(2,1)S(1)}, bf16[4,8,128]{2,1,0:T(8,128)(2,1)S(1)}, u32[]{:S(2)}, u32[]{:S(2)}) collective-permute-start(bf16[4,8,128]{2,1,0:T(8,128)(2,1)S(1)} %collective-permute-done.10.refs_2_), channel_id=1, source_target_pairs={{0,1},{1,0},{2,3},{3,2},{4,5},{5,4},{6,7},{7,6},{8,9},{9,8},{10,11... | collective-permute-start | bytes 24584 | tf_op jit(solution)/shard_map/ppermute | solution.py:17
  21.3 4.0 %copy-start = (bf16[2,5120,512]{2,1,0:T(8,128)(2,1)S(1)}, bf16[2,5120,512]{2,1,0:T(8,128)(2,1)}, u32[]{:S(2)}) copy-start(bf16[2,5120,512]{2,1,0:T(8,128)(2,1)} %gate.7) | copy-start | bytes 31457284
  25.2 4.0 %copy-start.2 = (bf16[2,5120,512]{2,1,0:T(8,128)(2,1)S(1)}, bf16[2,5120,512]{2,1,0:T(8,128)(2,1)}, u32[]{:S(2)}) copy-start(bf16[2,5120,512]{2,1,0:T(8,128)(2,1)} %up.7) | copy-start | bytes 31457284
  29.2 1.7 %copy-start.4 = (bf16[5120,256]{1,0:T(8,128)(2,1)S(1)}, bf16[5120,256]{1,0:T(8,128)(2,1)}, u32[]{:S(2)}) copy-start(bf16[5120,256]{1,0:T(8,128)(2,1)} %s_gate.7) | copy-start | bytes 7864324
  31.0 1.7 %copy-start.6 = (bf16[5120,256]{1,0:T(8,128)(2,1)S(1)}, bf16[5120,256]{1,0:T(8,128)(2,1)}, u32[]{:S(2)}) copy-start(bf16[5120,256]{1,0:T(8,128)(2,1)} %s_up.7) | copy-start | bytes 7864324
  33.4 4.4 %copy-start.1 = (bf16[2,5120,512]{2,1,0:T(8,128)(2,1)S(1)}, bf16[2,5120,512]{2,1,0:T(8,128)(2,1)}, u32[]{:S(2)}) copy-start(bf16[2,5120,512]{2,1,0:T(8,128)(2,1)} %gate.7) | copy-start | bytes 31457284
  33.4 7.3 %copy-start.3 = (bf16[2,5120,512]{2,1,0:T(8,128)(2,1)S(1)}, bf16[2,5120,512]{2,1,0:T(8,128)(2,1)}, u32[]{:S(2)}) copy-start(bf16[2,5120,512]{2,1,0:T(8,128)(2,1)} %up.7) | copy-start | bytes 31457284
  33.4 8.1 %copy-start.5 = (bf16[5120,256]{1,0:T(8,128)(2,1)S(1)}, bf16[5120,256]{1,0:T(8,128)(2,1)}, u32[]{:S(2)}) copy-start(bf16[5120,256]{1,0:T(8,128)(2,1)} %s_gate.7) | copy-start | bytes 7864324
  33.4 8.1 %copy-start.12 = (f32[5120]{0:T(1024)S(1)}, f32[5120]{0:T(1024)}, u32[]{:S(2)}) copy-start(f32[5120]{0:T(1024)} %param.11) | copy-start | bytes 61444
  34.5 1.0 %copy-start.8 = (f32[128,2048]{1,0:T(8,128)}, f32[128,2048]{1,0:T(8,128)S(1)}, u32[]{:S(2)}) copy-start(f32[128,2048]{1,0:T(8,128)S(1)} %get-tuple-element.18.refs_0_) | copy-start | bytes 3145732
  35.5 14.1 %collective-permute-start.5 = (bf16[128,1280]{1,0:T(8,128)(2,1)}, bf16[128,1280]{1,0:T(8,128)(2,1)S(1)}, u32[]{:S(2)}, u32[]{:S(2)}) collective-permute-start(bf16[128,1280]{1,0:T(8,128)(2,1)} %collective-permute-done.4.chunk_ref), channel_id=1, source_target_pairs={{0,1},{1,0},{2,3},{3,2},{4,5},{5,4},{6,7},{7,6},{8,9},{9,8},{10,11... | collective-permute-start | bytes 983048 | tf_op jit(solution)/shard_map/ppermute | solution.py:17
  41.5 1.7 %copy-start.7 = (bf16[5120,256]{1,0:T(8,128)(2,1)S(1)}, bf16[5120,256]{1,0:T(8,128)(2,1)}, u32[]{:S(2)}) copy-start(bf16[5120,256]{1,0:T(8,128)(2,1)} %s_up.7) | copy-start | bytes 7864324
  43.3 1.2 %copy-start.9 = (f32[128,2048]{1,0:T(8,128)S(1)}, f32[128,2048]{1,0:T(8,128)}, u32[]{:S(2)}) copy-start(f32[128,2048]{1,0:T(8,128)} %copy-done.8) | copy-start | bytes 3145732
  49.6 2.2 %slice-start = ((s8[10485760]{0:T(1024)(128)(4,1)}), s8[4194304]{0:T(1024)(128)(4,1)S(1)}, s32[]{:S(2)}) async-start(s8[10485760]{0:T(1024)(128)(4,1)} %bitcast.57), calls=%async_computation | async-start | bytes 8388608
  49.7 3.5 %slice-start.1 = ((s8[10485760]{0:T(1024)(128)(4,1)}), s8[4194304]{0:T(1024)(128)(4,1)S(1)}, s32[]{:S(2)}) async-start(s8[10485760]{0:T(1024)(128)(4,1)} %bitcast.57), calls=%async_computation.1 | async-start | bytes 8388608
  49.7 4.0 %slice-start.2 = ((s8[10485760]{0:T(1024)(128)(4,1)}), s8[2097152]{0:T(1024)(128)(4,1)S(1)}, s32[]{:S(2)}) async-start(s8[10485760]{0:T(1024)(128)(4,1)} %bitcast.57), calls=%async_computation.2 | async-start | bytes 4194304
  49.7 4.8 %copy-start.10 = (bf16[256,5120]{1,0:T(8,128)(2,1)S(1)}, bf16[256,5120]{1,0:T(8,128)(2,1)}, u32[]{:S(2)}) copy-start(bf16[256,5120]{1,0:T(8,128)(2,1)} %s_down.1) | copy-start | bytes 7864324
  57.1 2.2 %collective-permute-start.12 = (bf16[2,4,8,5120]{3,2,1,0:T(8,128)(2,1)S(1)}, bf16[2,4,8,5120]{3,2,1,0:T(8,128)(2,1)S(1)}, u32[]{:S(2)}, u32[]{:S(2)}) collective-permute-start(bf16[2,4,8,5120]{3,2,1,0:T(8,128)(2,1)S(1)} %get-tuple-element.30), channel_id=1, source_target_pairs={{0,1},{1,0},{2,3},{3,2},{4,5},{5,4},{6,7},{7,6},{8,9},{9,8},{10,11... | collective-permute-start | bytes 1966088 | tf_op jit(solution)/shard_map/ppermute | solution.py:17
  59.5 10.1 %collective-permute-start.13 = (bf16[4,8,5120]{2,1,0:T(8,128)(2,1)S(1)}, bf16[4,8,5120]{2,1,0:T(8,128)(2,1)S(1)}, u32[]{:S(2)}, u32[]{:S(2)}) collective-permute-start(bf16[4,8,5120]{2,1,0:T(8,128)(2,1)S(1)} %fusion.1), channel_id=1, source_target_pairs={{0,2},{1,3},{2,0},{3,1},{4,6},{5,7},{6,4},{7,5},{8,10},{9,11},{10,... | collective-permute-start | bytes 983048 | tf_op jit(solution)/shard_map/ppermute | solution.py:17
  69.6 7.3 %collective-permute-start.16 = (bf16[8,5120]{1,0:T(8,128)(2,1)S(1)}, bf16[8,5120]{1,0:T(8,128)(2,1)S(1)}, u32[]{:S(2)}, u32[]{:S(2)}) collective-permute-start(bf16[8,5120]{1,0:T(8,128)(2,1)S(1)} %get-tuple-element.34), channel_id=1, source_target_pairs={{0,12},{4,8},{8,4},{12,0},{1,13},{5,9},{9,5},{13,1},{2,14},{6,10},... | collective-permute-start | bytes 245768 | tf_op jit(solution)/shard_map/ppermute | solution.py:17
  69.9 8.2 %collective-permute-start.15 = (bf16[8,5120]{1,0:T(8,128)(2,1)S(1)}, bf16[8,5120]{1,0:T(8,128)(2,1)S(1)}, u32[]{:S(2)}, u32[]{:S(2)}) collective-permute-start(bf16[8,5120]{1,0:T(8,128)(2,1)S(1)} %get-tuple-element.35), channel_id=1, source_target_pairs={{0,8},{4,12},{8,0},{12,4},{1,9},{5,13},{9,1},{13,5},{2,10},{6,14},... | collective-permute-start | bytes 245768 | tf_op jit(solution)/shard_map/ppermute | solution.py:17
  70.0 8.1 %collective-permute-start.14 = (bf16[8,5120]{1,0:T(8,128)(2,1)S(1)}, bf16[8,5120]{1,0:T(8,128)(2,1)S(1)}, u32[]{:S(2)}, u32[]{:S(2)}) collective-permute-start(bf16[8,5120]{1,0:T(8,128)(2,1)S(1)} %get-tuple-element.33), channel_id=1, source_target_pairs={{0,4},{4,0},{8,12},{12,8},{1,5},{5,1},{9,13},{13,9},{2,6},{6,2},{1... | collective-permute-start | bytes 245768 | tf_op jit(solution)/shard_map/ppermute | solution.py:17
  (1 other events, 0.7 us)

commit v2 on v0

v2 whole, which is shorter than its diff:
```python
import functools

import jax
import jax.numpy as jnp
from jax import lax
from jax.experimental import pallas as pl
from jax.experimental.pallas import tpu as pltpu
from jax.sharding import PartitionSpec as P

ROWS = 128
LANES = 128
CORES = 2
WINDOW = 5
LATE = 2
VMEM = pl.BlockSpec(memory_space=pltpu.VMEM)
SMEM = pl.BlockSpec(memory_space=pltpu.SMEM)
ANY = pl.BlockSpec(memory_space=pl.ANY)
HBM = pl.BlockSpec(memory_space=pltpu.HBM)


def swap(x, axis, offset):
    size = lax.axis_size(axis)
    return lax.ppermute(x, axis, [(i, i ^ offset) for i in range(size)])


def in_hbm(x):
    return pltpu.with_memory_space_constraint(x, pltpu.HBM)


def row_loop(total, body):
    block = min(ROWS, total)
    if total == block:
        body(pl.ds(0, block))
        return

    @pl.loop(0, total // block)
    def _(index):
        body(pl.ds(pl.multiple_of(index * block, block), block))


def pack_kernel(pick, experts, place_ref, *refs):
    sources, (block_ref, rows_ref, ids_ref, gates_ref, sems) = refs[:3], refs[3:]
    own, depth = rows_ref.shape
    moves = [
        pltpu.make_async_copy(source, target, sems.at[index])
        for index, (source, target) in enumerate(zip(sources, (rows_ref, ids_ref, gates_ref)))
    ]
    for move in moves:
        move.start()
    for move in moves:
        move.wait()
    tokens = ids_ref.shape[1]
    diagonal = lax.broadcasted_iota(jnp.int32, (tokens, tokens), 0) == lax.broadcasted_iota(
        jnp.int32, (tokens, tokens), 1
    )
    lane = lax.broadcasted_iota(jnp.int32, (tokens, LANES), 1)
    tag = jnp.zeros((tokens, LANES), jnp.float32)
    for index in range(pick * (1 + experts)):
        ref, row = (ids_ref, index) if index < pick else (gates_ref, index - pick)
        values = ref[row : row + 1, :].astype(jnp.float32)
        column = jnp.sum(jnp.where(diagonal, values, 0.0), axis=1, keepdims=True)
        tag = jnp.where(lane == index, column, tag)
    tags = jnp.concatenate([tag] * (own // tokens), axis=0)
    row = lax.broadcasted_iota(jnp.int32, (own, LANES), 0)
    first = place_ref[0] * tokens
    mine = (row >= first) & (row < first + tokens)
    block_ref[:, :depth] = rows_ref[...]
    block_ref[:, depth:] = jnp.where(mine, tags, 0.0).astype(jnp.bfloat16)


class Queue:
    def __init__(self, moves):
        self.moves, self.waited = moves, 0
        for move in moves[:WINDOW]:
            move.start()

    def wait(self):
        self.moves[self.waited].wait()
        if self.waited + WINDOW < len(self.moves):
            self.moves[self.waited + WINDOW].start()
        self.waited += 1


def weight_moves(parts, weights, buffers, sems):
    gate, up, s_gate, s_up = weights
    buffer, shared_buffer = buffers
    experts, depth = gate.shape[0], buffer.shape[2]
    moves = []

    def move(source, target):
        moves.append(pltpu.make_async_copy(source, target, sems.at[len(moves)]))

    blocks = [pl.ds(pl.multiple_of(part * depth, depth), depth) for part in parts]
    for slot in range(experts * 2):
        for index, rows in enumerate(blocks):
            move((gate, up)[slot % 2].at[slot // 2, rows, :], buffer.at[index, slot])
    for which, weight in enumerate((s_gate, s_up)):
        for index, rows in enumerate(blocks):
            move(weight.at[rows, :], shared_buffer.at[index, which])
    return moves


def scaled_rows(chunk_ref, gain, rows):
    values = chunk_ref[rows, : gain.shape[1]].astype(jnp.float32)
    return values, (values * gain).astype(jnp.bfloat16)


def square_sums(chunk_ref, gain, lhs_ref, square_ref, square_in):
    def body(rows):
        values, lhs = scaled_rows(chunk_ref, gain, rows)
        lhs_ref[rows, :] = lhs
        square = jnp.sum(values * values, axis=1, keepdims=True)
        square = jnp.broadcast_to(square, (square.shape[0], LANES))
        square_ref[rows, :] = square if square_in is None else square + square_in[rows, :]

    row_loop(chunk_ref.shape[0], body)


def project_kernel(first, extra, part_ref, chunk_ref, gain_ref, *refs):
    weights, refs = refs[:4], refs[4 + extra :]
    (acc_in, shared_in, square_in), refs = ((None,) * 3, refs) if first else (refs[:3], refs[3:])
    acc_ref, shared_ref, square_ref, lhs_ref, buffer, shared_buffer, sems = refs
    part = part_ref[0]
    queue = Queue(weight_moves([part], weights, (buffer, shared_buffer), sems))
    square_sums(chunk_ref, gain_ref[part], lhs_ref, square_ref, square_in)
    inner, shared_inner = buffer.shape[3], shared_buffer.shape[3]
    for slot in range(buffer.shape[1]):
        queue.wait()
        columns = slice(slot * inner, (slot + 1) * inner)

        def body(rows):
            term = jnp.dot(lhs_ref[rows, :], buffer[0, slot], preferred_element_type=jnp.float32)
            acc_ref[rows, columns] = term if first else term + acc_in[rows, columns]

        row_loop(chunk_ref.shape[0], body)
    own = shared_ref.shape[0]
    for which in range(2):
        queue.wait()
        columns = slice(which * shared_inner, (which + 1) * shared_inner)
        term = jnp.dot(
            lhs_ref[:own, :], shared_buffer[0, which], preferred_element_type=jnp.float32
        )
        shared_ref[:, columns] = term if first else term + shared_in[:, columns]


def join_kernel(count, *refs):
    out_ref = refs[-1]
    start = 0
    for ref in refs[:count]:
        out_ref[start : start + ref.shape[0], :] = ref[...]
        start += ref.shape[0]


def relay_kernel(half, mine_ref, *refs):
    pairs, nodes = mine_ref.shape[:2]
    came, sums, near = refs[: pairs - 1], refs[pairs - 1 : pairs - 1 + nodes - half], refs[pairs - 1 + nodes - half :]
    for index, sum_ref in enumerate(sums):
        total = mine_ref[0, half + index]
        for ref in came:
            total = total + ref[index].astype(jnp.float32)
        sum_ref[...] = total.astype(jnp.bfloat16)
    for pair, ref in enumerate(near):
        ref[...] = mine_ref[pair + 1, :half].astype(jnp.bfloat16)


def act(gate, up):
    return gate / (1.0 + jnp.exp(-gate)) * up


def row_share(tag, node, pick, experts, expert):
    share = jnp.zeros((tag.shape[0], 1), jnp.float32)
    for k in range(pick):
        column = pick + k * experts + expert
        share = share + jnp.where(
            tag[:, k : k + 1] == node.astype(jnp.float32), tag[:, column : column + 1], 0.0
        )
    return share


def down_part(me, hidden_ref, shared_hidden_ref, wait, down, s_down, out_ref, keep_ref, send_ref):
    experts, inner = down.shape[0], down.shape[1]
    own = shared_hidden_ref.shape[0]
    for expert in range(experts):
        wait()

        def body(rows):
            term = jnp.dot(
                hidden_ref[rows, expert * inner : (expert + 1) * inner],
                down[expert],
                preferred_element_type=jnp.float32,
            )
            out_ref[rows, :] = term if expert == 0 else term + out_ref[rows, :]

        row_loop(hidden_ref.shape[0], body)
    wait()
    out_ref[:own, :] += jnp.dot(
        shared_hidden_ref[...], s_down[...], preferred_element_type=jnp.float32
    )
    pairs, nodes, tokens = keep_ref.shape[:3]
    for pair in range(pairs):
        for side, to_ref in enumerate((keep_ref, send_ref)):
            place = lax.bitwise_xor(me, pair * CORES + side) * tokens
            for other in range(nodes):
                rows = pl.ds(pl.multiple_of(other * own + place, tokens), tokens)
                to_ref[pair, other] = out_ref[rows, :].astype(to_ref.dtype)


def down_moves(columns, down, s_down, buffer, shared_buffer, sems, base):
    experts = down.shape[0]
    moves = [
        pltpu.make_async_copy(down.at[e, :, columns], buffer.at[e], sems.at[base + e])
        for e in range(experts)
    ]
    return moves + [
        pltpu.make_async_copy(s_down.at[:, columns], shared_buffer, sems.at[base + experts])
    ]


def finish_kernel(
    width, pick, columns, part_count, place_ref, gain_ref, gate, up, s_gate, s_up,
    acc_in, shared_in, square_in, down, s_down, *refs
):
    chunks, refs = refs[:part_count], refs[part_count:]
    (
        hidden_ref, shared_hidden_ref, keep_ref, send_ref,
        lhs_ref, square_ref, buffer, shared_buffer, down_buffer, s_down_buffer, out_ref, sems,
    ) = refs
    me, node = place_ref[0], place_ref[1]
    late = buffer.shape[0]
    parts = [lax.bitwise_xor(me, part_count - late + index) for index in range(late)]
    moves = weight_moves(parts, (gate, up, s_gate, s_up), (buffer, shared_buffer), sems)
    moves += down_moves(columns, down, s_down, down_buffer, s_down_buffer, sems, len(moves))
    queue = Queue(moves)
    experts, inner, shared_inner = gate.shape[0], gate.shape[2], s_gate.shape[1]
    own, depth = shared_in.shape[0], gain_ref.shape[2]
    for index, part in enumerate(parts):
        square_sums(
            chunks[index - late], gain_ref[part], lhs_ref.at[index], square_ref,
            square_ref if index else square_in,
        )
    for expert in range(experts):

        def body(rows):
            tag = sum(chunk[rows, depth:].astype(jnp.float32) for chunk in chunks)
            scale = lax.rsqrt(square_ref[rows, :][:, :1] / width + 1e-06)
            projs = []
            for slot in (2 * expert, 2 * expert + 1):
                term = acc_in[rows, slot * inner : (slot + 1) * inner]
                for index in range(late):
                    term = term + jnp.dot(
                        lhs_ref[index, rows, :],
                        buffer[index, slot],
                        preferred_element_type=jnp.float32,
                    )
                projs.append(term * scale)
            share = row_share(tag, node, pick, experts, expert)
            hidden_ref[rows, expert * inner : (expert + 1) * inner] = (
                act(*projs) * share
            ).astype(jnp.bfloat16)

        for _ in range(2 * late):
            queue.wait()
        row_loop(chunks[-1].shape[0], body)
    scale = lax.rsqrt(square_ref[:own, :][:, :1] / width + 1e-06)
    projs = []
    for which in range(2):
        term = shared_in[:, which * shared_inner : (which + 1) * shared_inner]
        for index in range(late):
            queue.wait()
            term = term + jnp.dot(
                lhs_ref[index, :own, :],
                shared_buffer[index, which],
                preferred_element_type=jnp.float32,
            )
        projs.append(term * scale)
    shared_hidden_ref[...] = act(*projs).astype(jnp.bfloat16)
    down_part(
        me, hidden_ref, shared_hidden_ref, queue.wait, down_buffer, s_down_buffer,
        out_ref, keep_ref, send_ref,
    )


def down_kernel(columns, place_ref, hidden_ref, shared_hidden_ref, down, s_down, keep_ref, send_ref, buffer, shared_buffer, out_ref, sems):
    queue = Queue(down_moves(columns, down, s_down, buffer, shared_buffer, sems, 0))
    down_part(
        place_ref[0], hidden_ref, shared_hidden_ref, queue.wait, buffer, shared_buffer,
        out_ref, keep_ref, send_ref,
    )


def call(kernel, name, out_shape, in_specs, scratch, args, flops=0, read=0, aliases=None):
    held = [a for a, spec in zip(args, in_specs) if spec is VMEM] + list(out_shape)
    held += [s for s in scratch if hasattr(s, "dtype") and s.memory_space == pltpu.VMEM]
    size = 0
    for array in held:
        count = jnp.dtype(array.dtype).itemsize
        for extent in array.shape:
            count *= extent
        size += count
    return pl.pallas_call(
        kernel,
        out_shape=out_shape,
        in_specs=in_specs,
        out_specs=[VMEM] * len(out_shape),
        scratch_shapes=scratch,
        input_output_aliases=aliases or {},
        compiler_params=pltpu.CompilerParams(vmem_limit_bytes=size + 8 * 2**20),
        cost_estimate=pl.CostEstimate(flops=flops, bytes_accessed=read, transcendentals=0),
        name=name,
    )(*args)


def on_device(attended, norm_gain, node_ids, gates, w_gate, w_up, w_down, s_gate, s_up, s_down):
    node_count = lax.axis_size("node")
    local_count = lax.axis_size("local")
    pairs = local_count // CORES
    node, me = lax.axis_index("node"), lax.axis_index("local")
    own, depth = attended.shape
    tokens, pick = node_ids.shape
    experts, width, inner = w_gate.shape
    shared_inner = s_gate.shape[1]
    total = node_count * own
    up_weights = tuple(in_hbm(w) for w in (w_gate, w_up, s_gate, s_up))
    down_weights = tuple(in_hbm(w) for w in (w_down, s_down))
    f32, bf16 = jnp.float32, jnp.bfloat16

    inputs = (
        in_hbm(attended),
        in_hbm(node_ids.T),
        in_hbm(gates.transpose(1, 2, 0).reshape(pick * experts, tokens)),
    )
    (block,) = call(
        functools.partial(pack_kernel, pick, experts),
        "pack",
        [jax.ShapeDtypeStruct((own, depth + LANES), bf16)],
        [SMEM, HBM, HBM, HBM],
        [pltpu.VMEM(x.shape, x.dtype) for x in inputs] + [pltpu.SemaphoreType.DMA((3,))],
        (me[None], *inputs),
    )
    blocks = [block] + [swap(block, "node", k) for k in range(1, node_count)]
    rest = jnp.concatenate(blocks[1:], axis=0)
    column = jnp.concatenate([block, rest], axis=0)
    chunks = [column, swap(column, "local", 1)]

    def neighbour(k, sums):
        (column,) = call(
            functools.partial(join_kernel, 2),
            "join",
            [jax.ShapeDtypeStruct(chunks[0].shape, bf16)],
            [VMEM, VMEM, ANY],
            [],
            (first_rows[k - 1], other_rows[k - 1], sums[2]),
        )
        return [column, swap(column, "local", 1)]

    first_rows = [swap(block, "local", k * CORES) for k in range(1, pairs)]
    other_rows = [swap(rest, "local", k * CORES) for k in range(1, pairs)]

    gain = norm_gain.reshape(local_count, 1, depth)
    sums_shape = [
        jax.ShapeDtypeStruct((total, experts * 2 * inner), f32),
        jax.ShapeDtypeStruct((own, 2 * shared_inner), f32),
        jax.ShapeDtypeStruct((total, LANES), f32),
    ]
    flops = 2 * depth * (total * experts * 2 * inner + own * 2 * shared_inner)
    read = 2 * depth * (experts * 2 * inner + 2 * shared_inner)
    weight_scratch = [
        pltpu.VMEM((1, experts * 2, depth, inner), bf16),
        pltpu.VMEM((1, 2, depth, shared_inner), bf16),
    ]
    lhs_scratch = pltpu.VMEM((total, depth), bf16)
    moves = experts * 2 + 2
    sums = None
    for offset in range(local_count - LATE):
        first = sums is None
        if offset == CORES - 1:
            for k in range(1, pairs):
                chunks += neighbour(k, sums)
        args = (lax.bitwise_xor(me, offset)[None], chunks[offset], gain, *up_weights)
        more = tuple(first_rows) if first else tuple(sums)
        sums = call(
            functools.partial(project_kernel, first, len(more) if first else 0),
            "project",
            sums_shape,
            [SMEM, VMEM, VMEM] + [HBM] * 4 + [ANY if first else VMEM] * len(more),
            [lhs_scratch, *weight_scratch, pltpu.SemaphoreType.DMA((moves,))],
            args + more,
            flops,
            read,
            aliases={} if first else {7: 0, 8: 1, 9: 2},
        )
    place = jnp.stack([me, node])

    slices = max(1, total // ROWS)
    step = width // slices
    shape = (pairs, node_count, tokens, step)
    out_shape = [jax.ShapeDtypeStruct(shape, f32), jax.ShapeDtypeStruct(shape, bf16)]
    down_scratch = [
        pltpu.VMEM((experts, inner, step), bf16),
        pltpu.VMEM((shared_inner, step), bf16),
        pltpu.VMEM((total, step), f32),
    ]
    down_flops = 2 * step * (total * experts * inner + own * shared_inner)
    down_read = 2 * step * (experts * inner + shared_inner)
    partials = []
    for index in range(slices):
        columns = slice(index * step, (index + 1) * step)
        if index == 0:
            hidden, shared_hidden, keep, send = call(
                functools.partial(finish_kernel, width, pick, columns, local_count),
                "finish",
                [
                    jax.ShapeDtypeStruct((total, experts * inner), bf16),
                    jax.ShapeDtypeStruct((own, shared_inner), bf16),
                ]
                + out_shape,
                [SMEM, VMEM] + [HBM] * 4 + [VMEM] * 3 + [HBM] * 2 + [VMEM] * local_count,
                [
                    pltpu.VMEM((LATE, total, depth), bf16),
                    pltpu.VMEM((total, LANES), f32),
                    *(pltpu.VMEM((LATE, *w.shape[1:]), bf16) for w in weight_scratch),
                    *down_scratch,
                    pltpu.SemaphoreType.DMA((LATE * moves + experts + 1,)),
                ],
                (place, gain, *up_weights, *sums, *down_weights, *chunks),
                flops + down_flops,
                read + down_read,
            )
        else:
            keep, send = call(
                functools.partial(down_kernel, columns),
                "down",
                out_shape,
                [SMEM, VMEM, VMEM, HBM, HBM],
                [*down_scratch, pltpu.SemaphoreType.DMA((experts + 1,))],
                (place, hidden, shared_hidden, *down_weights),
                down_flops,
                down_read,
            )
        partials.append((keep, send))

    half = node_count // 2
    results = []
    for keep, send in partials:
        mine = keep + swap(send, "local", 1).astype(f32)
        came = [swap(mine[k, half:].astype(bf16), "local", k * CORES) for k in range(1, pairs)]
        rows_shape = jax.ShapeDtypeStruct((tokens, step), bf16)
        near_shape = jax.ShapeDtypeStruct((half, tokens, step), bf16)
        out = call(
            functools.partial(relay_kernel, half),
            "relay",
            [rows_shape] * (node_count - half) + [near_shape] * (pairs - 1),
            [VMEM] * pairs,
            [],
            (mine, *came),
        )
        far, near = out[: node_count - half], out[node_count - half :]
        near_came = [swap(x, "local", k * CORES).astype(f32) for k, x in enumerate(near, 1)]
        far_came = [swap(x, "node", half + k).astype(f32) for k, x in enumerate(far)]
        result = sum(near_came, mine[0, :half])
        total_here = result[0]
        for k in range(1, half):
            total_here = total_here + swap(result[k].astype(bf16), "node", k).astype(f32)
        total_here = sum(far_came, total_here)
        results.append(total_here)
    mixed = jnp.concatenate(results, axis=1)

    rows = jnp.stack(
        [lax.dynamic_slice(c, (me * tokens, 0), (tokens, depth)) for c in chunks]
    )
    bit = 1
    while bit < local_count:
        flipped = rows.reshape(local_count // (2 * bit), 2, bit, tokens, depth)[:, ::-1]
        rows = jnp.where((me & bit) != 0, flipped.reshape(rows.shape), rows)
        bit *= 2
    residual = rows.transpose(1, 0, 2).reshape(tokens, width).astype(jnp.float32)
    return (residual + mixed).astype(jnp.bfloat16)


def solution(mesh):
    in_specs = (
        P(("group", "node"), "local"),
        P(),
        P(("group", "node", "local"), None),
        P(("group", "node", "local"), None, None),
        P("node", None, "local"),
        P("node", None, "local"),
        P("node", "local", None),
        P(None, "local"),
        P(None, "local"),
        P("local", None),
    )
    out_specs = P(("group", "node", "local"), None)
    return jax.shard_map(
        on_device, mesh=mesh, in_specs=in_specs, out_specs=out_specs, check_vma=False
    )
```

time: 147 us -> 57.6 us (0.39)
  waiting for transfers between devices: 52.9 us -> 17.4 us
  matrix products: 32 us -> 0 us
  Pallas kernels: 0 us -> 19.7 us
  blocking collectives: 13.7 us -> 0 us
  between operations: 13.5 us -> 0.15 us
  local copies, waits for them, and re-layouts: 8.45 us -> 0.06 us
  starting transfers between devices: 22.4 us -> 19.2 us
  other arithmetic: 3.06 us -> 1.06 us
    all_to_all x4 -> x0, waiting for transfers between devices: 41.5 us -> none  [the longest x1 27.3 us: on_device(): lax.all_to_all(fan_rows.reshape(node_count * local_count, capacity, width...]
    dot_general x9 -> x0, matrix products: 32 us -> none  [the longest x2 15.3 us: expert_term(): jnp.dot(hidden, w_down[expert], preferred_element_type=jnp.float32)]
    all_to_all x4 -> x0, starting transfers between devices: 22.4 us -> none  [the longest x1 8.03 us: on_device(): lax.all_to_all(partial_term.reshape(node_count * local_count, capacity, w...]
    pallas_call x0 -> x6, Pallas kernels: none -> 19.7 us  [call(): pl.pallas_call(kernel, out_shape=out_shape, in_specs=in_specs, out_specs=...]
    ppermute x0 -> x13, starting transfers between devices: none -> 19.2 us  [swap(): return lax.ppermute(x, axis, [(i, i ^ offset) for i in range(size)])]
    ppermute x0 -> x13, waiting for transfers between devices: none -> 17.4 us  [swap(): return lax.ppermute(x, axis, [(i, i ^ offset) for i in range(size)])]
    all_gather x1 -> x0, blocking collectives: 13.7 us -> none  [on_device(): node_tokens = lax.all_gather(normed, 'local', axis=0, tiled=True)]
    reduce_scatter x1 -> x0, waiting for transfers between devices: 11.4 us -> none  [on_device(): lax.psum_scatter(jnp.dot(shared_hidden, s_down, preferred_element_type=jn...]
  transfers between devices with their start and end apart: 5 -> 13, of which waited for: 5 -> 7; matrix products, arithmetic and copies ran while one was open for 9% -> 0% of each run, Pallas kernels for 0% -> 12%
where the time goes in v2:
time: 57.6 us; the launch traced here: 57.4 us
  Pallas kernels  19.7 us (34%)
  starting transfers between devices  19.2 us (33%)
  waiting for transfers between devices  17.4 us (30%)
  other arithmetic  1.06 us (2%)
    pallas_call x6, Pallas kernels, call(): pl.pallas_call(kernel, out_shape=out_shape, in_specs=in_specs, out_specs=...  19.7 us
    ppermute x13, starting transfers between devices, swap(): return lax.ppermute(x, axis, [(i, i ^ offset) for i in range(size)])  19.2 us
    ppermute x13, waiting for transfers between devices, swap(): return lax.ppermute(x, axis, [(i, i ^ offset) for i in range(size)])  17.4 us
  transfers between devices with their start and end apart: 13, of which 7 were waited for; matrix products, arithmetic and copies ran while one was open for 0% of the time, Pallas kernels for 12%

profile of v2, /device:TPU:0, one launch (start us, length us, event | category | flops | bytes accessed | tf_op | source)
XLA Modules:
  0.0 57.4 jit_solution(16120103734186254055)
XLA Ops:
  0.0 1.0 %pack.1 = bf16[32,1408]{1,0:T(8,128)(2,1)S(1)} custom-call(s32[1]{0:T(128)} %bitcast.place_ref.part_ref, bf16[32,1280]{1,0:T(8,128)(2,1)} %refs_0_.3, s32[2,8]{1,0:T(2,128)} %bitcast.58, bf16[4,8]{1,0:T(4,128)(2,1)} %bitcast.59), custom_call_target="tpu_custom_call" | custom-call | tf_op jit(solution)/shard_map/pack/pallas_call | solution.py:300
  1.0 3.1 %collective-permute-start = (bf16[32,1408]{1,0:T(8,128)(2,1)S(1)}, bf16[32,1408]{1,0:T(8,128)(2,1)S(1)}, u32[]{:S(2)}, u32[]{:S(2)}) collective-permute-start(bf16[32,1408]{1,0:T(8,128)(2,1)S(1)} %pack.1), channel_id=1, source_target_pairs={{0,4},{4,0},{8,12},{12,8},{1,5},{5,1},{9,13},{13,9},{2,6},{6,2},{1... | collective-permute-start | bytes 270344 | tf_op jit(solution)/shard_map/ppermute | solution.py:23
  4.1 2.6 %collective-permute-start.1 = (bf16[32,1408]{1,0:T(8,128)(2,1)S(1)}, bf16[32,1408]{1,0:T(8,128)(2,1)S(1)}, u32[]{:S(2)}, u32[]{:S(2)}) collective-permute-start(bf16[32,1408]{1,0:T(8,128)(2,1)S(1)} %pack.1), channel_id=1, source_target_pairs={{0,8},{4,12},{8,0},{12,4},{1,9},{5,13},{9,1},{13,5},{2,10},{6,14},... | collective-permute-start | bytes 270344 | tf_op jit(solution)/shard_map/ppermute | solution.py:23
  6.7 0.0 collective-permute-start.2
  6.7 1.7 %collective-permute-start.4 = (bf16[32,1408]{1,0:T(8,128)(2,1)S(1)}, bf16[32,1408]{1,0:T(8,128)(2,1)S(1)}, u32[]{:S(2)}, u32[]{:S(2)}) collective-permute-start(bf16[32,1408]{1,0:T(8,128)(2,1)S(1)} %pack.1), channel_id=1, source_target_pairs={{0,2},{1,3},{2,0},{3,1},{4,6},{5,7},{6,4},{7,5},{8,10},{9,11},{10,... | collective-permute-start | bytes 270344 | tf_op jit(solution)/shard_map/ppermute | solution.py:23
  8.4 0.0 collective-permute-done
  8.4 5.5 %collective-permute-done.1 = bf16[32,1408]{1,0:T(8,128)(2,1)S(1)} collective-permute-done((bf16[32,1408]{1,0:T(8,128)(2,1)S(1)}, bf16[32,1408]{1,0:T(8,128)(2,1)S(1)}, u32[]{:S(2)}, u32[]{:S(2)}) %collective-permute-start.1) | collective-permute-done | bytes 90144 | tf_op jit(solution)/shard_map/ppermute | solution.py:23
  13.9 0.0 collective-permute-done.2
  13.9 1.6 %collective-permute-start.5 = (bf16[96,1408]{1,0:T(8,128)(2,1)S(1)}, bf16[96,1408]{1,0:T(8,128)(2,1)S(1)}, u32[]{:S(2)}, u32[]{:S(2)}) collective-permute-start(bf16[96,1408]{1,0:T(8,128)(2,1)S(1)} %pad_maximum_fusion.1), channel_id=1, source_target_pairs={{0,2},{1,3},{2,0},{3,1},{4,6},{5,7},{6,4},{7,5},{8,10},{9,11},{10,... | collective-permute-start | bytes 811016 | tf_op jit(solution)/shard_map/ppermute | solution.py:23
  15.5 0.1 collective-permute-start.3
  15.6 0.0 collective-permute-done.4.refs_4_.refs_0_
  15.6 3.5 %project.2 = (f32[128,2048]{1,0:T(8,128)S(1)}, f32[32,512]{1,0:T(8,128)S(1)}, f32[128,128]{1,0:T(8,128)S(1)}) custom-call(s32[1]{0:T(128)} %bitcast.place_ref.part_ref, bf16[128,1408]{1,0:T(8,128)(2,1)S(1)} %pad_maximum_fusion.chunk_ref.refs_0_, f32[4,1,1280]{2,1,0:T(1,128)S(1)} %bitcast.51, bf16[2,5120,512]{2,1,0:T(8,128)(2,1)} %gate.1, ...), custom_call_target="tpu_custom_call" | custom-call | flops 713031680 | bytes 6553600 | tf_op jit(solution)/shard_map/project/pallas_call | solution.py:300
  19.1 1.3 %collective-permute-done.5.refs_1_ = bf16[96,1408]{1,0:T(8,128)(2,1)S(1)} collective-permute-done((bf16[96,1408]{1,0:T(8,128)(2,1)S(1)}, bf16[96,1408]{1,0:T(8,128)(2,1)S(1)}, u32[]{:S(2)}, u32[]{:S(2)}) %collective-permute-start.5) | collective-permute-done | bytes 270368 | tf_op jit(solution)/shard_map/ppermute | solution.py:23
  20.5 0.1 collective-permute-start.6
  20.6 0.1 pad_add_fusion.place_ref
  20.7 0.0 collective-permute-done.3.chunk_ref.refs_1_
  20.7 3.5 %project.3 = (f32[128,2048]{1,0:T(8,128)S(1)}, f32[32,512]{1,0:T(8,128)S(1)}, f32[128,128]{1,0:T(8,128)S(1)}) custom-call(s32[1]{0:T(128)} %bitcast.17.part_ref, bf16[128,1408]{1,0:T(8,128)(2,1)S(1)} %collective-permute-done.3.chunk_ref.refs_1_, f32[4,1,1280]{2,1,0:T(1,128)S(1)} %bitcast.52, ...), custom_call_target="tpu_custom_call", output_to_operand_aliasing={{0}: (7, {}), {1}: (8, {}), {2}: (9, {})} | custom-call | flops 713031680 | bytes 6553600 | tf_op jit(solution)/shard_map/project/pallas_call | solution.py:300
  24.2 0.0 collective-permute-done.6.refs_3_
  24.2 11.6 %finish.1 = (bf16[128,1024]{1,0:T(8,128)(2,1)}, bf16[32,256]{1,0:T(8,128)(2,1)}, f32[2,4,8,5120]{3,2,1,0:T(8,128)S(1)}, bf16[2,4,8,5120]{3,2,1,0:T(8,128)(2,1)S(1)}) custom-call(s32[2]{0:T(128)S(1)} %pad_add_fusion.place_ref, f32[4,1,1280]{2,1,0:T(1,128)S(1)} %bitcast.53, bf16[2,5120,512]{2,1,0:T(8,128)(2,1)} %gate.1, bf16[2,5120,512]{2,1,0:T(8,128)(2,1)} %up.1, ...), custom_call_target="tpu_custom_call" | custom-call | flops 2139095040 | bytes 19660800 | tf_op jit(solution)/shard_map/finish/pallas_call | solution.py:300
  35.8 0.6 collective-permute-start.7
  36.3 1.7 %collective-permute-done.7 = bf16[2,4,8,5120]{3,2,1,0:T(8,128)(2,1)S(1)} collective-permute-done((bf16[2,4,8,5120]{3,2,1,0:T(8,128)(2,1)S(1)}, bf16[2,4,8,5120]{3,2,1,0:T(8,128)(2,1)S(1)}, u32[]{:S(2)}, u32[]{:S(2)}) %collective-permute-start.7) | collective-permute-done | bytes 655392 | tf_op jit(solution)/shard_map/ppermute | solution.py:23
  38.1 0.1 convert_add_fusion.mine_ref
  38.2 1.6 %collective-permute-start.8 = (bf16[2,8,5120]{2,1,0:T(8,128)(2,1)S(1)}, bf16[2,8,5120]{2,1,0:T(8,128)(2,1)S(1)}, u32[]{:S(2)}, u32[]{:S(2)}) collective-permute-start(bf16[2,8,5120]{2,1,0:T(8,128)(2,1)S(1)} %fusion.1), channel_id=1, source_target_pairs={{0,2},{1,3},{2,0},{3,1},{4,6},{5,7},{6,4},{7,5},{8,10},{9,11},{10,... | collective-permute-start | bytes 491528 | tf_op jit(solution)/shard_map/ppermute | solution.py:23
  39.8 5.0 %collective-permute-done.8.refs_0_ = bf16[2,8,5120]{2,1,0:T(8,128)(2,1)S(1)} collective-permute-done((bf16[2,8,5120]{2,1,0:T(8,128)(2,1)S(1)}, bf16[2,8,5120]{2,1,0:T(8,128)(2,1)S(1)}, u32[]{:S(2)}, u32[]{:S(2)}) %collective-permute-start.8) | collective-permute-done | bytes 163872 | tf_op jit(solution)/shard_map/ppermute | solution.py:23
  44.8 1.6 %collective-permute-start.9 = (bf16[2,8,5120]{2,1,0:T(8,128)(2,1)S(1)}, bf16[2,8,5120]{2,1,0:T(8,128)(2,1)S(1)}, u32[]{:S(2)}, u32[]{:S(2)}) collective-permute-start(bf16[2,8,5120]{2,1,0:T(8,128)(2,1)S(1)} %get-tuple-element.24), channel_id=1, source_target_pairs={{0,2},{1,3},{2,0},{3,1},{4,6},{5,7},{6,4},{7,5},{8,10},{9,11},{10,... | collective-permute-start | bytes 491528 | tf_op jit(solution)/shard_map/ppermute | solution.py:23
  46.4 3.2 %collective-permute-start.11 = (bf16[8,5120]{1,0:T(8,128)(2,1)S(1)}, bf16[8,5120]{1,0:T(8,128)(2,1)S(1)}, u32[]{:S(2)}, u32[]{:S(2)}) collective-permute-start(bf16[8,5120]{1,0:T(8,128)(2,1)S(1)} %get-tuple-element.25), channel_id=1, source_target_pairs={{0,8},{4,12},{8,0},{12,4},{1,9},{5,13},{9,1},{13,5},{2,10},{6,14},... | collective-permute-start | bytes 245768 | tf_op jit(solution)/shard_map/ppermute | solution.py:23
  49.6 1.4 %collective-permute-start.12 = (bf16[8,5120]{1,0:T(8,128)(2,1)S(1)}, bf16[8,5120]{1,0:T(8,128)(2,1)S(1)}, u32[]{:S(2)}, u32[]{:S(2)}) collective-permute-start(bf16[8,5120]{1,0:T(8,128)(2,1)S(1)} %get-tuple-element.26), channel_id=1, source_target_pairs={{0,12},{4,8},{8,4},{12,0},{1,13},{5,9},{9,5},{13,1},{2,14},{6,10},... | collective-permute-start | bytes 245768 | tf_op jit(solution)/shard_map/ppermute | solution.py:23
  51.1 1.8 %collective-permute-start.10 = (bf16[8,5120]{1,0:T(8,128)(2,1)S(1)}, bf16[8,5120]{1,0:T(8,128)(2,1)S(1)}, u32[]{:S(2)}, u32[]{:S(2)}) collective-permute-start(bf16[8,5120]{1,0:T(8,128)(2,1)S(1)} %fusion.7), channel_id=1, source_target_pairs={{0,4},{4,0},{8,12},{12,8},{1,5},{5,1},{9,13},{13,9},{2,6},{6,2},{1... | collective-permute-start | bytes 245768 | tf_op jit(solution)/shard_map/ppermute | solution.py:23
  52.9 2.1 %collective-permute-done.11 = bf16[8,5120]{1,0:T(8,128)(2,1)S(1)} collective-permute-done((bf16[8,5120]{1,0:T(8,128)(2,1)S(1)}, bf16[8,5120]{1,0:T(8,128)(2,1)S(1)}, u32[]{:S(2)}, u32[]{:S(2)}) %collective-permute-start.11) | collective-permute-done | bytes 81952 | tf_op jit(solution)/shard_map/ppermute | solution.py:23
  55.0 1.2 %collective-permute-done.12 = bf16[8,5120]{1,0:T(8,128)(2,1)S(1)} collective-permute-done((bf16[8,5120]{1,0:T(8,128)(2,1)S(1)}, bf16[8,5120]{1,0:T(8,128)(2,1)S(1)}, u32[]{:S(2)}, u32[]{:S(2)}) %collective-permute-start.12) | collective-permute-done | bytes 81952 | tf_op jit(solution)/shard_map/ppermute | solution.py:23
  56.3 0.5 collective-permute-done.10
  56.8 0.7 %fusion.6 = bf16[8,5120]{1,0:T(8,128)(2,1)} fusion(f32[8,5120]{1,0:T(8,128)S(1)} %bitcast.57, f32[2,8,5120]{2,1,0:T(8,128)S(1)} %fusion, bf16[8,5120]{1,0:T(8,128)(2,1)S(1)} %collective-permute-done.12, bf16[8,5120]{1,0:T(8,128)(2,1)S(1)} %collective-permute-done.11, bf16[8,5120]{1,0:T(8,128)(2,1)S(1)} %collective-permute-done.10), kind=kLoop, calls=%fused_computation.13 | loop fusion | flops 327680 | bytes 655360 | tf_op jit(solution)/shard_map/convert_element_type | solution.py:477
  (19 shorter events, 0.3 us)
Async XLA Ops:
  0.0 15.6 %copy-start = (f32[5120]{0:T(1024)S(1)}, f32[5120]{0:T(1024)}, u32[]{:S(2)}) copy-start(f32[5120]{0:T(1024)} %param.11) | copy-start | bytes 61444
  1.0 7.4 %collective-permute-start = (bf16[32,1408]{1,0:T(8,128)(2,1)S(1)}, bf16[32,1408]{1,0:T(8,128)(2,1)S(1)}, u32[]{:S(2)}, u32[]{:S(2)}) collective-permute-start(bf16[32,1408]{1,0:T(8,128)(2,1)S(1)} %pack.1), channel_id=1, source_target_pairs={{0,4},{4,0},{8,12},{12,8},{1,5},{5,1},{9,13},{13,9},{2,6},{6,2},{1... | collective-permute-start | bytes 270344 | tf_op jit(solution)/shard_map/ppermute | solution.py:23
  4.1 9.8 %collective-permute-start.1 = (bf16[32,1408]{1,0:T(8,128)(2,1)S(1)}, bf16[32,1408]{1,0:T(8,128)(2,1)S(1)}, u32[]{:S(2)}, u32[]{:S(2)}) collective-permute-start(bf16[32,1408]{1,0:T(8,128)(2,1)S(1)} %pack.1), channel_id=1, source_target_pairs={{0,8},{4,12},{8,0},{12,4},{1,9},{5,13},{9,1},{13,5},{2,10},{6,14},... | collective-permute-start | bytes 270344 | tf_op jit(solution)/shard_map/ppermute | solution.py:23
  6.7 7.2 %collective-permute-start.2 = (bf16[32,1408]{1,0:T(8,128)(2,1)S(1)}, bf16[32,1408]{1,0:T(8,128)(2,1)S(1)}, u32[]{:S(2)}, u32[]{:S(2)}) collective-permute-start(bf16[32,1408]{1,0:T(8,128)(2,1)S(1)} %pack.1), channel_id=1, source_target_pairs={{0,12},{4,8},{8,4},{12,0},{1,13},{5,9},{9,5},{13,1},{2,14},{6,10},... | collective-permute-start | bytes 270344 | tf_op jit(solution)/shard_map/ppermute | solution.py:23
  6.7 8.9 %collective-permute-start.4 = (bf16[32,1408]{1,0:T(8,128)(2,1)S(1)}, bf16[32,1408]{1,0:T(8,128)(2,1)S(1)}, u32[]{:S(2)}, u32[]{:S(2)}) collective-permute-start(bf16[32,1408]{1,0:T(8,128)(2,1)S(1)} %pack.1), channel_id=1, source_target_pairs={{0,2},{1,3},{2,0},{3,1},{4,6},{5,7},{6,4},{7,5},{8,10},{9,11},{10,... | collective-permute-start | bytes 270344 | tf_op jit(solution)/shard_map/ppermute | solution.py:23
  13.9 6.5 %collective-permute-start.5 = (bf16[96,1408]{1,0:T(8,128)(2,1)S(1)}, bf16[96,1408]{1,0:T(8,128)(2,1)S(1)}, u32[]{:S(2)}, u32[]{:S(2)}) collective-permute-start(bf16[96,1408]{1,0:T(8,128)(2,1)S(1)} %pad_maximum_fusion.1), channel_id=1, source_target_pairs={{0,2},{1,3},{2,0},{3,1},{4,6},{5,7},{6,4},{7,5},{8,10},{9,11},{10,... | collective-permute-start | bytes 811016 | tf_op jit(solution)/shard_map/ppermute | solution.py:23
  15.5 5.1 %collective-permute-start.3 = (bf16[128,1408]{1,0:T(8,128)(2,1)S(1)}, bf16[128,1408]{1,0:T(8,128)(2,1)S(1)}, u32[]{:S(2)}, u32[]{:S(2)}) collective-permute-start(bf16[128,1408]{1,0:T(8,128)(2,1)S(1)} %pad_maximum_fusion.chunk_ref.refs_0_), channel_id=1, source_target_pairs={{0,1},{1,0},{2,3},{3,2},{4,5},{5,4},{6,7},{7,6},{8,9},{9,8},{10,11... | collective-permute-start | bytes 1081352 | tf_op jit(solution)/shard_map/ppermute | solution.py:23
  20.5 3.7 %collective-permute-start.6 = (bf16[128,1408]{1,0:T(8,128)(2,1)S(1)}, bf16[128,1408]{1,0:T(8,128)(2,1)S(1)}, u32[]{:S(2)}, u32[]{:S(2)}) collective-permute-start(bf16[128,1408]{1,0:T(8,128)(2,1)S(1)} %join.1.refs_2_), channel_id=1, source_target_pairs={{0,1},{1,0},{2,3},{3,2},{4,5},{5,4},{6,7},{7,6},{8,9},{9,8},{10,11... | collective-permute-start | bytes 1081352 | tf_op jit(solution)/shard_map/ppermute | solution.py:23
  35.8 2.3 %collective-permute-start.7 = (bf16[2,4,8,5120]{3,2,1,0:T(8,128)(2,1)S(1)}, bf16[2,4,8,5120]{3,2,1,0:T(8,128)(2,1)S(1)}, u32[]{:S(2)}, u32[]{:S(2)}) collective-permute-start(bf16[2,4,8,5120]{3,2,1,0:T(8,128)(2,1)S(1)} %get-tuple-element.23), channel_id=1, source_target_pairs={{0,1},{1,0},{2,3},{3,2},{4,5},{5,4},{6,7},{7,6},{8,9},{9,8},{10,11... | collective-permute-start | bytes 1966088 | tf_op jit(solution)/shard_map/ppermute | solution.py:23
  38.2 6.5 %collective-permute-start.8 = (bf16[2,8,5120]{2,1,0:T(8,128)(2,1)S(1)}, bf16[2,8,5120]{2,1,0:T(8,128)(2,1)S(1)}, u32[]{:S(2)}, u32[]{:S(2)}) collective-permute-start(bf16[2,8,5120]{2,1,0:T(8,128)(2,1)S(1)} %fusion.1), channel_id=1, source_target_pairs={{0,2},{1,3},{2,0},{3,1},{4,6},{5,7},{6,4},{7,5},{8,10},{9,11},{10,... | collective-permute-start | bytes 491528 | tf_op jit(solution)/shard_map/ppermute | solution.py:23
  44.8 6.2 %collective-permute-start.9 = (bf16[2,8,5120]{2,1,0:T(8,128)(2,1)S(1)}, bf16[2,8,5120]{2,1,0:T(8,128)(2,1)S(1)}, u32[]{:S(2)}, u32[]{:S(2)}) collective-permute-start(bf16[2,8,5120]{2,1,0:T(8,128)(2,1)S(1)} %get-tuple-element.24), channel_id=1, source_target_pairs={{0,2},{1,3},{2,0},{3,1},{4,6},{5,7},{6,4},{7,5},{8,10},{9,11},{10,... | collective-permute-start | bytes 491528 | tf_op jit(solution)/shard_map/ppermute | solution.py:23
  46.4 8.6 %collective-permute-start.11 = (bf16[8,5120]{1,0:T(8,128)(2,1)S(1)}, bf16[8,5120]{1,0:T(8,128)(2,1)S(1)}, u32[]{:S(2)}, u32[]{:S(2)}) collective-permute-start(bf16[8,5120]{1,0:T(8,128)(2,1)S(1)} %get-tuple-element.25), channel_id=1, source_target_pairs={{0,8},{4,12},{8,0},{12,4},{1,9},{5,13},{9,1},{13,5},{2,10},{6,14},... | collective-permute-start | bytes 245768 | tf_op jit(solution)/shard_map/ppermute | solution.py:23
  49.6 6.6 %collective-permute-start.12 = (bf16[8,5120]{1,0:T(8,128)(2,1)S(1)}, bf16[8,5120]{1,0:T(8,128)(2,1)S(1)}, u32[]{:S(2)}, u32[]{:S(2)}) collective-permute-start(bf16[8,5120]{1,0:T(8,128)(2,1)S(1)} %get-tuple-element.26), channel_id=1, source_target_pairs={{0,12},{4,8},{8,4},{12,0},{1,13},{5,9},{9,5},{13,1},{2,14},{6,10},... | collective-permute-start | bytes 245768 | tf_op jit(solution)/shard_map/ppermute | solution.py:23
  51.1 5.6 %collective-permute-start.10 = (bf16[8,5120]{1,0:T(8,128)(2,1)S(1)}, bf16[8,5120]{1,0:T(8,128)(2,1)S(1)}, u32[]{:S(2)}, u32[]{:S(2)}) collective-permute-start(bf16[8,5120]{1,0:T(8,128)(2,1)S(1)} %fusion.7), channel_id=1, source_target_pairs={{0,4},{4,0},{8,12},{12,8},{1,5},{5,1},{9,13},{13,9},{2,6},{6,2},{1... | collective-permute-start | bytes 245768 | tf_op jit(solution)/shard_map/ppermute | solution.py:23

commit v3 on v2

--- a/solution.py
+++ b/solution.py
@@ -10,7 +10,7 @@
 ROWS = 128
 LANES = 128
 CORES = 2
-WINDOW = 5
+WINDOW = 40
 LATE = 2
 VMEM = pl.BlockSpec(memory_space=pltpu.VMEM)
 SMEM = pl.BlockSpec(memory_space=pltpu.SMEM)
@@ -39,11 +39,11 @@
 
 
 def pack_kernel(pick, experts, place_ref, *refs):
-    sources, (block_ref, rows_ref, ids_ref, gates_ref, sems) = refs[:3], refs[3:]
+    sources, (block_ref, gain_ref, rows_ref, ids_ref, gates_ref, sems) = refs[:4], refs[4:]
     own, depth = rows_ref.shape
     moves = [
         pltpu.make_async_copy(source, target, sems.at[index])
-        for index, (source, target) in enumerate(zip(sources, (rows_ref, ids_ref, gates_ref)))
+        for index, (source, target) in enumerate(zip(sources, (rows_ref, ids_ref, gates_ref, gain_ref)))
     ]
     for move in moves:
         move.start()
@@ -91,12 +91,12 @@
         moves.append(pltpu.make_async_copy(source, target, sems.at[len(moves)]))
 
     blocks = [pl.ds(pl.multiple_of(part * depth, depth), depth) for part in parts]
+    for which, weight in enumerate((s_gate, s_up)):
+        for index, rows in enumerate(blocks):
+            move(weight.at[rows, :], shared_buffer.at[index, which])
     for slot in range(experts * 2):
         for index, rows in enumerate(blocks):
             move((gate, up)[slot % 2].at[slot // 2, rows, :], buffer.at[index, slot])
-    for which, weight in enumerate((s_gate, s_up)):
-        for index, rows in enumerate(blocks):
-            move(weight.at[rows, :], shared_buffer.at[index, which])
     return moves
 
 
@@ -124,15 +124,6 @@
     queue = Queue(weight_moves([part], weights, (buffer, shared_buffer), sems))
     square_sums(chunk_ref, gain_ref[part], lhs_ref, square_ref, square_in)
     inner, shared_inner = buffer.shape[3], shared_buffer.shape[3]
-    for slot in range(buffer.shape[1]):
-        queue.wait()
-        columns = slice(slot * inner, (slot + 1) * inner)
-
-        def body(rows):
-            term = jnp.dot(lhs_ref[rows, :], buffer[0, slot], preferred_element_type=jnp.float32)
-            acc_ref[rows, columns] = term if first else term + acc_in[rows, columns]
-
-        row_loop(chunk_ref.shape[0], body)
     own = shared_ref.shape[0]
     for which in range(2):
         queue.wait()
@@ -141,6 +132,15 @@
             lhs_ref[:own, :], shared_buffer[0, which], preferred_element_type=jnp.float32
         )
         shared_ref[:, columns] = term if first else term + shared_in[:, columns]
+    for slot in range(buffer.shape[1]):
+        queue.wait()
+        columns = slice(slot * inner, (slot + 1) * inner)
+
+        def body(rows):
+            term = jnp.dot(lhs_ref[rows, :], buffer[0, slot], preferred_element_type=jnp.float32)
+            acc_ref[rows, columns] = term if first else term + acc_in[rows, columns]
+
+        row_loop(chunk_ref.shape[0], body)
 
 
 def join_kernel(count, *refs):
@@ -151,16 +151,16 @@
         start += ref.shape[0]
 
 
-def relay_kernel(half, mine_ref, *refs):
-    pairs, nodes = mine_ref.shape[:2]
-    came, sums, near = refs[: pairs - 1], refs[pairs - 1 : pairs - 1 + nodes - half], refs[pairs - 1 + nodes - half :]
+def relay_kernel(far_ref, near_ref, *refs):
+    pairs, nodes = far_ref.shape[:2]
+    came, sums, near = refs[: pairs - 1], refs[pairs - 1 : pairs - 1 + nodes], refs[pairs - 1 + nodes :]
     for index, sum_ref in enumerate(sums):
-        total = mine_ref[0, half + index]
+        total = far_ref[0, index]
         for ref in came:
             total = total + ref[index].astype(jnp.float32)
         sum_ref[...] = total.astype(jnp.bfloat16)
     for pair, ref in enumerate(near):
-        ref[...] = mine_ref[pair + 1, :half].astype(jnp.bfloat16)
+        ref[...] = near_ref[pair + 1].astype(jnp.bfloat16)
 
 
 def act(gate, up):
@@ -177,59 +177,58 @@
     return share
 
 
-def down_part(me, hidden_ref, shared_hidden_ref, wait, down, s_down, out_ref, keep_ref, send_ref):
-    experts, inner = down.shape[0], down.shape[1]
+def row_blocks(total):
+    block = min(ROWS, total)
+    return [slice(start, start + block) for start in range(0, total, block)]
+
+
+def down_expert(hidden_ref, shared_hidden_ref, expert, first, down, s_down, out_ref):
+    inner = down.shape[1]
+    count, _, step = out_ref.shape
     own = shared_hidden_ref.shape[0]
-    for expert in range(experts):
-        wait()
-
-        def body(rows):
+    for index in range(count):
+        taken = slice(first + index * step, first + (index + 1) * step)
+        for rows in row_blocks(hidden_ref.shape[0]):
             term = jnp.dot(
                 hidden_ref[rows, expert * inner : (expert + 1) * inner],
-                down[expert],
+                down[expert, :, taken],
                 preferred_element_type=jnp.float32,
             )
-            out_ref[rows, :] = term if expert == 0 else term + out_ref[rows, :]
-
-        row_loop(hidden_ref.shape[0], body)
-    wait()
-    out_ref[:own, :] += jnp.dot(
-        shared_hidden_ref[...], s_down[...], preferred_element_type=jnp.float32
-    )
-    pairs, nodes, tokens = keep_ref.shape[:3]
-    for pair in range(pairs):
-        for side, to_ref in enumerate((keep_ref, send_ref)):
-            place = lax.bitwise_xor(me, pair * CORES + side) * tokens
-            for other in range(nodes):
-                rows = pl.ds(pl.multiple_of(other * own + place, tokens), tokens)
-                to_ref[pair, other] = out_ref[rows, :].astype(to_ref.dtype)
-
-
-def down_moves(columns, down, s_down, buffer, shared_buffer, sems, base):
-    experts = down.shape[0]
-    moves = [
-        pltpu.make_async_copy(down.at[e, :, columns], buffer.at[e], sems.at[base + e])
-        for e in range(experts)
-    ]
-    return moves + [
-        pltpu.make_async_copy(s_down.at[:, columns], shared_buffer, sems.at[base + experts])
-    ]
+            out_ref[index, rows, :] = term if expert == 0 else term + out_ref[index, rows, :]
+        if expert == 0:
+            out_ref[index, :own, :] += jnp.dot(
+                shared_hidden_ref[...], s_down[:, taken], preferred_element_type=jnp.float32
+            )
+
+
+def leave(me, own, out_ref, outs):
+    count, _, step = out_ref.shape
+    keep_far, keep_near, send_far, send_near = outs
+    pairs, near, tokens = keep_near.shape[:3]
+    for index in range(count):
+        columns = slice(index * step, (index + 1) * step)
+        for pair in range(pairs):
+            for side, to_refs in enumerate(((keep_near, keep_far), (send_near, send_far))):
+                place = lax.bitwise_xor(me, pair * CORES + side) * tokens
+                for other in range(near + keep_far.shape[1]):
+                    rows = pl.ds(pl.multiple_of(other * own + place, tokens), tokens)
+                    to_ref = to_refs[other >= near]
+                    to_ref[pair, other % near, :, columns] = out_ref[index, rows, :].astype(to_ref.dtype)
 
 
 def finish_kernel(
-    width, pick, columns, part_count, place_ref, gain_ref, gate, up, s_gate, s_up,
+    width, pick, part_count, place_ref, gain_ref, gate, up, s_gate, s_up,
     acc_in, shared_in, square_in, down, s_down, *refs
 ):
     chunks, refs = refs[:part_count], refs[part_count:]
     (
-        hidden_ref, shared_hidden_ref, keep_ref, send_ref,
-        lhs_ref, square_ref, buffer, shared_buffer, down_buffer, s_down_buffer, out_ref, sems,
+        hidden_ref, shared_hidden_ref, *outs,
+        lhs_ref, square_ref, share_ref, buffer, shared_buffer, out_ref, sems,
     ) = refs
     me, node = place_ref[0], place_ref[1]
     late = buffer.shape[0]
     parts = [lax.bitwise_xor(me, part_count - late + index) for index in range(late)]
     moves = weight_moves(parts, (gate, up, s_gate, s_up), (buffer, shared_buffer), sems)
-    moves += down_moves(columns, down, s_down, down_buffer, s_down_buffer, sems, len(moves))
     queue = Queue(moves)
     experts, inner, shared_inner = gate.shape[0], gate.shape[2], s_gate.shape[1]
     own, depth = shared_in.shape[0], gain_ref.shape[2]
@@ -238,58 +237,57 @@
             chunks[index - late], gain_ref[part], lhs_ref.at[index], square_ref,
             square_ref if index else square_in,
         )
-    for expert in range(experts):
-
-        def body(rows):
-            tag = sum(chunk[rows, depth:].astype(jnp.float32) for chunk in chunks)
-            scale = lax.rsqrt(square_ref[rows, :][:, :1] / width + 1e-06)
-            projs = []
-            for slot in (2 * expert, 2 * expert + 1):
-                term = acc_in[rows, slot * inner : (slot + 1) * inner]
-                for index in range(late):
-                    term = term + jnp.dot(
-                        lhs_ref[index, rows, :],
-                        buffer[index, slot],
-                        preferred_element_type=jnp.float32,
-                    )
-                projs.append(term * scale)
+    blocks = row_blocks(chunks[-1].shape[0])
+    for rows in blocks:
+        tag = sum(chunk[rows, depth:].astype(jnp.float32) for chunk in chunks)
+        for expert in range(experts):
             share = row_share(tag, node, pick, experts, expert)
-            hidden_ref[rows, expert * inner : (expert + 1) * inner] = (
-                act(*projs) * share
-            ).astype(jnp.bfloat16)
-
-        for _ in range(2 * late):
+            share_ref[expert, rows, :] = jnp.broadcast_to(share, (share.shape[0], LANES))
+        square_ref[rows, :] = lax.rsqrt(square_ref[rows, :] / width + 1e-06)
+
+    def project(rows_list, before, weights):
+        terms = [before[rows] for rows in rows_list]
+        for index in range(late):
             queue.wait()
-        row_loop(chunks[-1].shape[0], body)
-    scale = lax.rsqrt(square_ref[:own, :][:, :1] / width + 1e-06)
+            for at, rows in enumerate(rows_list):
+                terms[at] = terms[at] + jnp.dot(
+                    lhs_ref[index, rows, :], weights(index), preferred_element_type=jnp.float32
+                )
+        return [term * square_ref[rows, :][:, :1] for term, rows in zip(terms, rows_list)]
+
+    class Columns:
+        def __init__(self, ref, start, count):
+            self.ref, self.columns = ref, slice(start, start + count)
+
+        def __getitem__(self, rows):
+            return self.ref[rows, self.columns]
+
     projs = []
     for which in range(2):
-        term = shared_in[:, which * shared_inner : (which + 1) * shared_inner]
-        for index in range(late):
-            queue.wait()
-            term = term + jnp.dot(
-                lhs_ref[index, :own, :],
-                shared_buffer[index, which],
-                preferred_element_type=jnp.float32,
-            )
-        projs.append(term * scale)
+        before = Columns(shared_in, which * shared_inner, shared_inner)
+        projs += project([slice(0, own)], before, lambda index: shared_buffer[index, which])
     shared_hidden_ref[...] = act(*projs).astype(jnp.bfloat16)
-    down_part(
-        me, hidden_ref, shared_hidden_ref, queue.wait, down_buffer, s_down_buffer,
-        out_ref, keep_ref, send_ref,
-    )
-
-
-def down_kernel(columns, place_ref, hidden_ref, shared_hidden_ref, down, s_down, keep_ref, send_ref, buffer, shared_buffer, out_ref, sems):
-    queue = Queue(down_moves(columns, down, s_down, buffer, shared_buffer, sems, 0))
-    down_part(
-        place_ref[0], hidden_ref, shared_hidden_ref, queue.wait, buffer, shared_buffer,
-        out_ref, keep_ref, send_ref,
-    )
+    for expert in range(experts):
+        projs = []
+        for slot in (2 * expert, 2 * expert + 1):
+            before = Columns(acc_in, slot * inner, inner)
+            projs.append(project(blocks, before, lambda index: buffer[index, slot]))
+        for rows, gate_proj, up_proj in zip(blocks, *projs):
+            hidden_ref[rows, expert * inner : (expert + 1) * inner] = (
+                act(gate_proj, up_proj) * share_ref[expert, rows, :][:, :1]
+            ).astype(jnp.bfloat16)
+        down_expert(hidden_ref, shared_hidden_ref, expert, 0, down, s_down, out_ref)
+    leave(me, own, out_ref, outs)
+
+
+def down_kernel(first, place_ref, hidden_ref, shared_hidden_ref, down, s_down, *refs):
+    for expert in range(down.shape[0]):
+        down_expert(hidden_ref, shared_hidden_ref, expert, first, down, s_down, refs[-1])
+    leave(place_ref[0], shared_hidden_ref.shape[0], refs[-1], refs[:4])
 
 
 def call(kernel, name, out_shape, in_specs, scratch, args, flops=0, read=0, aliases=None):
-    held = [a for a, spec in zip(args, in_specs) if spec is VMEM] + list(out_shape)
+    held = [a for a, spec in zip(args, in_specs) if spec is VMEM and a.ndim < 3] + list(out_shape)
     held += [s for s in scratch if hasattr(s, "dtype") and s.memory_space == pltpu.VMEM]
     size = 0
     for array in held:
@@ -321,21 +319,26 @@
     shared_inner = s_gate.shape[1]
     total = node_count * own
     up_weights = tuple(in_hbm(w) for w in (w_gate, w_up, s_gate, s_up))
-    down_weights = tuple(in_hbm(w) for w in (w_down, s_down))
+    down_weights = (w_down, s_down)
     f32, bf16 = jnp.float32, jnp.bfloat16
 
     inputs = (
         in_hbm(attended),
         in_hbm(node_ids.T),
         in_hbm(gates.transpose(1, 2, 0).reshape(pick * experts, tokens)),
+        in_hbm(norm_gain.reshape(local_count, 1, depth)),
     )
-    (block,) = call(
+    block, gain = call(
         functools.partial(pack_kernel, pick, experts),
         "pack",
-        [jax.ShapeDtypeStruct((own, depth + LANES), bf16)],
-        [SMEM, HBM, HBM, HBM],
-        [pltpu.VMEM(x.shape, x.dtype) for x in inputs] + [pltpu.SemaphoreType.DMA((3,))],
+        [
+            jax.ShapeDtypeStruct((own, depth + LANES), bf16),
+            jax.ShapeDtypeStruct((local_count, 1, depth), f32),
+        ],
+        [SMEM] + [HBM] * 4,
+        [pltpu.VMEM(x.shape, x.dtype) for x in inputs[:3]] + [pltpu.SemaphoreType.DMA((4,))],
         (me[None], *inputs),
+        flops=4 * 10**10,
     )
     blocks = [block] + [swap(block, "node", k) for k in range(1, node_count)]
     rest = jnp.concatenate(blocks[1:], axis=0)
@@ -356,7 +359,6 @@
     first_rows = [swap(block, "local", k * CORES) for k in range(1, pairs)]
     other_rows = [swap(rest, "local", k * CORES) for k in range(1, pairs)]
 
-    gain = norm_gain.reshape(local_count, 1, depth)
     sums_shape = [
         jax.ShapeDtypeStruct((total, experts * 2 * inner), f32),
         jax.ShapeDtypeStruct((own, 2 * shared_inner), f32),
@@ -393,71 +395,73 @@
 
     slices = max(1, total // ROWS)
     step = width // slices
-    shape = (pairs, node_count, tokens, step)
-    out_shape = [jax.ShapeDtypeStruct(shape, f32), jax.ShapeDtypeStruct(shape, bf16)]
+    half = node_count // 2
+    out_shape = [
+        jax.ShapeDtypeStruct((pairs, half, tokens, step), dtype)
+        for dtype in (f32, f32, bf16, bf16)
+    ]
+    pieces = max(1, step // (10 * LANES))
     down_scratch = [
-        pltpu.VMEM((experts, inner, step), bf16),
-        pltpu.VMEM((shared_inner, step), bf16),
-        pltpu.VMEM((total, step), f32),
+        pltpu.VMEM((pieces, total, step // pieces), f32),
     ]
     down_flops = 2 * step * (total * experts * inner + own * shared_inner)
     down_read = 2 * step * (experts * inner + shared_inner)
     partials = []
     for index in range(slices):
-        columns = slice(index * step, (index + 1) * step)
         if index == 0:
-            hidden, shared_hidden, keep, send = call(
-                functools.partial(finish_kernel, width, pick, columns, local_count),
+            hidden, shared_hidden, *out = call(
+                functools.partial(finish_kernel, width, pick, local_count),
                 "finish",
                 [
                     jax.ShapeDtypeStruct((total, experts * inner), bf16),
                     jax.ShapeDtypeStruct((own, shared_inner), bf16),
                 ]
                 + out_shape,
-                [SMEM, VMEM] + [HBM] * 4 + [VMEM] * 3 + [HBM] * 2 + [VMEM] * local_count,
+                [SMEM, VMEM] + [HBM] * 4 + [VMEM] * (5 + local_count),
                 [
                     pltpu.VMEM((LATE, total, depth), bf16),
                     pltpu.VMEM((total, LANES), f32),
+                    pltpu.VMEM((experts, total, LANES), f32),
                     *(pltpu.VMEM((LATE, *w.shape[1:]), bf16) for w in weight_scratch),
                     *down_scratch,
-                    pltpu.SemaphoreType.DMA((LATE * moves + experts + 1,)),
+                    pltpu.SemaphoreType.DMA((LATE * moves,)),
                 ],
                 (place, gain, *up_weights, *sums, *down_weights, *chunks),
                 flops + down_flops,
                 read + down_read,
             )
         else:
-            keep, send = call(
-                functools.partial(down_kernel, columns),
+            out = call(
+                functools.partial(down_kernel, index * step),
                 "down",
                 out_shape,
-                [SMEM, VMEM, VMEM, HBM, HBM],
-                [*down_scratch, pltpu.SemaphoreType.DMA((experts + 1,))],
+                [SMEM] + [VMEM] * 4,
+                down_scratch,
                 (place, hidden, shared_hidden, *down_weights),
                 down_flops,
                 down_read,
             )
-        partials.append((keep, send))
-
-    half = node_count // 2
+        partials.append(out)
+
     results = []
-    for keep, send in partials:
-        mine = keep + swap(send, "local", 1).astype(f32)
-        came = [swap(mine[k, half:].astype(bf16), "local", k * CORES) for k in range(1, pairs)]
+    for keep_far, keep_near, send_far, send_near in partials:
+        far = keep_far + swap(send_far, "local", 1).astype(f32)
+        came = [swap(far[k].astype(bf16), "local", k * CORES) for k in range(1, pairs)]
+        near = keep_near + swap(send_near, "local", 1).astype(f32)
         rows_shape = jax.ShapeDtypeStruct((tokens, step), bf16)
         near_shape = jax.ShapeDtypeStruct((half, tokens, step), bf16)
         out = call(
-            functools.partial(relay_kernel, half),
+            relay_kernel,
             "relay",
             [rows_shape] * (node_count - half) + [near_shape] * (pairs - 1),
-            [VMEM] * pairs,
+            [VMEM] * (pairs + 1),
             [],
-            (mine, *came),
+            (far, near, *came),
         )
-        far, near = out[: node_count - half], out[node_count - half :]
-        near_came = [swap(x, "local", k * CORES).astype(f32) for k, x in enumerate(near, 1)]
-        far_came = [swap(x, "node", half + k).astype(f32) for k, x in enumerate(far)]
-        result = sum(near_came, mine[0, :half])
+        far_rows, near_rows = out[: node_count - half], out[node_count - half :]
+        near_came = [swap(x, "local", k * CORES).astype(f32) for k, x in enumerate(near_rows, 1)]
+        far_came = [swap(x, "node", half + k).astype(f32) for k, x in enumerate(far_rows)]
+        result = sum(near_came, near[0])
         total_here = result[0]
         for k in range(1, half):
             total_here = total_here + swap(result[k].astype(bf16), "node", k).astype(f32)

time: 57.6 us -> 54.7 us (0.950)
  Pallas kernels: 19.7 us -> 16.5 us
  local copies, waits for them, and re-layouts: 0.06 us -> 1.03 us
  waiting for transfers between devices: 17.4 us -> 16.7 us
    pallas_call x6, Pallas kernels: 19.7 us -> 16.5 us  [call(): pl.pallas_call(kernel, out_shape=out_shape, in_specs=in_specs, out_specs=...]
    unnamed x2 -> x11, local copies, waits for them, and re-layouts: 0.01 us -> 0.93 us
    ppermute x13 -> x14, waiting for transfers between devices: 17.4 us -> 16.7 us  [swap(): return lax.ppermute(x, axis, [(i, i ^ offset) for i in range(size)])]
    ppermute x13 -> x14, starting transfers between devices: 19.2 us -> 19 us  [swap(): return lax.ppermute(x, axis, [(i, i ^ offset) for i in range(size)])]
  transfers between devices with their start and end apart: 13 -> 14, of which waited for: 7 -> 7; matrix products, arithmetic and copies ran while one was open for 0% -> 1% of each run, Pallas kernels for 12% -> 13%
where the time goes in v3:
time: 54.7 us; the launch traced here: 54.6 us
  starting transfers between devices  19 us (35%)
  waiting for transfers between devices  16.7 us (31%)
  Pallas kernels  16.5 us (30%)
  local copies, waits for them, and re-layouts  1.03 us (2%)
  other arithmetic  1.02 us (2%)
    ppermute x14, starting transfers between devices, swap(): return lax.ppermute(x, axis, [(i, i ^ offset) for i in range(size)])  19 us
    ppermute x14, waiting for transfers between devices, swap(): return lax.ppermute(x, axis, [(i, i ^ offset) for i in range(size)])  16.7 us
    pallas_call x6, Pallas kernels, call(): pl.pallas_call(kernel, out_shape=out_shape, in_specs=in_specs, out_specs=...  16.5 us
  transfers between devices with their start and end apart: 14, of which 7 were waited for; matrix products, arithmetic and copies ran while one was open for 1% of the time, Pallas kernels for 13%

profile of v3, /device:TPU:0, one launch (start us, length us, event | category | flops | bytes accessed | tf_op | source)
XLA Modules:
  0.0 54.6 jit_solution(466890139164496701)
XLA Ops:
  0.0 1.0 %pack.1 = (bf16[32,1408]{1,0:T(8,128)(2,1)S(1)}, f32[4,1,1280]{2,1,0:T(1,128)S(1)}) custom-call(s32[1]{0:T(128)} %bitcast.place_ref.part_ref, bf16[32,1280]{1,0:T(8,128)(2,1)} %refs_0_.3, s32[2,8]{1,0:T(2,128)} %bitcast.58, bf16[4,8]{1,0:T(4,128)(2,1)} %bitcast.59, f32[4,1,1280]{2,1,0:T(1,128)} %bitcast.57), custom_call_target="tpu_custom_call" | custom-call | flops 40000000000 | tf_op jit(solution)/shard_map/pack/pallas_call | solution.py:298
  1.0 3.1 %collective-permute-start = (bf16[32,1408]{1,0:T(8,128)(2,1)S(1)}, bf16[32,1408]{1,0:T(8,128)(2,1)S(1)}, u32[]{:S(2)}, u32[]{:S(2)}) collective-permute-start(bf16[32,1408]{1,0:T(8,128)(2,1)S(1)} %get-tuple-element.20), channel_id=1, source_target_pairs={{0,4},{4,0},{8,12},{12,8},{1,5},{5,1},{9,13},{13,9},{2,6},{6,2},{1... | collective-permute-start | bytes 270344 | tf_op jit(solution)/shard_map/ppermute | solution.py:23
  4.1 2.6 %collective-permute-start.1 = (bf16[32,1408]{1,0:T(8,128)(2,1)S(1)}, bf16[32,1408]{1,0:T(8,128)(2,1)S(1)}, u32[]{:S(2)}, u32[]{:S(2)}) collective-permute-start(bf16[32,1408]{1,0:T(8,128)(2,1)S(1)} %get-tuple-element.20), channel_id=1, source_target_pairs={{0,8},{4,12},{8,0},{12,4},{1,9},{5,13},{9,1},{13,5},{2,10},{6,14},... | collective-permute-start | bytes 270344 | tf_op jit(solution)/shard_map/ppermute | solution.py:23
  6.7 1.7 %collective-permute-start.4 = (bf16[32,1408]{1,0:T(8,128)(2,1)S(1)}, bf16[32,1408]{1,0:T(8,128)(2,1)S(1)}, u32[]{:S(2)}, u32[]{:S(2)}) collective-permute-start(bf16[32,1408]{1,0:T(8,128)(2,1)S(1)} %get-tuple-element.20), channel_id=1, source_target_pairs={{0,2},{1,3},{2,0},{3,1},{4,6},{5,7},{6,4},{7,5},{8,10},{9,11},{10,... | collective-permute-start | bytes 270344 | tf_op jit(solution)/shard_map/ppermute | solution.py:23
  8.4 0.1 pad_add_fusion.place_ref
  8.5 5.4 %collective-permute-done.1 = bf16[32,1408]{1,0:T(8,128)(2,1)S(1)} collective-permute-done((bf16[32,1408]{1,0:T(8,128)(2,1)S(1)}, bf16[32,1408]{1,0:T(8,128)(2,1)S(1)}, u32[]{:S(2)}, u32[]{:S(2)}) %collective-permute-start.1) | collective-permute-done | bytes 90144 | tf_op jit(solution)/shard_map/ppermute | solution.py:23
  13.9 1.6 %collective-permute-start.5 = (bf16[96,1408]{1,0:T(8,128)(2,1)S(1)}, bf16[96,1408]{1,0:T(8,128)(2,1)S(1)}, u32[]{:S(2)}, u32[]{:S(2)}) collective-permute-start(bf16[96,1408]{1,0:T(8,128)(2,1)S(1)} %pad_maximum_fusion), channel_id=1, source_target_pairs={{0,2},{1,3},{2,0},{3,1},{4,6},{5,7},{6,4},{7,5},{8,10},{9,11},{10,... | collective-permute-start | bytes 811016 | tf_op jit(solution)/shard_map/ppermute | solution.py:23
  15.6 0.1 collective-permute-start.3
  15.7 3.4 %project.2 = (f32[128,2048]{1,0:T(8,128)S(1)}, f32[32,512]{1,0:T(8,128)S(1)}, f32[128,128]{1,0:T(8,128)S(1)}) custom-call(s32[1]{0:T(128)} %bitcast.place_ref.part_ref, bf16[128,1408]{1,0:T(8,128)(2,1)S(1)} %constant_dynamic-update-slice_fusion.chunk_ref.refs_0_, f32[4,1,1280]{2,1,0:T(1,128)S(1)} %get-tuple-element.21.gain_ref, bf16[2,5120,512]{2,1,0:T(8,128)(2,1)} %gate.1, ...), custom_call_target="tpu_custom_call" | custom-call | flops 713031680 | bytes 6553600 | tf_op jit(solution)/shard_map/project/pallas_call | solution.py:298
  19.1 1.3 %collective-permute-done.5.refs_1_ = bf16[96,1408]{1,0:T(8,128)(2,1)S(1)} collective-permute-done((bf16[96,1408]{1,0:T(8,128)(2,1)S(1)}, bf16[96,1408]{1,0:T(8,128)(2,1)S(1)}, u32[]{:S(2)}, u32[]{:S(2)}) %collective-permute-start.5) | collective-permute-done | bytes 270368 | tf_op jit(solution)/shard_map/ppermute | solution.py:23
  20.5 0.1 collective-permute-start.6
  20.6 0.0 slice-start.2
  20.6 3.4 %project.3 = (f32[128,2048]{1,0:T(8,128)S(1)}, f32[32,512]{1,0:T(8,128)S(1)}, f32[128,128]{1,0:T(8,128)S(1)}) custom-call(s32[1]{0:T(128)} %bitcast.17.part_ref, bf16[128,1408]{1,0:T(8,128)(2,1)S(1)} %collective-permute-done.3.chunk_ref.refs_1_, ...), custom_call_target="tpu_custom_call", output_to_operand_aliasing={{0}: (7, {}), {1}: (8, {}), {2}: (9, {})} | custom-call | flops 713031680 | bytes 6553600 | tf_op jit(solution)/shard_map/project/pallas_call | solution.py:298
  24.1 0.1 slice-done.2
  24.3 0.8 %copy-done = bf16[256,5120]{1,0:T(8,128)(2,1)S(1)} copy-done((bf16[256,5120]{1,0:T(8,128)(2,1)S(1)}, bf16[256,5120]{1,0:T(8,128)(2,1)}, u32[]{:S(2)}) %copy-start) | copy-done | bytes 2621464
  25.0 8.6 %finish.1 = (bf16[128,1024]{1,0:T(8,128)(2,1)}, bf16[32,256]{1,0:T(8,128)(2,1)}, f32[2,2,8,5120]{3,2,1,0:T(8,128)S(1)}, f32[2,2,8,5120]{3,2,1,0:T(8,128)S(1)}, b...) custom-call(s32[2]{0:T(128)S(1)} %pad_add_fusion.place_ref, ...), custom_call_target="tpu_custom_call" | custom-call | flops 2139095040 | bytes 19660800 | tf_op jit(solution)/shard_map/finish/pallas_call | solution.py:298
  33.6 0.5 collective-permute-start.8
  34.1 0.1 collective-permute-start.7
  34.2 1.2 %collective-permute-done.8 = bf16[2,2,8,5120]{3,2,1,0:T(8,128)(2,1)S(1)} collective-permute-done((bf16[2,2,8,5120]{3,2,1,0:T(8,128)(2,1)S(1)}, bf16[2,2,8,5120]{3,2,1,0:T(8,128)(2,1)S(1)}, u32[]{:S(2)}, u32[]{:S(2)}) %collective-permute-start.8) | collective-permute-done | bytes 327712 | tf_op jit(solution)/shard_map/ppermute | solution.py:23
  35.4 0.1 convert_add_fusion.far_ref
  35.5 1.5 %collective-permute-start.9 = (bf16[2,8,5120]{2,1,0:T(8,128)(2,1)S(1)}, bf16[2,8,5120]{2,1,0:T(8,128)(2,1)S(1)}, u32[]{:S(2)}, u32[]{:S(2)}) collective-permute-start(bf16[2,8,5120]{2,1,0:T(8,128)(2,1)S(1)} %fusion.1), channel_id=1, source_target_pairs={{0,2},{1,3},{2,0},{3,1},{4,6},{5,7},{6,4},{7,5},{8,10},{9,11},{10,... | collective-permute-start | bytes 491528 | tf_op jit(solution)/shard_map/ppermute | solution.py:23
  37.0 0.1 convert_add_fusion.1.near_ref
  37.0 5.0 %collective-permute-done.9.refs_0_ = bf16[2,8,5120]{2,1,0:T(8,128)(2,1)S(1)} collective-permute-done((bf16[2,8,5120]{2,1,0:T(8,128)(2,1)S(1)}, bf16[2,8,5120]{2,1,0:T(8,128)(2,1)S(1)}, u32[]{:S(2)}, u32[]{:S(2)}) %collective-permute-start.9) | collective-permute-done | bytes 163872 | tf_op jit(solution)/shard_map/ppermute | solution.py:23
  42.0 0.1 relay.1
  42.1 1.5 %collective-permute-start.10 = (bf16[2,8,5120]{2,1,0:T(8,128)(2,1)S(1)}, bf16[2,8,5120]{2,1,0:T(8,128)(2,1)S(1)}, u32[]{:S(2)}, u32[]{:S(2)}) collective-permute-start(bf16[2,8,5120]{2,1,0:T(8,128)(2,1)S(1)} %get-tuple-element.32), channel_id=1, source_target_pairs={{0,2},{1,3},{2,0},{3,1},{4,6},{5,7},{6,4},{7,5},{8,10},{9,11},{10,... | collective-permute-start | bytes 491528 | tf_op jit(solution)/shard_map/ppermute | solution.py:23
  43.6 3.2 %collective-permute-start.12 = (bf16[8,5120]{1,0:T(8,128)(2,1)S(1)}, bf16[8,5120]{1,0:T(8,128)(2,1)S(1)}, u32[]{:S(2)}, u32[]{:S(2)}) collective-permute-start(bf16[8,5120]{1,0:T(8,128)(2,1)S(1)} %get-tuple-element.33), channel_id=1, source_target_pairs={{0,8},{4,12},{8,0},{12,4},{1,9},{5,13},{9,1},{13,5},{2,10},{6,14},... | collective-permute-start | bytes 245768 | tf_op jit(solution)/shard_map/ppermute | solution.py:23
  46.8 1.5 %collective-permute-start.13 = (bf16[8,5120]{1,0:T(8,128)(2,1)S(1)}, bf16[8,5120]{1,0:T(8,128)(2,1)S(1)}, u32[]{:S(2)}, u32[]{:S(2)}) collective-permute-start(bf16[8,5120]{1,0:T(8,128)(2,1)S(1)} %get-tuple-element.34), channel_id=1, source_target_pairs={{0,12},{4,8},{8,4},{12,0},{1,13},{5,9},{9,5},{13,1},{2,14},{6,10},... | collective-permute-start | bytes 245768 | tf_op jit(solution)/shard_map/ppermute | solution.py:23
  48.3 1.8 %collective-permute-start.11 = (bf16[8,5120]{1,0:T(8,128)(2,1)S(1)}, bf16[8,5120]{1,0:T(8,128)(2,1)S(1)}, u32[]{:S(2)}, u32[]{:S(2)}) collective-permute-start(bf16[8,5120]{1,0:T(8,128)(2,1)S(1)} %fusion.7), channel_id=1, source_target_pairs={{0,4},{4,0},{8,12},{12,8},{1,5},{5,1},{9,13},{13,9},{2,6},{6,2},{1... | collective-permute-start | bytes 245768 | tf_op jit(solution)/shard_map/ppermute | solution.py:23
  50.1 2.1 %collective-permute-done.12 = bf16[8,5120]{1,0:T(8,128)(2,1)S(1)} collective-permute-done((bf16[8,5120]{1,0:T(8,128)(2,1)S(1)}, bf16[8,5120]{1,0:T(8,128)(2,1)S(1)}, u32[]{:S(2)}, u32[]{:S(2)}) %collective-permute-start.12) | collective-permute-done | bytes 81952 | tf_op jit(solution)/shard_map/ppermute | solution.py:23
  52.2 1.2 %collective-permute-done.13 = bf16[8,5120]{1,0:T(8,128)(2,1)S(1)} collective-permute-done((bf16[8,5120]{1,0:T(8,128)(2,1)S(1)}, bf16[8,5120]{1,0:T(8,128)(2,1)S(1)}, u32[]{:S(2)}, u32[]{:S(2)}) %collective-permute-start.13) | collective-permute-done | bytes 81952 | tf_op jit(solution)/shard_map/ppermute | solution.py:23
  53.4 0.5 collective-permute-done.11
  53.9 0.7 %fusion.6 = bf16[8,5120]{1,0:T(8,128)(2,1)} fusion(f32[8,5120]{1,0:T(8,128)S(1)} %bitcast.56, f32[2,8,5120]{2,1,0:T(8,128)S(1)} %fusion, bf16[8,5120]{1,0:T(8,128)(2,1)S(1)} %collective-permute-done.13, bf16[8,5120]{1,0:T(8,128)(2,1)S(1)} %collective-permute-done.12, bf16[8,5120]{1,0:T(8,128)(2,1)S(1)} %collective-permute-done.11), kind=kLoop, calls=%fused_computation.13 | loop fusion | flops 327680 | bytes 655360 | tf_op jit(solution)/shard_map/convert_element_type | solution.py:481
  (32 shorter events, 0.3 us)
Async XLA Ops:
  1.0 7.5 %collective-permute-start = (bf16[32,1408]{1,0:T(8,128)(2,1)S(1)}, bf16[32,1408]{1,0:T(8,128)(2,1)S(1)}, u32[]{:S(2)}, u32[]{:S(2)}) collective-permute-start(bf16[32,1408]{1,0:T(8,128)(2,1)S(1)} %get-tuple-element.20), channel_id=1, source_target_pairs={{0,4},{4,0},{8,12},{12,8},{1,5},{5,1},{9,13},{13,9},{2,6},{6,2},{1... | collective-permute-start | bytes 270344 | tf_op jit(solution)/shard_map/ppermute | solution.py:23
  4.1 9.8 %collective-permute-start.1 = (bf16[32,1408]{1,0:T(8,128)(2,1)S(1)}, bf16[32,1408]{1,0:T(8,128)(2,1)S(1)}, u32[]{:S(2)}, u32[]{:S(2)}) collective-permute-start(bf16[32,1408]{1,0:T(8,128)(2,1)S(1)} %get-tuple-element.20), channel_id=1, source_target_pairs={{0,8},{4,12},{8,0},{12,4},{1,9},{5,13},{9,1},{13,5},{2,10},{6,14},... | collective-permute-start | bytes 270344 | tf_op jit(solution)/shard_map/ppermute | solution.py:23
  6.7 7.2 %collective-permute-start.2 = (bf16[32,1408]{1,0:T(8,128)(2,1)S(1)}, bf16[32,1408]{1,0:T(8,128)(2,1)S(1)}, u32[]{:S(2)}, u32[]{:S(2)}) collective-permute-start(bf16[32,1408]{1,0:T(8,128)(2,1)S(1)} %get-tuple-element.20), channel_id=1, source_target_pairs={{0,12},{4,8},{8,4},{12,0},{1,13},{5,9},{9,5},{13,1},{2,14},{6,10},... | collective-permute-start | bytes 270344 | tf_op jit(solution)/shard_map/ppermute | solution.py:23
  6.7 9.0 %collective-permute-start.4 = (bf16[32,1408]{1,0:T(8,128)(2,1)S(1)}, bf16[32,1408]{1,0:T(8,128)(2,1)S(1)}, u32[]{:S(2)}, u32[]{:S(2)}) collective-permute-start(bf16[32,1408]{1,0:T(8,128)(2,1)S(1)} %get-tuple-element.20), channel_id=1, source_target_pairs={{0,2},{1,3},{2,0},{3,1},{4,6},{5,7},{6,4},{7,5},{8,10},{9,11},{10,... | collective-permute-start | bytes 270344 | tf_op jit(solution)/shard_map/ppermute | solution.py:23
  13.9 6.5 %collective-permute-start.5 = (bf16[96,1408]{1,0:T(8,128)(2,1)S(1)}, bf16[96,1408]{1,0:T(8,128)(2,1)S(1)}, u32[]{:S(2)}, u32[]{:S(2)}) collective-permute-start(bf16[96,1408]{1,0:T(8,128)(2,1)S(1)} %pad_maximum_fusion), channel_id=1, source_target_pairs={{0,2},{1,3},{2,0},{3,1},{4,6},{5,7},{6,4},{7,5},{8,10},{9,11},{10,... | collective-permute-start | bytes 811016 | tf_op jit(solution)/shard_map/ppermute | solution.py:23
  15.6 5.1 %collective-permute-start.3 = (bf16[128,1408]{1,0:T(8,128)(2,1)S(1)}, bf16[128,1408]{1,0:T(8,128)(2,1)S(1)}, u32[]{:S(2)}, u32[]{:S(2)}) collective-permute-start(bf16[128,1408]{1,0:T(8,128)(2,1)S(1)} %constant_dynamic-update-slice_fusion.chunk_ref.refs_0_), channel_id=1, source_target_pairs={{0,1},{1,0},{2,3},{3,2},{4,5},{5,4},{6,7},{7,6},{8,9},{9,8},{10,11... | collective-permute-start | bytes 1081352 | tf_op jit(solution)/shard_map/ppermute | solution.py:23
  15.7 8.5 %slice-start = ((s8[10485760]{0:T(1024)(128)(4,1)}), s8[4194304]{0:T(1024)(128)(4,1)S(1)}, s32[]{:S(2)}) async-start(s8[10485760]{0:T(1024)(128)(4,1)} %bitcast.51), calls=%async_computation | async-start | bytes 8388608
  15.7 8.5 %slice-start.1 = ((s8[10485760]{0:T(1024)(128)(4,1)}), s8[4194304]{0:T(1024)(128)(4,1)S(1)}, s32[]{:S(2)}) async-start(s8[10485760]{0:T(1024)(128)(4,1)} %bitcast.51), calls=%async_computation.1 | async-start | bytes 8388608
  20.5 3.6 %collective-permute-start.6 = (bf16[128,1408]{1,0:T(8,128)(2,1)S(1)}, bf16[128,1408]{1,0:T(8,128)(2,1)S(1)}, u32[]{:S(2)}, u32[]{:S(2)}) collective-permute-start(bf16[128,1408]{1,0:T(8,128)(2,1)S(1)} %join.1.refs_2_), channel_id=1, source_target_pairs={{0,1},{1,0},{2,3},{3,2},{4,5},{5,4},{6,7},{7,6},{8,9},{9,8},{10,11... | collective-permute-start | bytes 1081352 | tf_op jit(solution)/shard_map/ppermute | solution.py:23
  20.6 3.7 %slice-start.2 = ((s8[10485760]{0:T(1024)(128)(4,1)}), s8[2097152]{0:T(1024)(128)(4,1)S(1)}, s32[]{:S(2)}) async-start(s8[10485760]{0:T(1024)(128)(4,1)} %bitcast.51), calls=%async_computation.2 | async-start | bytes 4194304
  20.6 4.4 %copy-start = (bf16[256,5120]{1,0:T(8,128)(2,1)S(1)}, bf16[256,5120]{1,0:T(8,128)(2,1)}, u32[]{:S(2)}) copy-start(bf16[256,5120]{1,0:T(8,128)(2,1)} %s_down.1) | copy-start | bytes 7864324
  33.6 1.8 %collective-permute-start.8 = (bf16[2,2,8,5120]{3,2,1,0:T(8,128)(2,1)S(1)}, bf16[2,2,8,5120]{3,2,1,0:T(8,128)(2,1)S(1)}, u32[]{:S(2)}, u32[]{:S(2)}) collective-permute-start(bf16[2,2,8,5120]{3,2,1,0:T(8,128)(2,1)S(1)} %get-tuple-element.31), channel_id=1, source_target_pairs={{0,1},{1,0},{2,3},{3,2},{4,5},{5,4},{6,7},{7,6},{8,9},{9,8},{10,11... | collective-permute-start | bytes 983048 | tf_op jit(solution)/shard_map/ppermute | solution.py:23
  34.1 2.8 %collective-permute-start.7 = (bf16[2,2,8,5120]{3,2,1,0:T(8,128)(2,1)S(1)}, bf16[2,2,8,5120]{3,2,1,0:T(8,128)(2,1)S(1)}, u32[]{:S(2)}, u32[]{:S(2)}) collective-permute-start(bf16[2,2,8,5120]{3,2,1,0:T(8,128)(2,1)S(1)} %get-tuple-element.29), channel_id=1, source_target_pairs={{0,1},{1,0},{2,3},{3,2},{4,5},{5,4},{6,7},{7,6},{8,9},{9,8},{10,11... | collective-permute-start | bytes 983048 | tf_op jit(solution)/shard_map/ppermute | solution.py:23
  35.5 6.5 %collective-permute-start.9 = (bf16[2,8,5120]{2,1,0:T(8,128)(2,1)S(1)}, bf16[2,8,5120]{2,1,0:T(8,128)(2,1)S(1)}, u32[]{:S(2)}, u32[]{:S(2)}) collective-permute-start(bf16[2,8,5120]{2,1,0:T(8,128)(2,1)S(1)} %fusion.1), channel_id=1, source_target_pairs={{0,2},{1,3},{2,0},{3,1},{4,6},{5,7},{6,4},{7,5},{8,10},{9,11},{10,... | collective-permute-start | bytes 491528 | tf_op jit(solution)/shard_map/ppermute | solution.py:23
  42.1 6.2 %collective-permute-start.10 = (bf16[2,8,5120]{2,1,0:T(8,128)(2,1)S(1)}, bf16[2,8,5120]{2,1,0:T(8,128)(2,1)S(1)}, u32[]{:S(2)}, u32[]{:S(2)}) collective-permute-start(bf16[2,8,5120]{2,1,0:T(8,128)(2,1)S(1)} %get-tuple-element.32), channel_id=1, source_target_pairs={{0,2},{1,3},{2,0},{3,1},{4,6},{5,7},{6,4},{7,5},{8,10},{9,11},{10,... | collective-permute-start | bytes 491528 | tf_op jit(solution)/shard_map/ppermute | solution.py:23
  43.6 8.6 %collective-permute-start.12 = (bf16[8,5120]{1,0:T(8,128)(2,1)S(1)}, bf16[8,5120]{1,0:T(8,128)(2,1)S(1)}, u32[]{:S(2)}, u32[]{:S(2)}) collective-permute-start(bf16[8,5120]{1,0:T(8,128)(2,1)S(1)} %get-tuple-element.33), channel_id=1, source_target_pairs={{0,8},{4,12},{8,0},{12,4},{1,9},{5,13},{9,1},{13,5},{2,10},{6,14},... | collective-permute-start | bytes 245768 | tf_op jit(solution)/shard_map/ppermute | solution.py:23
  46.8 6.7 %collective-permute-start.13 = (bf16[8,5120]{1,0:T(8,128)(2,1)S(1)}, bf16[8,5120]{1,0:T(8,128)(2,1)S(1)}, u32[]{:S(2)}, u32[]{:S(2)}) collective-permute-start(bf16[8,5120]{1,0:T(8,128)(2,1)S(1)} %get-tuple-element.34), channel_id=1, source_target_pairs={{0,12},{4,8},{8,4},{12,0},{1,13},{5,9},{9,5},{13,1},{2,14},{6,10},... | collective-permute-start | bytes 245768 | tf_op jit(solution)/shard_map/ppermute | solution.py:23
  48.3 5.6 %collective-permute-start.11 = (bf16[8,5120]{1,0:T(8,128)(2,1)S(1)}, bf16[8,5120]{1,0:T(8,128)(2,1)S(1)}, u32[]{:S(2)}, u32[]{:S(2)}) collective-permute-start(bf16[8,5120]{1,0:T(8,128)(2,1)S(1)} %fusion.7), channel_id=1, source_target_pairs={{0,4},{4,0},{8,12},{12,8},{1,5},{5,1},{9,13},{13,9},{2,6},{6,2},{1... | collective-permute-start | bytes 245768 | tf_op jit(solution)/shard_map/ppermute | solution.py:23

commit v4 on v3

--- a/solution.py
+++ b/solution.py
@@ -151,16 +151,13 @@
         start += ref.shape[0]
 
 
-def relay_kernel(far_ref, near_ref, *refs):
-    pairs, nodes = far_ref.shape[:2]
-    came, sums, near = refs[: pairs - 1], refs[pairs - 1 : pairs - 1 + nodes], refs[pairs - 1 + nodes :]
-    for index, sum_ref in enumerate(sums):
+def relay_kernel(far_ref, *refs):
+    pairs = far_ref.shape[0]
+    for index, sum_ref in enumerate(refs[pairs - 1 :]):
         total = far_ref[0, index]
-        for ref in came:
+        for ref in refs[: pairs - 1]:
             total = total + ref[index].astype(jnp.float32)
         sum_ref[...] = total.astype(jnp.bfloat16)
-    for pair, ref in enumerate(near):
-        ref[...] = near_ref[pair + 1].astype(jnp.bfloat16)
 
 
 def act(gate, up):
@@ -448,18 +445,17 @@
         far = keep_far + swap(send_far, "local", 1).astype(f32)
         came = [swap(far[k].astype(bf16), "local", k * CORES) for k in range(1, pairs)]
         near = keep_near + swap(send_near, "local", 1).astype(f32)
-        rows_shape = jax.ShapeDtypeStruct((tokens, step), bf16)
-        near_shape = jax.ShapeDtypeStruct((half, tokens, step), bf16)
-        out = call(
+        near_came = [
+            swap(near[k].astype(bf16), "local", k * CORES).astype(f32) for k in range(1, pairs)
+        ]
+        far_rows = call(
             relay_kernel,
             "relay",
-            [rows_shape] * (node_count - half) + [near_shape] * (pairs - 1),
-            [VMEM] * (pairs + 1),
+            [jax.ShapeDtypeStruct((tokens, step), bf16)] * (node_count - half),
+            [VMEM] * pairs,
             [],
-            (far, near, *came),
-        )
-        far_rows, near_rows = out[: node_count - half], out[node_count - half :]
-        near_came = [swap(x, "local", k * CORES).astype(f32) for k, x in enumerate(near_rows, 1)]
+            (far, *came),
+        )
         far_came = [swap(x, "node", half + k).astype(f32) for k, x in enumerate(far_rows)]
         result = sum(near_came, near[0])
         total_here = result[0]

time: 54.7 us -> 53.5 us (0.978)
  starting transfers between devices: 19 us -> 17 us
  waiting for transfers between devices: 16.7 us -> 17.5 us
    ppermute x14, starting transfers between devices: 19 us -> 17 us  [swap(): return lax.ppermute(x, axis, [(i, i ^ offset) for i in range(size)])]
    ppermute x14, waiting for transfers between devices: 16.7 us -> 17.5 us  [swap(): return lax.ppermute(x, axis, [(i, i ^ offset) for i in range(size)])]
where the time goes in v4:
time: 53.5 us; the launch traced here: 53.3 us
  waiting for transfers between devices  17.5 us (33%)
  starting transfers between devices  17 us (32%)
  Pallas kernels  16.5 us (31%)
  local copies, waits for them, and re-layouts  1.05 us (2%)
  other arithmetic  1.02 us (2%)
    ppermute x14, waiting for transfers between devices, swap(): return lax.ppermute(x, axis, [(i, i ^ offset) for i in range(size)])  17.5 us
    ppermute x14, starting transfers between devices, swap(): return lax.ppermute(x, axis, [(i, i ^ offset) for i in range(size)])  17 us
    pallas_call x6, Pallas kernels, call(): pl.pallas_call(kernel, out_shape=out_shape, in_specs=in_specs, out_specs=...  16.5 us
  transfers between devices with their start and end apart: 14, of which 7 were waited for; matrix products, arithmetic and copies ran while one was open for 1% of the time, Pallas kernels for 13%

profile of v4, /device:TPU:0, one launch (start us, length us, event | category | flops | bytes accessed | tf_op | source)
XLA Modules:
  0.0 53.3 jit_solution(17233560490748900587)
XLA Ops:
  0.0 1.0 %pack.1 = (bf16[32,1408]{1,0:T(8,128)(2,1)S(1)}, f32[4,1,1280]{2,1,0:T(1,128)S(1)}) custom-call(s32[1]{0:T(128)} %bitcast.place_ref.part_ref, bf16[32,1280]{1,0:T(8,128)(2,1)} %refs_0_.3, s32[2,8]{1,0:T(2,128)} %bitcast.60, bf16[4,8]{1,0:T(4,128)(2,1)} %bitcast.61, f32[4,1,1280]{2,1,0:T(1,128)} %bitcast.59), custom_call_target="tpu_custom_call" | custom-call | flops 40000000000 | tf_op jit(solution)/shard_map/pack/pallas_call | solution.py:295
  1.0 3.1 %collective-permute-start = (bf16[32,1408]{1,0:T(8,128)(2,1)S(1)}, bf16[32,1408]{1,0:T(8,128)(2,1)S(1)}, u32[]{:S(2)}, u32[]{:S(2)}) collective-permute-start(bf16[32,1408]{1,0:T(8,128)(2,1)S(1)} %get-tuple-element.19), channel_id=1, source_target_pairs={{0,4},{4,0},{8,12},{12,8},{1,5},{5,1},{9,13},{13,9},{2,6},{6,2},{1... | collective-permute-start | bytes 270344 | tf_op jit(solution)/shard_map/ppermute | solution.py:23
  4.1 2.6 %collective-permute-start.1 = (bf16[32,1408]{1,0:T(8,128)(2,1)S(1)}, bf16[32,1408]{1,0:T(8,128)(2,1)S(1)}, u32[]{:S(2)}, u32[]{:S(2)}) collective-permute-start(bf16[32,1408]{1,0:T(8,128)(2,1)S(1)} %get-tuple-element.19), channel_id=1, source_target_pairs={{0,8},{4,12},{8,0},{12,4},{1,9},{5,13},{9,1},{13,5},{2,10},{6,14},... | collective-permute-start | bytes 270344 | tf_op jit(solution)/shard_map/ppermute | solution.py:23
  6.7 1.7 %collective-permute-start.4 = (bf16[32,1408]{1,0:T(8,128)(2,1)S(1)}, bf16[32,1408]{1,0:T(8,128)(2,1)S(1)}, u32[]{:S(2)}, u32[]{:S(2)}) collective-permute-start(bf16[32,1408]{1,0:T(8,128)(2,1)S(1)} %get-tuple-element.19), channel_id=1, source_target_pairs={{0,2},{1,3},{2,0},{3,1},{4,6},{5,7},{6,4},{7,5},{8,10},{9,11},{10,... | collective-permute-start | bytes 270344 | tf_op jit(solution)/shard_map/ppermute | solution.py:23
  8.4 0.1 pad_add_fusion.place_ref
  8.5 5.4 %collective-permute-done.1 = bf16[32,1408]{1,0:T(8,128)(2,1)S(1)} collective-permute-done((bf16[32,1408]{1,0:T(8,128)(2,1)S(1)}, bf16[32,1408]{1,0:T(8,128)(2,1)S(1)}, u32[]{:S(2)}, u32[]{:S(2)}) %collective-permute-start.1) | collective-permute-done | bytes 90144 | tf_op jit(solution)/shard_map/ppermute | solution.py:23
  13.9 1.6 %collective-permute-start.5 = (bf16[96,1408]{1,0:T(8,128)(2,1)S(1)}, bf16[96,1408]{1,0:T(8,128)(2,1)S(1)}, u32[]{:S(2)}, u32[]{:S(2)}) collective-permute-start(bf16[96,1408]{1,0:T(8,128)(2,1)S(1)} %pad_maximum_fusion), channel_id=1, source_target_pairs={{0,2},{1,3},{2,0},{3,1},{4,6},{5,7},{6,4},{7,5},{8,10},{9,11},{10,... | collective-permute-start | bytes 811016 | tf_op jit(solution)/shard_map/ppermute | solution.py:23
  15.6 0.1 collective-permute-start.3
  15.7 0.0 slice-start
  15.7 3.4 %project.2 = (f32[128,2048]{1,0:T(8,128)S(1)}, f32[32,512]{1,0:T(8,128)S(1)}, f32[128,128]{1,0:T(8,128)S(1)}) custom-call(s32[1]{0:T(128)} %bitcast.place_ref.part_ref, bf16[128,1408]{1,0:T(8,128)(2,1)S(1)} %constant_dynamic-update-slice_fusion.chunk_ref.refs_0_, f32[4,1,1280]{2,1,0:T(1,128)S(1)} %get-tuple-element.20.gain_ref, bf16[2,5120,512]{2,1,0:T(8,128)(2,1)} %gate.1, ...), custom_call_target="tpu_custom_call" | custom-call | flops 713031680 | bytes 6553600 | tf_op jit(solution)/shard_map/project/pallas_call | solution.py:295
  19.1 1.3 %collective-permute-done.5.refs_1_ = bf16[96,1408]{1,0:T(8,128)(2,1)S(1)} collective-permute-done((bf16[96,1408]{1,0:T(8,128)(2,1)S(1)}, bf16[96,1408]{1,0:T(8,128)(2,1)S(1)}, u32[]{:S(2)}, u32[]{:S(2)}) %collective-permute-start.5) | collective-permute-done | bytes 270368 | tf_op jit(solution)/shard_map/ppermute | solution.py:23
  20.5 0.1 collective-permute-start.6
  20.6 0.0 slice-start.2
  20.6 3.4 %project.3 = (f32[128,2048]{1,0:T(8,128)S(1)}, f32[32,512]{1,0:T(8,128)S(1)}, f32[128,128]{1,0:T(8,128)S(1)}) custom-call(s32[1]{0:T(128)} %bitcast.17.part_ref, bf16[128,1408]{1,0:T(8,128)(2,1)S(1)} %collective-permute-done.3.chunk_ref.refs_1_, ...), custom_call_target="tpu_custom_call", output_to_operand_aliasing={{0}: (7, {}), {1}: (8, {}), {2}: (9, {})} | custom-call | flops 713031680 | bytes 6553600 | tf_op jit(solution)/shard_map/project/pallas_call | solution.py:295
  24.1 0.1 slice-done.2
  24.3 0.8 %copy-done = bf16[256,5120]{1,0:T(8,128)(2,1)S(1)} copy-done((bf16[256,5120]{1,0:T(8,128)(2,1)S(1)}, bf16[256,5120]{1,0:T(8,128)(2,1)}, u32[]{:S(2)}) %copy-start) | copy-done | bytes 2621464
  25.0 8.6 %finish.1 = (bf16[128,1024]{1,0:T(8,128)(2,1)}, bf16[32,256]{1,0:T(8,128)(2,1)}, f32[2,2,8,5120]{3,2,1,0:T(8,128)S(1)}, f32[2,2,8,5120]{3,2,1,0:T(8,128)S(1)}, b...) custom-call(s32[2]{0:T(128)S(1)} %pad_add_fusion.place_ref, ...), custom_call_target="tpu_custom_call" | custom-call | flops 2139095040 | bytes 19660800 | tf_op jit(solution)/shard_map/finish/pallas_call | solution.py:295
  33.6 0.5 %collective-permute-start.10 = (bf16[2,2,8,5120]{3,2,1,0:T(8,128)(2,1)S(1)}, bf16[2,2,8,5120]{3,2,1,0:T(8,128)(2,1)S(1)}, u32[]{:S(2)}, u32[]{:S(2)}) collective-permute-start(bf16[2,2,8,5120]{3,2,1,0:T(8,128)(2,1)S(1)} %get-tuple-element.30), channel_id=1, source_target_pairs={{0,1},{1,0},{2,3},{3,2},{4,5},{5,4},{6,7},{7,6},{8,9},{9,8},{10,11... | collective-permute-start | bytes 983048 | tf_op jit(solution)/shard_map/ppermute | solution.py:23
  34.1 0.1 collective-permute-start.7
  34.2 1.2 %collective-permute-done.10 = bf16[2,2,8,5120]{3,2,1,0:T(8,128)(2,1)S(1)} collective-permute-done((bf16[2,2,8,5120]{3,2,1,0:T(8,128)(2,1)S(1)}, bf16[2,2,8,5120]{3,2,1,0:T(8,128)(2,1)S(1)}, u32[]{:S(2)}, u32[]{:S(2)}) %collective-permute-start.10) | collective-permute-done | bytes 327712 | tf_op jit(solution)/shard_map/ppermute | solution.py:23
  35.4 0.1 convert_add_fusion.far_ref
  35.5 1.5 %collective-permute-start.11 = (bf16[2,8,5120]{2,1,0:T(8,128)(2,1)S(1)}, bf16[2,8,5120]{2,1,0:T(8,128)(2,1)S(1)}, u32[]{:S(2)}, u32[]{:S(2)}) collective-permute-start(bf16[2,8,5120]{2,1,0:T(8,128)(2,1)S(1)} %fusion.2), channel_id=1, source_target_pairs={{0,2},{1,3},{2,0},{3,1},{4,6},{5,7},{6,4},{7,5},{8,10},{9,11},{10,... | collective-permute-start | bytes 491528 | tf_op jit(solution)/shard_map/ppermute | solution.py:23
  37.0 0.1 convert_add_fusion.1
  37.1 0.7 %collective-permute-start.8 = (bf16[2,8,5120]{2,1,0:T(8,128)(2,1)S(1)}, bf16[2,8,5120]{2,1,0:T(8,128)(2,1)S(1)}, u32[]{:S(2)}, u32[]{:S(2)}) collective-permute-start(bf16[2,8,5120]{2,1,0:T(8,128)(2,1)S(1)} %fusion.1), channel_id=1, source_target_pairs={{0,2},{1,3},{2,0},{3,1},{4,6},{5,7},{6,4},{7,5},{8,10},{9,11},{10,... | collective-permute-start | bytes 491528 | tf_op jit(solution)/shard_map/ppermute | solution.py:23
  37.8 4.8 %collective-permute-done.11.refs_0_ = bf16[2,8,5120]{2,1,0:T(8,128)(2,1)S(1)} collective-permute-done((bf16[2,8,5120]{2,1,0:T(8,128)(2,1)S(1)}, bf16[2,8,5120]{2,1,0:T(8,128)(2,1)S(1)}, u32[]{:S(2)}, u32[]{:S(2)}) %collective-permute-start.11) | collective-permute-done | bytes 163872 | tf_op jit(solution)/shard_map/ppermute | solution.py:23
  42.6 3.1 %collective-permute-start.12 = (bf16[8,5120]{1,0:T(8,128)(2,1)S(1)}, bf16[8,5120]{1,0:T(8,128)(2,1)S(1)}, u32[]{:S(2)}, u32[]{:S(2)}) collective-permute-start(bf16[8,5120]{1,0:T(8,128)(2,1)S(1)} %get-tuple-element.31), channel_id=1, source_target_pairs={{0,8},{4,12},{8,0},{12,4},{1,9},{5,13},{9,1},{13,5},{2,10},{6,14},... | collective-permute-start | bytes 245768 | tf_op jit(solution)/shard_map/ppermute | solution.py:23
  45.7 1.4 %collective-permute-start.13 = (bf16[8,5120]{1,0:T(8,128)(2,1)S(1)}, bf16[8,5120]{1,0:T(8,128)(2,1)S(1)}, u32[]{:S(2)}, u32[]{:S(2)}) collective-permute-start(bf16[8,5120]{1,0:T(8,128)(2,1)S(1)} %get-tuple-element.32), channel_id=1, source_target_pairs={{0,12},{4,8},{8,4},{12,0},{1,13},{5,9},{9,5},{13,1},{2,14},{6,10},... | collective-permute-start | bytes 245768 | tf_op jit(solution)/shard_map/ppermute | solution.py:23
  47.2 0.6 %collective-permute-start.9 = (bf16[8,5120]{1,0:T(8,128)(2,1)S(1)}, bf16[8,5120]{1,0:T(8,128)(2,1)S(1)}, u32[]{:S(2)}, u32[]{:S(2)}) collective-permute-start(bf16[8,5120]{1,0:T(8,128)(2,1)S(1)} %fusion.8), channel_id=1, source_target_pairs={{0,4},{4,0},{8,12},{12,8},{1,5},{5,1},{9,13},{13,9},{2,6},{6,2},{1... | collective-permute-start | bytes 245768 | tf_op jit(solution)/shard_map/ppermute | solution.py:23
  47.8 3.1 %collective-permute-done.12 = bf16[8,5120]{1,0:T(8,128)(2,1)S(1)} collective-permute-done((bf16[8,5120]{1,0:T(8,128)(2,1)S(1)}, bf16[8,5120]{1,0:T(8,128)(2,1)S(1)}, u32[]{:S(2)}, u32[]{:S(2)}) %collective-permute-start.12) | collective-permute-done | bytes 81952 | tf_op jit(solution)/shard_map/ppermute | solution.py:23
  50.9 1.6 %collective-permute-done.13 = bf16[8,5120]{1,0:T(8,128)(2,1)S(1)} collective-permute-done((bf16[8,5120]{1,0:T(8,128)(2,1)S(1)}, bf16[8,5120]{1,0:T(8,128)(2,1)S(1)}, u32[]{:S(2)}, u32[]{:S(2)}) %collective-permute-start.13) | collective-permute-done | bytes 81952 | tf_op jit(solution)/shard_map/ppermute | solution.py:23
  52.4 0.2 collective-permute-done.9
  52.6 0.7 %fusion.7 = bf16[8,5120]{1,0:T(8,128)(2,1)} fusion(f32[8,5120]{1,0:T(8,128)S(1)} %bitcast.58, f32[2,8,5120]{2,1,0:T(8,128)S(1)} %fusion, bf16[8,5120]{1,0:T(8,128)(2,1)S(1)} %collective-permute-done.13, bf16[8,5120]{1,0:T(8,128)(2,1)S(1)} %collective-permute-done.12, bf16[8,5120]{1,0:T(8,128)(2,1)S(1)} %collective-permute-done.9), kind=kLoop, calls=%fused_computation.15 | loop fusion | flops 327680 | bytes 655360 | tf_op jit(solution)/shard_map/convert_element_type | solution.py:477
  (33 shorter events, 0.4 us)
Async XLA Ops:
  1.0 7.5 %collective-permute-start = (bf16[32,1408]{1,0:T(8,128)(2,1)S(1)}, bf16[32,1408]{1,0:T(8,128)(2,1)S(1)}, u32[]{:S(2)}, u32[]{:S(2)}) collective-permute-start(bf16[32,1408]{1,0:T(8,128)(2,1)S(1)} %get-tuple-element.19), channel_id=1, source_target_pairs={{0,4},{4,0},{8,12},{12,8},{1,5},{5,1},{9,13},{13,9},{2,6},{6,2},{1... | collective-permute-start | bytes 270344 | tf_op jit(solution)/shard_map/ppermute | solution.py:23
  4.1 9.8 %collective-permute-start.1 = (bf16[32,1408]{1,0:T(8,128)(2,1)S(1)}, bf16[32,1408]{1,0:T(8,128)(2,1)S(1)}, u32[]{:S(2)}, u32[]{:S(2)}) collective-permute-start(bf16[32,1408]{1,0:T(8,128)(2,1)S(1)} %get-tuple-element.19), channel_id=1, source_target_pairs={{0,8},{4,12},{8,0},{12,4},{1,9},{5,13},{9,1},{13,5},{2,10},{6,14},... | collective-permute-start | bytes 270344 | tf_op jit(solution)/shard_map/ppermute | solution.py:23
  6.7 7.2 %collective-permute-start.2 = (bf16[32,1408]{1,0:T(8,128)(2,1)S(1)}, bf16[32,1408]{1,0:T(8,128)(2,1)S(1)}, u32[]{:S(2)}, u32[]{:S(2)}) collective-permute-start(bf16[32,1408]{1,0:T(8,128)(2,1)S(1)} %get-tuple-element.19), channel_id=1, source_target_pairs={{0,12},{4,8},{8,4},{12,0},{1,13},{5,9},{9,5},{13,1},{2,14},{6,10},... | collective-permute-start | bytes 270344 | tf_op jit(solution)/shard_map/ppermute | solution.py:23
  6.7 9.0 %collective-permute-start.4 = (bf16[32,1408]{1,0:T(8,128)(2,1)S(1)}, bf16[32,1408]{1,0:T(8,128)(2,1)S(1)}, u32[]{:S(2)}, u32[]{:S(2)}) collective-permute-start(bf16[32,1408]{1,0:T(8,128)(2,1)S(1)} %get-tuple-element.19), channel_id=1, source_target_pairs={{0,2},{1,3},{2,0},{3,1},{4,6},{5,7},{6,4},{7,5},{8,10},{9,11},{10,... | collective-permute-start | bytes 270344 | tf_op jit(solution)/shard_map/ppermute | solution.py:23
  13.9 6.5 %collective-permute-start.5 = (bf16[96,1408]{1,0:T(8,128)(2,1)S(1)}, bf16[96,1408]{1,0:T(8,128)(2,1)S(1)}, u32[]{:S(2)}, u32[]{:S(2)}) collective-permute-start(bf16[96,1408]{1,0:T(8,128)(2,1)S(1)} %pad_maximum_fusion), channel_id=1, source_target_pairs={{0,2},{1,3},{2,0},{3,1},{4,6},{5,7},{6,4},{7,5},{8,10},{9,11},{10,... | collective-permute-start | bytes 811016 | tf_op jit(solution)/shard_map/ppermute | solution.py:23
  15.6 5.1 %collective-permute-start.3 = (bf16[128,1408]{1,0:T(8,128)(2,1)S(1)}, bf16[128,1408]{1,0:T(8,128)(2,1)S(1)}, u32[]{:S(2)}, u32[]{:S(2)}) collective-permute-start(bf16[128,1408]{1,0:T(8,128)(2,1)S(1)} %constant_dynamic-update-slice_fusion.chunk_ref.refs_0_), channel_id=1, source_target_pairs={{0,1},{1,0},{2,3},{3,2},{4,5},{5,4},{6,7},{7,6},{8,9},{9,8},{10,11... | collective-permute-start | bytes 1081352 | tf_op jit(solution)/shard_map/ppermute | solution.py:23
  15.7 8.5 %slice-start = ((s8[10485760]{0:T(1024)(128)(4,1)}), s8[4194304]{0:T(1024)(128)(4,1)S(1)}, s32[]{:S(2)}) async-start(s8[10485760]{0:T(1024)(128)(4,1)} %bitcast.53), calls=%async_computation | async-start | bytes 8388608
  15.7 8.5 %slice-start.1 = ((s8[10485760]{0:T(1024)(128)(4,1)}), s8[4194304]{0:T(1024)(128)(4,1)S(1)}, s32[]{:S(2)}) async-start(s8[10485760]{0:T(1024)(128)(4,1)} %bitcast.53), calls=%async_computation.1 | async-start | bytes 8388608
  20.5 3.6 %collective-permute-start.6 = (bf16[128,1408]{1,0:T(8,128)(2,1)S(1)}, bf16[128,1408]{1,0:T(8,128)(2,1)S(1)}, u32[]{:S(2)}, u32[]{:S(2)}) collective-permute-start(bf16[128,1408]{1,0:T(8,128)(2,1)S(1)} %join.1.refs_2_), channel_id=1, source_target_pairs={{0,1},{1,0},{2,3},{3,2},{4,5},{5,4},{6,7},{7,6},{8,9},{9,8},{10,11... | collective-permute-start | bytes 1081352 | tf_op jit(solution)/shard_map/ppermute | solution.py:23
  20.6 3.7 %slice-start.2 = ((s8[10485760]{0:T(1024)(128)(4,1)}), s8[2097152]{0:T(1024)(128)(4,1)S(1)}, s32[]{:S(2)}) async-start(s8[10485760]{0:T(1024)(128)(4,1)} %bitcast.53), calls=%async_computation.2 | async-start | bytes 4194304
  20.6 4.4 %copy-start = (bf16[256,5120]{1,0:T(8,128)(2,1)S(1)}, bf16[256,5120]{1,0:T(8,128)(2,1)}, u32[]{:S(2)}) copy-start(bf16[256,5120]{1,0:T(8,128)(2,1)} %s_down.1) | copy-start | bytes 7864324
  33.6 1.8 %collective-permute-start.10 = (bf16[2,2,8,5120]{3,2,1,0:T(8,128)(2,1)S(1)}, bf16[2,2,8,5120]{3,2,1,0:T(8,128)(2,1)S(1)}, u32[]{:S(2)}, u32[]{:S(2)}) collective-permute-start(bf16[2,2,8,5120]{3,2,1,0:T(8,128)(2,1)S(1)} %get-tuple-element.30), channel_id=1, source_target_pairs={{0,1},{1,0},{2,3},{3,2},{4,5},{5,4},{6,7},{7,6},{8,9},{9,8},{10,11... | collective-permute-start | bytes 983048 | tf_op jit(solution)/shard_map/ppermute | solution.py:23
  34.1 2.8 %collective-permute-start.7 = (bf16[2,2,8,5120]{3,2,1,0:T(8,128)(2,1)S(1)}, bf16[2,2,8,5120]{3,2,1,0:T(8,128)(2,1)S(1)}, u32[]{:S(2)}, u32[]{:S(2)}) collective-permute-start(bf16[2,2,8,5120]{3,2,1,0:T(8,128)(2,1)S(1)} %get-tuple-element.28), channel_id=1, source_target_pairs={{0,1},{1,0},{2,3},{3,2},{4,5},{5,4},{6,7},{7,6},{8,9},{9,8},{10,11... | collective-permute-start | bytes 983048 | tf_op jit(solution)/shard_map/ppermute | solution.py:23
  35.5 7.1 %collective-permute-start.11 = (bf16[2,8,5120]{2,1,0:T(8,128)(2,1)S(1)}, bf16[2,8,5120]{2,1,0:T(8,128)(2,1)S(1)}, u32[]{:S(2)}, u32[]{:S(2)}) collective-permute-start(bf16[2,8,5120]{2,1,0:T(8,128)(2,1)S(1)} %fusion.2), channel_id=1, source_target_pairs={{0,2},{1,3},{2,0},{3,1},{4,6},{5,7},{6,4},{7,5},{8,10},{9,11},{10,... | collective-permute-start | bytes 491528 | tf_op jit(solution)/shard_map/ppermute | solution.py:23
  37.1 10.1 %collective-permute-start.8 = (bf16[2,8,5120]{2,1,0:T(8,128)(2,1)S(1)}, bf16[2,8,5120]{2,1,0:T(8,128)(2,1)S(1)}, u32[]{:S(2)}, u32[]{:S(2)}) collective-permute-start(bf16[2,8,5120]{2,1,0:T(8,128)(2,1)S(1)} %fusion.1), channel_id=1, source_target_pairs={{0,2},{1,3},{2,0},{3,1},{4,6},{5,7},{6,4},{7,5},{8,10},{9,11},{10,... | collective-permute-start | bytes 491528 | tf_op jit(solution)/shard_map/ppermute | solution.py:23
  42.6 8.2 %collective-permute-start.12 = (bf16[8,5120]{1,0:T(8,128)(2,1)S(1)}, bf16[8,5120]{1,0:T(8,128)(2,1)S(1)}, u32[]{:S(2)}, u32[]{:S(2)}) collective-permute-start(bf16[8,5120]{1,0:T(8,128)(2,1)S(1)} %get-tuple-element.31), channel_id=1, source_target_pairs={{0,8},{4,12},{8,0},{12,4},{1,9},{5,13},{9,1},{13,5},{2,10},{6,14},... | collective-permute-start | bytes 245768 | tf_op jit(solution)/shard_map/ppermute | solution.py:23
  45.7 6.7 %collective-permute-start.13 = (bf16[8,5120]{1,0:T(8,128)(2,1)S(1)}, bf16[8,5120]{1,0:T(8,128)(2,1)S(1)}, u32[]{:S(2)}, u32[]{:S(2)}) collective-permute-start(bf16[8,5120]{1,0:T(8,128)(2,1)S(1)} %get-tuple-element.32), channel_id=1, source_target_pairs={{0,12},{4,8},{8,4},{12,0},{1,13},{5,9},{9,5},{13,1},{2,14},{6,10},... | collective-permute-start | bytes 245768 | tf_op jit(solution)/shard_map/ppermute | solution.py:23
  47.2 5.4 %collective-permute-start.9 = (bf16[8,5120]{1,0:T(8,128)(2,1)S(1)}, bf16[8,5120]{1,0:T(8,128)(2,1)S(1)}, u32[]{:S(2)}, u32[]{:S(2)}) collective-permute-start(bf16[8,5120]{1,0:T(8,128)(2,1)S(1)} %fusion.8), channel_id=1, source_target_pairs={{0,4},{4,0},{8,12},{12,8},{1,5},{5,1},{9,13},{13,9},{2,6},{6,2},{1... | collective-permute-start | bytes 245768 | tf_op jit(solution)/shard_map/ppermute | solution.py:23

commit v5 on v4

--- a/solution.py
+++ b/solution.py
@@ -10,7 +10,7 @@
 ROWS = 128
 LANES = 128
 CORES = 2
-WINDOW = 40
+WINDOW = 9
 LATE = 2
 VMEM = pl.BlockSpec(memory_space=pltpu.VMEM)
 SMEM = pl.BlockSpec(memory_space=pltpu.SMEM)
@@ -179,10 +179,19 @@
     return [slice(start, start + block) for start in range(0, total, block)]
 
 
-def down_expert(hidden_ref, shared_hidden_ref, expert, first, down, s_down, out_ref):
+def down_shared(shared_hidden_ref, first, s_down, out_ref):
+    count, _, step = out_ref.shape
+    own = shared_hidden_ref.shape[0]
+    for index in range(count):
+        taken = slice(first + index * step, first + (index + 1) * step)
+        out_ref[index, :own, :] += jnp.dot(
+            shared_hidden_ref[...], s_down[:, taken], preferred_element_type=jnp.float32
+        )
+
+
+def down_expert(hidden_ref, expert, first, down, out_ref):
     inner = down.shape[1]
     count, _, step = out_ref.shape
-    own = shared_hidden_ref.shape[0]
     for index in range(count):
         taken = slice(first + index * step, first + (index + 1) * step)
         for rows in row_blocks(hidden_ref.shape[0]):
@@ -192,10 +201,6 @@
                 preferred_element_type=jnp.float32,
             )
             out_ref[index, rows, :] = term if expert == 0 else term + out_ref[index, rows, :]
-        if expert == 0:
-            out_ref[index, :own, :] += jnp.dot(
-                shared_hidden_ref[...], s_down[:, taken], preferred_element_type=jnp.float32
-            )
 
 
 def leave(me, own, out_ref, outs):
@@ -220,12 +225,13 @@
     chunks, refs = refs[:part_count], refs[part_count:]
     (
         hidden_ref, shared_hidden_ref, *outs,
-        lhs_ref, square_ref, share_ref, buffer, shared_buffer, out_ref, sems,
+        lhs_ref, square_ref, share_ref, buffer, shared_buffer, s_down_buffer, out_ref, sems,
     ) = refs
     me, node = place_ref[0], place_ref[1]
     late = buffer.shape[0]
     parts = [lax.bitwise_xor(me, part_count - late + index) for index in range(late)]
     moves = weight_moves(parts, (gate, up, s_gate, s_up), (buffer, shared_buffer), sems)
+    moves.append(pltpu.make_async_copy(s_down, s_down_buffer, sems.at[len(moves)]))
     queue = Queue(moves)
     experts, inner, shared_inner = gate.shape[0], gate.shape[2], s_gate.shape[1]
     own, depth = shared_in.shape[0], gain_ref.shape[2]
@@ -273,13 +279,16 @@
             hidden_ref[rows, expert * inner : (expert + 1) * inner] = (
                 act(gate_proj, up_proj) * share_ref[expert, rows, :][:, :1]
             ).astype(jnp.bfloat16)
-        down_expert(hidden_ref, shared_hidden_ref, expert, 0, down, s_down, out_ref)
+        down_expert(hidden_ref, expert, 0, down, out_ref)
+    queue.wait()
+    down_shared(shared_hidden_ref, 0, s_down_buffer, out_ref)
     leave(me, own, out_ref, outs)
 
 
 def down_kernel(first, place_ref, hidden_ref, shared_hidden_ref, down, s_down, *refs):
     for expert in range(down.shape[0]):
-        down_expert(hidden_ref, shared_hidden_ref, expert, first, down, s_down, refs[-1])
+        down_expert(hidden_ref, expert, first, down, refs[-1])
+    down_shared(shared_hidden_ref, first, s_down, refs[-1])
     leave(place_ref[0], shared_hidden_ref.shape[0], refs[-1], refs[:4])
 
 
@@ -414,16 +423,17 @@
                     jax.ShapeDtypeStruct((own, shared_inner), bf16),
                 ]
                 + out_shape,
-                [SMEM, VMEM] + [HBM] * 4 + [VMEM] * (5 + local_count),
+                [SMEM, VMEM] + [HBM] * 4 + [VMEM] * 4 + [HBM] + [VMEM] * local_count,
                 [
                     pltpu.VMEM((LATE, total, depth), bf16),
                     pltpu.VMEM((total, LANES), f32),
                     pltpu.VMEM((experts, total, LANES), f32),
                     *(pltpu.VMEM((LATE, *w.shape[1:]), bf16) for w in weight_scratch),
+                    pltpu.VMEM(s_down.shape, bf16),
                     *down_scratch,
-                    pltpu.SemaphoreType.DMA((LATE * moves,)),
+                    pltpu.SemaphoreType.DMA((LATE * moves + 1,)),
                 ],
-                (place, gain, *up_weights, *sums, *down_weights, *chunks),
+                (place, gain, *up_weights, *sums, w_down, in_hbm(s_down), *chunks),
                 flops + down_flops,
                 read + down_read,
             )

time: 53.5 us -> 52.9 us (0.989)
  local copies, waits for them, and re-layouts: 1.05 us -> 0.31 us
    unnamed x11 -> x9, local copies, waits for them, and re-layouts: 0.93 us -> 0.19 us
where the time goes in v5:
time: 52.9 us; the launch traced here: 52.8 us
  waiting for transfers between devices  17.5 us (33%)
  starting transfers between devices  17 us (32%)
  Pallas kernels  16.7 us (32%)
  other arithmetic  1.04 us (2%)
    ppermute x14, waiting for transfers between devices, swap(): return lax.ppermute(x, axis, [(i, i ^ offset) for i in range(size)])  17.5 us
    ppermute x14, starting transfers between devices, swap(): return lax.ppermute(x, axis, [(i, i ^ offset) for i in range(size)])  17 us
    pallas_call x6, Pallas kernels, call(): pl.pallas_call(kernel, out_shape=out_shape, in_specs=in_specs, out_specs=...  16.7 us
  transfers between devices with their start and end apart: 14, of which 7 were waited for; matrix products, arithmetic and copies ran while one was open for 1% of the time, Pallas kernels for 13%

profile of v5, /device:TPU:0, one launch (start us, length us, event | category | flops | bytes accessed | tf_op | source)
XLA Modules:
  0.0 52.8 jit_solution(13041890964197988432)
XLA Ops:
  0.0 1.0 %pack.1 = (bf16[32,1408]{1,0:T(8,128)(2,1)S(1)}, f32[4,1,1280]{2,1,0:T(1,128)S(1)}) custom-call(s32[1]{0:T(128)} %bitcast.place_ref.part_ref, bf16[32,1280]{1,0:T(8,128)(2,1)} %refs_0_.3, s32[2,8]{1,0:T(2,128)} %bitcast.60, bf16[4,8]{1,0:T(4,128)(2,1)} %bitcast.61, f32[4,1,1280]{2,1,0:T(1,128)} %bitcast.59), custom_call_target="tpu_custom_call" | custom-call | flops 40000000000 | tf_op jit(solution)/shard_map/pack/pallas_call | solution.py:304
  1.0 3.1 %collective-permute-start = (bf16[32,1408]{1,0:T(8,128)(2,1)S(1)}, bf16[32,1408]{1,0:T(8,128)(2,1)S(1)}, u32[]{:S(2)}, u32[]{:S(2)}) collective-permute-start(bf16[32,1408]{1,0:T(8,128)(2,1)S(1)} %get-tuple-element.19), channel_id=1, source_target_pairs={{0,4},{4,0},{8,12},{12,8},{1,5},{5,1},{9,13},{13,9},{2,6},{6,2},{1... | collective-permute-start | bytes 270344 | tf_op jit(solution)/shard_map/ppermute | solution.py:23
  4.1 2.6 %collective-permute-start.1 = (bf16[32,1408]{1,0:T(8,128)(2,1)S(1)}, bf16[32,1408]{1,0:T(8,128)(2,1)S(1)}, u32[]{:S(2)}, u32[]{:S(2)}) collective-permute-start(bf16[32,1408]{1,0:T(8,128)(2,1)S(1)} %get-tuple-element.19), channel_id=1, source_target_pairs={{0,8},{4,12},{8,0},{12,4},{1,9},{5,13},{9,1},{13,5},{2,10},{6,14},... | collective-permute-start | bytes 270344 | tf_op jit(solution)/shard_map/ppermute | solution.py:23
  6.7 1.7 %collective-permute-start.4 = (bf16[32,1408]{1,0:T(8,128)(2,1)S(1)}, bf16[32,1408]{1,0:T(8,128)(2,1)S(1)}, u32[]{:S(2)}, u32[]{:S(2)}) collective-permute-start(bf16[32,1408]{1,0:T(8,128)(2,1)S(1)} %get-tuple-element.19), channel_id=1, source_target_pairs={{0,2},{1,3},{2,0},{3,1},{4,6},{5,7},{6,4},{7,5},{8,10},{9,11},{10,... | collective-permute-start | bytes 270344 | tf_op jit(solution)/shard_map/ppermute | solution.py:23
  8.4 0.1 pad_add_fusion.place_ref
  8.5 5.4 %collective-permute-done.1 = bf16[32,1408]{1,0:T(8,128)(2,1)S(1)} collective-permute-done((bf16[32,1408]{1,0:T(8,128)(2,1)S(1)}, bf16[32,1408]{1,0:T(8,128)(2,1)S(1)}, u32[]{:S(2)}, u32[]{:S(2)}) %collective-permute-start.1) | collective-permute-done | bytes 90144 | tf_op jit(solution)/shard_map/ppermute | solution.py:23
  13.9 1.6 %collective-permute-start.5 = (bf16[96,1408]{1,0:T(8,128)(2,1)S(1)}, bf16[96,1408]{1,0:T(8,128)(2,1)S(1)}, u32[]{:S(2)}, u32[]{:S(2)}) collective-permute-start(bf16[96,1408]{1,0:T(8,128)(2,1)S(1)} %pad_maximum_fusion), channel_id=1, source_target_pairs={{0,2},{1,3},{2,0},{3,1},{4,6},{5,7},{6,4},{7,5},{8,10},{9,11},{10,... | collective-permute-start | bytes 811016 | tf_op jit(solution)/shard_map/ppermute | solution.py:23
  15.6 0.1 collective-permute-start.3
  15.7 0.0 slice-start
  15.7 0.0 slice-start.1
  15.7 3.4 %project.2 = (f32[128,2048]{1,0:T(8,128)S(1)}, f32[32,512]{1,0:T(8,128)S(1)}, f32[128,128]{1,0:T(8,128)S(1)}) custom-call(s32[1]{0:T(128)} %bitcast.place_ref.part_ref, bf16[128,1408]{1,0:T(8,128)(2,1)S(1)} %constant_dynamic-update-slice_fusion.chunk_ref.refs_0_, f32[4,1,1280]{2,1,0:T(1,128)S(1)} %get-tuple-element.20.gain_ref, bf16[2,5120,512]{2,1,0:T(8,128)(2,1)} %gate.1, ...), custom_call_target="tpu_custom_call" | custom-call | flops 713031680 | bytes 6553600 | tf_op jit(solution)/shard_map/project/pallas_call | solution.py:304
  19.1 1.3 %collective-permute-done.5.refs_1_ = bf16[96,1408]{1,0:T(8,128)(2,1)S(1)} collective-permute-done((bf16[96,1408]{1,0:T(8,128)(2,1)S(1)}, bf16[96,1408]{1,0:T(8,128)(2,1)S(1)}, u32[]{:S(2)}, u32[]{:S(2)}) %collective-permute-start.5) | collective-permute-done | bytes 270368 | tf_op jit(solution)/shard_map/ppermute | solution.py:23
  20.5 0.1 collective-permute-start.6
  20.6 0.0 slice-start.2
  20.6 3.4 %project.3 = (f32[128,2048]{1,0:T(8,128)S(1)}, f32[32,512]{1,0:T(8,128)S(1)}, f32[128,128]{1,0:T(8,128)S(1)}) custom-call(s32[1]{0:T(128)} %bitcast.17.part_ref, bf16[128,1408]{1,0:T(8,128)(2,1)S(1)} %collective-permute-done.3.chunk_ref.refs_1_, ...), custom_call_target="tpu_custom_call", output_to_operand_aliasing={{0}: (7, {}), {1}: (8, {}), {2}: (9, {})} | custom-call | flops 713031680 | bytes 6553600 | tf_op jit(solution)/shard_map/project/pallas_call | solution.py:304
  24.1 0.1 slice-done.2
  24.3 8.8 %finish.1 = (bf16[128,1024]{1,0:T(8,128)(2,1)}, bf16[32,256]{1,0:T(8,128)(2,1)}, f32[2,2,8,5120]{3,2,1,0:T(8,128)S(1)}, f32[2,2,8,5120]{3,2,1,0:T(8,128)S(1)}, b...) custom-call(s32[2]{0:T(128)S(1)} %pad_add_fusion.place_ref, ...), custom_call_target="tpu_custom_call" | custom-call | flops 2139095040 | bytes 19660800 | tf_op jit(solution)/shard_map/finish/pallas_call | solution.py:304
  33.1 0.5 %collective-permute-start.10 = (bf16[2,2,8,5120]{3,2,1,0:T(8,128)(2,1)S(1)}, bf16[2,2,8,5120]{3,2,1,0:T(8,128)(2,1)S(1)}, u32[]{:S(2)}, u32[]{:S(2)}) collective-permute-start(bf16[2,2,8,5120]{3,2,1,0:T(8,128)(2,1)S(1)} %get-tuple-element.30), channel_id=1, source_target_pairs={{0,1},{1,0},{2,3},{3,2},{4,5},{5,4},{6,7},{7,6},{8,9},{9,8},{10,11... | collective-permute-start | bytes 983048 | tf_op jit(solution)/shard_map/ppermute | solution.py:23
  33.6 0.1 collective-permute-start.7
  33.7 1.2 %collective-permute-done.10 = bf16[2,2,8,5120]{3,2,1,0:T(8,128)(2,1)S(1)} collective-permute-done((bf16[2,2,8,5120]{3,2,1,0:T(8,128)(2,1)S(1)}, bf16[2,2,8,5120]{3,2,1,0:T(8,128)(2,1)S(1)}, u32[]{:S(2)}, u32[]{:S(2)}) %collective-permute-start.10) | collective-permute-done | bytes 327712 | tf_op jit(solution)/shard_map/ppermute | solution.py:23
  34.9 0.1 convert_add_fusion.far_ref
  35.0 1.5 %collective-permute-start.11 = (bf16[2,8,5120]{2,1,0:T(8,128)(2,1)S(1)}, bf16[2,8,5120]{2,1,0:T(8,128)(2,1)S(1)}, u32[]{:S(2)}, u32[]{:S(2)}) collective-permute-start(bf16[2,8,5120]{2,1,0:T(8,128)(2,1)S(1)} %fusion.2), channel_id=1, source_target_pairs={{0,2},{1,3},{2,0},{3,1},{4,6},{5,7},{6,4},{7,5},{8,10},{9,11},{10,... | collective-permute-start | bytes 491528 | tf_op jit(solution)/shard_map/ppermute | solution.py:23
  36.4 0.1 convert_add_fusion.1
  36.5 0.7 %collective-permute-start.8 = (bf16[2,8,5120]{2,1,0:T(8,128)(2,1)S(1)}, bf16[2,8,5120]{2,1,0:T(8,128)(2,1)S(1)}, u32[]{:S(2)}, u32[]{:S(2)}) collective-permute-start(bf16[2,8,5120]{2,1,0:T(8,128)(2,1)S(1)} %fusion.1), channel_id=1, source_target_pairs={{0,2},{1,3},{2,0},{3,1},{4,6},{5,7},{6,4},{7,5},{8,10},{9,11},{10,... | collective-permute-start | bytes 491528 | tf_op jit(solution)/shard_map/ppermute | solution.py:23
  37.3 4.8 %collective-permute-done.11.refs_0_ = bf16[2,8,5120]{2,1,0:T(8,128)(2,1)S(1)} collective-permute-done((bf16[2,8,5120]{2,1,0:T(8,128)(2,1)S(1)}, bf16[2,8,5120]{2,1,0:T(8,128)(2,1)S(1)}, u32[]{:S(2)}, u32[]{:S(2)}) %collective-permute-start.11) | collective-permute-done | bytes 163872 | tf_op jit(solution)/shard_map/ppermute | solution.py:23
  42.1 3.1 %collective-permute-start.12 = (bf16[8,5120]{1,0:T(8,128)(2,1)S(1)}, bf16[8,5120]{1,0:T(8,128)(2,1)S(1)}, u32[]{:S(2)}, u32[]{:S(2)}) collective-permute-start(bf16[8,5120]{1,0:T(8,128)(2,1)S(1)} %get-tuple-element.31), channel_id=1, source_target_pairs={{0,8},{4,12},{8,0},{12,4},{1,9},{5,13},{9,1},{13,5},{2,10},{6,14},... | collective-permute-start | bytes 245768 | tf_op jit(solution)/shard_map/ppermute | solution.py:23
  45.2 1.5 %collective-permute-start.13 = (bf16[8,5120]{1,0:T(8,128)(2,1)S(1)}, bf16[8,5120]{1,0:T(8,128)(2,1)S(1)}, u32[]{:S(2)}, u32[]{:S(2)}) collective-permute-start(bf16[8,5120]{1,0:T(8,128)(2,1)S(1)} %get-tuple-element.32), channel_id=1, source_target_pairs={{0,12},{4,8},{8,4},{12,0},{1,13},{5,9},{9,5},{13,1},{2,14},{6,10},... | collective-permute-start | bytes 245768 | tf_op jit(solution)/shard_map/ppermute | solution.py:23
  46.7 0.6 %collective-permute-start.9 = (bf16[8,5120]{1,0:T(8,128)(2,1)S(1)}, bf16[8,5120]{1,0:T(8,128)(2,1)S(1)}, u32[]{:S(2)}, u32[]{:S(2)}) collective-permute-start(bf16[8,5120]{1,0:T(8,128)(2,1)S(1)} %fusion.8), channel_id=1, source_target_pairs={{0,4},{4,0},{8,12},{12,8},{1,5},{5,1},{9,13},{13,9},{2,6},{6,2},{1... | collective-permute-start | bytes 245768 | tf_op jit(solution)/shard_map/ppermute | solution.py:23
  47.3 3.1 %collective-permute-done.12 = bf16[8,5120]{1,0:T(8,128)(2,1)S(1)} collective-permute-done((bf16[8,5120]{1,0:T(8,128)(2,1)S(1)}, bf16[8,5120]{1,0:T(8,128)(2,1)S(1)}, u32[]{:S(2)}, u32[]{:S(2)}) %collective-permute-start.12) | collective-permute-done | bytes 81952 | tf_op jit(solution)/shard_map/ppermute | solution.py:23
  50.3 1.5 %collective-permute-done.13 = bf16[8,5120]{1,0:T(8,128)(2,1)S(1)} collective-permute-done((bf16[8,5120]{1,0:T(8,128)(2,1)S(1)}, bf16[8,5120]{1,0:T(8,128)(2,1)S(1)}, u32[]{:S(2)}, u32[]{:S(2)}) %collective-permute-start.13) | collective-permute-done | bytes 81952 | tf_op jit(solution)/shard_map/ppermute | solution.py:23
  51.9 0.2 collective-permute-done.9
  52.1 0.7 %fusion.7 = bf16[8,5120]{1,0:T(8,128)(2,1)} fusion(f32[8,5120]{1,0:T(8,128)S(1)} %bitcast.58, f32[2,8,5120]{2,1,0:T(8,128)S(1)} %fusion, bf16[8,5120]{1,0:T(8,128)(2,1)S(1)} %collective-permute-done.13, bf16[8,5120]{1,0:T(8,128)(2,1)S(1)} %collective-permute-done.12, bf16[8,5120]{1,0:T(8,128)(2,1)S(1)} %collective-permute-done.9), kind=kLoop, calls=%fused_computation.15 | loop fusion | flops 327680 | bytes 655360 | tf_op jit(solution)/shard_map/convert_element_type | solution.py:487
  (31 shorter events, 0.4 us)
Async XLA Ops:
  1.0 7.5 %collective-permute-start = (bf16[32,1408]{1,0:T(8,128)(2,1)S(1)}, bf16[32,1408]{1,0:T(8,128)(2,1)S(1)}, u32[]{:S(2)}, u32[]{:S(2)}) collective-permute-start(bf16[32,1408]{1,0:T(8,128)(2,1)S(1)} %get-tuple-element.19), channel_id=1, source_target_pairs={{0,4},{4,0},{8,12},{12,8},{1,5},{5,1},{9,13},{13,9},{2,6},{6,2},{1... | collective-permute-start | bytes 270344 | tf_op jit(solution)/shard_map/ppermute | solution.py:23
  4.1 9.8 %collective-permute-start.1 = (bf16[32,1408]{1,0:T(8,128)(2,1)S(1)}, bf16[32,1408]{1,0:T(8,128)(2,1)S(1)}, u32[]{:S(2)}, u32[]{:S(2)}) collective-permute-start(bf16[32,1408]{1,0:T(8,128)(2,1)S(1)} %get-tuple-element.19), channel_id=1, source_target_pairs={{0,8},{4,12},{8,0},{12,4},{1,9},{5,13},{9,1},{13,5},{2,10},{6,14},... | collective-permute-start | bytes 270344 | tf_op jit(solution)/shard_map/ppermute | solution.py:23
  6.7 7.2 %collective-permute-start.2 = (bf16[32,1408]{1,0:T(8,128)(2,1)S(1)}, bf16[32,1408]{1,0:T(8,128)(2,1)S(1)}, u32[]{:S(2)}, u32[]{:S(2)}) collective-permute-start(bf16[32,1408]{1,0:T(8,128)(2,1)S(1)} %get-tuple-element.19), channel_id=1, source_target_pairs={{0,12},{4,8},{8,4},{12,0},{1,13},{5,9},{9,5},{13,1},{2,14},{6,10},... | collective-permute-start | bytes 270344 | tf_op jit(solution)/shard_map/ppermute | solution.py:23
  6.7 9.0 %collective-permute-start.4 = (bf16[32,1408]{1,0:T(8,128)(2,1)S(1)}, bf16[32,1408]{1,0:T(8,128)(2,1)S(1)}, u32[]{:S(2)}, u32[]{:S(2)}) collective-permute-start(bf16[32,1408]{1,0:T(8,128)(2,1)S(1)} %get-tuple-element.19), channel_id=1, source_target_pairs={{0,2},{1,3},{2,0},{3,1},{4,6},{5,7},{6,4},{7,5},{8,10},{9,11},{10,... | collective-permute-start | bytes 270344 | tf_op jit(solution)/shard_map/ppermute | solution.py:23
  13.9 6.5 %collective-permute-start.5 = (bf16[96,1408]{1,0:T(8,128)(2,1)S(1)}, bf16[96,1408]{1,0:T(8,128)(2,1)S(1)}, u32[]{:S(2)}, u32[]{:S(2)}) collective-permute-start(bf16[96,1408]{1,0:T(8,128)(2,1)S(1)} %pad_maximum_fusion), channel_id=1, source_target_pairs={{0,2},{1,3},{2,0},{3,1},{4,6},{5,7},{6,4},{7,5},{8,10},{9,11},{10,... | collective-permute-start | bytes 811016 | tf_op jit(solution)/shard_map/ppermute | solution.py:23
  15.6 5.1 %collective-permute-start.3 = (bf16[128,1408]{1,0:T(8,128)(2,1)S(1)}, bf16[128,1408]{1,0:T(8,128)(2,1)S(1)}, u32[]{:S(2)}, u32[]{:S(2)}) collective-permute-start(bf16[128,1408]{1,0:T(8,128)(2,1)S(1)} %constant_dynamic-update-slice_fusion.chunk_ref.refs_0_), channel_id=1, source_target_pairs={{0,1},{1,0},{2,3},{3,2},{4,5},{5,4},{6,7},{7,6},{8,9},{9,8},{10,11... | collective-permute-start | bytes 1081352 | tf_op jit(solution)/shard_map/ppermute | solution.py:23
  15.7 8.4 %slice-start = ((s8[10485760]{0:T(1024)(128)(4,1)}), s8[4194304]{0:T(1024)(128)(4,1)S(1)}, s32[]{:S(2)}) async-start(s8[10485760]{0:T(1024)(128)(4,1)} %bitcast.53), calls=%async_computation | async-start | bytes 8388608
  15.7 8.4 %slice-start.1 = ((s8[10485760]{0:T(1024)(128)(4,1)}), s8[4194304]{0:T(1024)(128)(4,1)S(1)}, s32[]{:S(2)}) async-start(s8[10485760]{0:T(1024)(128)(4,1)} %bitcast.53), calls=%async_computation.1 | async-start | bytes 8388608
  20.5 3.6 %collective-permute-start.6 = (bf16[128,1408]{1,0:T(8,128)(2,1)S(1)}, bf16[128,1408]{1,0:T(8,128)(2,1)S(1)}, u32[]{:S(2)}, u32[]{:S(2)}) collective-permute-start(bf16[128,1408]{1,0:T(8,128)(2,1)S(1)} %join.1.refs_2_), channel_id=1, source_target_pairs={{0,1},{1,0},{2,3},{3,2},{4,5},{5,4},{6,7},{7,6},{8,9},{9,8},{10,11... | collective-permute-start | bytes 1081352 | tf_op jit(solution)/shard_map/ppermute | solution.py:23
  20.6 3.7 %slice-start.2 = ((s8[10485760]{0:T(1024)(128)(4,1)}), s8[2097152]{0:T(1024)(128)(4,1)S(1)}, s32[]{:S(2)}) async-start(s8[10485760]{0:T(1024)(128)(4,1)} %bitcast.53), calls=%async_computation.2 | async-start | bytes 4194304
  33.1 1.8 %collective-permute-start.10 = (bf16[2,2,8,5120]{3,2,1,0:T(8,128)(2,1)S(1)}, bf16[2,2,8,5120]{3,2,1,0:T(8,128)(2,1)S(1)}, u32[]{:S(2)}, u32[]{:S(2)}) collective-permute-start(bf16[2,2,8,5120]{3,2,1,0:T(8,128)(2,1)S(1)} %get-tuple-element.30), channel_id=1, source_target_pairs={{0,1},{1,0},{2,3},{3,2},{4,5},{5,4},{6,7},{7,6},{8,9},{9,8},{10,11... | collective-permute-start | bytes 983048 | tf_op jit(solution)/shard_map/ppermute | solution.py:23
  33.6 2.8 %collective-permute-start.7 = (bf16[2,2,8,5120]{3,2,1,0:T(8,128)(2,1)S(1)}, bf16[2,2,8,5120]{3,2,1,0:T(8,128)(2,1)S(1)}, u32[]{:S(2)}, u32[]{:S(2)}) collective-permute-start(bf16[2,2,8,5120]{3,2,1,0:T(8,128)(2,1)S(1)} %get-tuple-element.28), channel_id=1, source_target_pairs={{0,1},{1,0},{2,3},{3,2},{4,5},{5,4},{6,7},{7,6},{8,9},{9,8},{10,11... | collective-permute-start | bytes 983048 | tf_op jit(solution)/shard_map/ppermute | solution.py:23
  35.0 7.1 %collective-permute-start.11 = (bf16[2,8,5120]{2,1,0:T(8,128)(2,1)S(1)}, bf16[2,8,5120]{2,1,0:T(8,128)(2,1)S(1)}, u32[]{:S(2)}, u32[]{:S(2)}) collective-permute-start(bf16[2,8,5120]{2,1,0:T(8,128)(2,1)S(1)} %fusion.2), channel_id=1, source_target_pairs={{0,2},{1,3},{2,0},{3,1},{4,6},{5,7},{6,4},{7,5},{8,10},{9,11},{10,... | collective-permute-start | bytes 491528 | tf_op jit(solution)/shard_map/ppermute | solution.py:23
  36.5 10.1 %collective-permute-start.8 = (bf16[2,8,5120]{2,1,0:T(8,128)(2,1)S(1)}, bf16[2,8,5120]{2,1,0:T(8,128)(2,1)S(1)}, u32[]{:S(2)}, u32[]{:S(2)}) collective-permute-start(bf16[2,8,5120]{2,1,0:T(8,128)(2,1)S(1)} %fusion.1), channel_id=1, source_target_pairs={{0,2},{1,3},{2,0},{3,1},{4,6},{5,7},{6,4},{7,5},{8,10},{9,11},{10,... | collective-permute-start | bytes 491528 | tf_op jit(solution)/shard_map/ppermute | solution.py:23
  42.1 8.2 %collective-permute-start.12 = (bf16[8,5120]{1,0:T(8,128)(2,1)S(1)}, bf16[8,5120]{1,0:T(8,128)(2,1)S(1)}, u32[]{:S(2)}, u32[]{:S(2)}) collective-permute-start(bf16[8,5120]{1,0:T(8,128)(2,1)S(1)} %get-tuple-element.31), channel_id=1, source_target_pairs={{0,8},{4,12},{8,0},{12,4},{1,9},{5,13},{9,1},{13,5},{2,10},{6,14},... | collective-permute-start | bytes 245768 | tf_op jit(solution)/shard_map/ppermute | solution.py:23
  45.2 6.7 %collective-permute-start.13 = (bf16[8,5120]{1,0:T(8,128)(2,1)S(1)}, bf16[8,5120]{1,0:T(8,128)(2,1)S(1)}, u32[]{:S(2)}, u32[]{:S(2)}) collective-permute-start(bf16[8,5120]{1,0:T(8,128)(2,1)S(1)} %get-tuple-element.32), channel_id=1, source_target_pairs={{0,12},{4,8},{8,4},{12,0},{1,13},{5,9},{9,5},{13,1},{2,14},{6,10},... | collective-permute-start | bytes 245768 | tf_op jit(solution)/shard_map/ppermute | solution.py:23
  46.7 5.4 %collective-permute-start.9 = (bf16[8,5120]{1,0:T(8,128)(2,1)S(1)}, bf16[8,5120]{1,0:T(8,128)(2,1)S(1)}, u32[]{:S(2)}, u32[]{:S(2)}) collective-permute-start(bf16[8,5120]{1,0:T(8,128)(2,1)S(1)} %fusion.8), channel_id=1, source_target_pairs={{0,4},{4,0},{8,12},{12,8},{1,5},{5,1},{9,13},{13,9},{2,6},{6,2},{1... | collective-permute-start | bytes 245768 | tf_op jit(solution)/shard_map/ppermute | solution.py:23

commit v6 on v5

--- a/solution.py
+++ b/solution.py
@@ -179,20 +179,20 @@
     return [slice(start, start + block) for start in range(0, total, block)]
 
 
-def down_shared(shared_hidden_ref, first, s_down, out_ref):
-    count, _, step = out_ref.shape
+def down_shared(shared_hidden_ref, first, s_down, out_ref, pieces):
+    step = out_ref.shape[2]
     own = shared_hidden_ref.shape[0]
-    for index in range(count):
+    for index in pieces:
         taken = slice(first + index * step, first + (index + 1) * step)
         out_ref[index, :own, :] += jnp.dot(
             shared_hidden_ref[...], s_down[:, taken], preferred_element_type=jnp.float32
         )
 
 
-def down_expert(hidden_ref, expert, first, down, out_ref):
+def down_expert(hidden_ref, expert, first, down, out_ref, pieces):
     inner = down.shape[1]
-    count, _, step = out_ref.shape
-    for index in range(count):
+    step = out_ref.shape[2]
+    for index in pieces:
         taken = slice(first + index * step, first + (index + 1) * step)
         for rows in row_blocks(hidden_ref.shape[0]):
             term = jnp.dot(
@@ -203,11 +203,11 @@
             out_ref[index, rows, :] = term if expert == 0 else term + out_ref[index, rows, :]
 
 
-def leave(me, own, out_ref, outs):
-    count, _, step = out_ref.shape
+def leave(me, own, out_ref, outs, pieces):
+    step = out_ref.shape[2]
     keep_far, keep_near, send_far, send_near = outs
     pairs, near, tokens = keep_near.shape[:3]
-    for index in range(count):
+    for index in pieces:
         columns = slice(index * step, (index + 1) * step)
         for pair in range(pairs):
             for side, to_refs in enumerate(((keep_near, keep_far), (send_near, send_far))):
@@ -279,17 +279,20 @@
             hidden_ref[rows, expert * inner : (expert + 1) * inner] = (
                 act(gate_proj, up_proj) * share_ref[expert, rows, :][:, :1]
             ).astype(jnp.bfloat16)
-        down_expert(hidden_ref, expert, 0, down, out_ref)
+        if expert < experts - 1:
+            down_expert(hidden_ref, expert, 0, down, out_ref, range(out_ref.shape[0]))
     queue.wait()
-    down_shared(shared_hidden_ref, 0, s_down_buffer, out_ref)
-    leave(me, own, out_ref, outs)
+    for index in range(out_ref.shape[0]):
+        down_expert(hidden_ref, experts - 1, 0, down, out_ref, [index])
+        down_shared(shared_hidden_ref, 0, s_down_buffer, out_ref, [index])
+        leave(me, own, out_ref, outs, [index])
 
 
 def down_kernel(first, place_ref, hidden_ref, shared_hidden_ref, down, s_down, *refs):
     for expert in range(down.shape[0]):
-        down_expert(hidden_ref, expert, first, down, refs[-1])
-    down_shared(shared_hidden_ref, first, s_down, refs[-1])
-    leave(place_ref[0], shared_hidden_ref.shape[0], refs[-1], refs[:4])
+        down_expert(hidden_ref, expert, first, down, refs[-1], range(refs[-1].shape[0]))
+    down_shared(shared_hidden_ref, first, s_down, refs[-1], range(refs[-1].shape[0]))
+    leave(place_ref[0], shared_hidden_ref.shape[0], refs[-1], refs[:4], range(refs[-1].shape[0]))
 
 
 def call(kernel, name, out_shape, in_specs, scratch, args, flops=0, read=0, aliases=None):

time: 52.9 us -> 52.5 us (level)
  no operation moved by 1% of the time
where the time goes in v6:
time: 52.5 us; the launch traced here: 52.4 us
  waiting for transfers between devices  17.5 us (33%)
  starting transfers between devices  16.9 us (32%)
  Pallas kernels  16.4 us (31%)
  other arithmetic  1.04 us (2%)
    ppermute x14, waiting for transfers between devices, swap(): return lax.ppermute(x, axis, [(i, i ^ offset) for i in range(size)])  17.5 us
    ppermute x14, starting transfers between devices, swap(): return lax.ppermute(x, axis, [(i, i ^ offset) for i in range(size)])  16.9 us
    pallas_call x6, Pallas kernels, call(): pl.pallas_call(kernel, out_shape=out_shape, in_specs=in_specs, out_specs=...  16.4 us
  transfers between devices with their start and end apart: 14, of which 7 were waited for; matrix products, arithmetic and copies ran while one was open for 1% of the time, Pallas kernels for 13%

profile of v6, /device:TPU:0, one launch (start us, length us, event | category | flops | bytes accessed | tf_op | source)
XLA Modules:
  0.0 52.4 jit_solution(7129578937184567210)
XLA Ops:
  0.0 1.0 %pack.1 = (bf16[32,1408]{1,0:T(8,128)(2,1)S(1)}, f32[4,1,1280]{2,1,0:T(1,128)S(1)}) custom-call(s32[1]{0:T(128)} %bitcast.place_ref.part_ref, bf16[32,1280]{1,0:T(8,128)(2,1)} %refs_0_.3, s32[2,8]{1,0:T(2,128)} %bitcast.60, bf16[4,8]{1,0:T(4,128)(2,1)} %bitcast.61, f32[4,1,1280]{2,1,0:T(1,128)} %bitcast.59), custom_call_target="tpu_custom_call" | custom-call | flops 40000000000 | tf_op jit(solution)/shard_map/pack/pallas_call | solution.py:307
  1.0 3.1 %collective-permute-start = (bf16[32,1408]{1,0:T(8,128)(2,1)S(1)}, bf16[32,1408]{1,0:T(8,128)(2,1)S(1)}, u32[]{:S(2)}, u32[]{:S(2)}) collective-permute-start(bf16[32,1408]{1,0:T(8,128)(2,1)S(1)} %get-tuple-element.19), channel_id=1, source_target_pairs={{0,4},{4,0},{8,12},{12,8},{1,5},{5,1},{9,13},{13,9},{2,6},{6,2},{1... | collective-permute-start | bytes 270344 | tf_op jit(solution)/shard_map/ppermute | solution.py:23
  4.1 2.6 %collective-permute-start.1 = (bf16[32,1408]{1,0:T(8,128)(2,1)S(1)}, bf16[32,1408]{1,0:T(8,128)(2,1)S(1)}, u32[]{:S(2)}, u32[]{:S(2)}) collective-permute-start(bf16[32,1408]{1,0:T(8,128)(2,1)S(1)} %get-tuple-element.19), channel_id=1, source_target_pairs={{0,8},{4,12},{8,0},{12,4},{1,9},{5,13},{9,1},{13,5},{2,10},{6,14},... | collective-permute-start | bytes 270344 | tf_op jit(solution)/shard_map/ppermute | solution.py:23
  6.7 1.7 %collective-permute-start.4 = (bf16[32,1408]{1,0:T(8,128)(2,1)S(1)}, bf16[32,1408]{1,0:T(8,128)(2,1)S(1)}, u32[]{:S(2)}, u32[]{:S(2)}) collective-permute-start(bf16[32,1408]{1,0:T(8,128)(2,1)S(1)} %get-tuple-element.19), channel_id=1, source_target_pairs={{0,2},{1,3},{2,0},{3,1},{4,6},{5,7},{6,4},{7,5},{8,10},{9,11},{10,... | collective-permute-start | bytes 270344 | tf_op jit(solution)/shard_map/ppermute | solution.py:23
  8.4 0.1 pad_add_fusion.place_ref
  8.5 5.4 %collective-permute-done.1 = bf16[32,1408]{1,0:T(8,128)(2,1)S(1)} collective-permute-done((bf16[32,1408]{1,0:T(8,128)(2,1)S(1)}, bf16[32,1408]{1,0:T(8,128)(2,1)S(1)}, u32[]{:S(2)}, u32[]{:S(2)}) %collective-permute-start.1) | collective-permute-done | bytes 90144 | tf_op jit(solution)/shard_map/ppermute | solution.py:23
  13.9 1.6 %collective-permute-start.5 = (bf16[96,1408]{1,0:T(8,128)(2,1)S(1)}, bf16[96,1408]{1,0:T(8,128)(2,1)S(1)}, u32[]{:S(2)}, u32[]{:S(2)}) collective-permute-start(bf16[96,1408]{1,0:T(8,128)(2,1)S(1)} %pad_maximum_fusion), channel_id=1, source_target_pairs={{0,2},{1,3},{2,0},{3,1},{4,6},{5,7},{6,4},{7,5},{8,10},{9,11},{10,... | collective-permute-start | bytes 811016 | tf_op jit(solution)/shard_map/ppermute | solution.py:23
  15.6 0.1 collective-permute-start.3
  15.7 0.0 slice-start
  15.7 0.0 slice-start.1
  15.7 3.4 %project.2 = (f32[128,2048]{1,0:T(8,128)S(1)}, f32[32,512]{1,0:T(8,128)S(1)}, f32[128,128]{1,0:T(8,128)S(1)}) custom-call(s32[1]{0:T(128)} %bitcast.place_ref.part_ref, bf16[128,1408]{1,0:T(8,128)(2,1)S(1)} %constant_dynamic-update-slice_fusion.chunk_ref.refs_0_, f32[4,1,1280]{2,1,0:T(1,128)S(1)} %get-tuple-element.20.gain_ref, bf16[2,5120,512]{2,1,0:T(8,128)(2,1)} %gate.1, ...), custom_call_target="tpu_custom_call" | custom-call | flops 713031680 | bytes 6553600 | tf_op jit(solution)/shard_map/project/pallas_call | solution.py:307
  19.1 1.3 %collective-permute-done.5.refs_1_ = bf16[96,1408]{1,0:T(8,128)(2,1)S(1)} collective-permute-done((bf16[96,1408]{1,0:T(8,128)(2,1)S(1)}, bf16[96,1408]{1,0:T(8,128)(2,1)S(1)}, u32[]{:S(2)}, u32[]{:S(2)}) %collective-permute-start.5) | collective-permute-done | bytes 270368 | tf_op jit(solution)/shard_map/ppermute | solution.py:23
  20.5 0.1 collective-permute-start.6
  20.6 0.0 slice-start.2
  20.6 3.4 %project.3 = (f32[128,2048]{1,0:T(8,128)S(1)}, f32[32,512]{1,0:T(8,128)S(1)}, f32[128,128]{1,0:T(8,128)S(1)}) custom-call(s32[1]{0:T(128)} %bitcast.17.part_ref, bf16[128,1408]{1,0:T(8,128)(2,1)S(1)} %collective-permute-done.3.chunk_ref.refs_1_, ...), custom_call_target="tpu_custom_call", output_to_operand_aliasing={{0}: (7, {}), {1}: (8, {}), {2}: (9, {})} | custom-call | flops 713031680 | bytes 6553600 | tf_op jit(solution)/shard_map/project/pallas_call | solution.py:307
  24.1 0.1 slice-done.2
  24.3 8.4 %finish.1 = (bf16[128,1024]{1,0:T(8,128)(2,1)}, bf16[32,256]{1,0:T(8,128)(2,1)}, f32[2,2,8,5120]{3,2,1,0:T(8,128)S(1)}, f32[2,2,8,5120]{3,2,1,0:T(8,128)S(1)}, b...) custom-call(s32[2]{0:T(128)S(1)} %pad_add_fusion.place_ref, ...), custom_call_target="tpu_custom_call" | custom-call | flops 2139095040 | bytes 19660800 | tf_op jit(solution)/shard_map/finish/pallas_call | solution.py:307
  32.7 0.5 %collective-permute-start.10 = (bf16[2,2,8,5120]{3,2,1,0:T(8,128)(2,1)S(1)}, bf16[2,2,8,5120]{3,2,1,0:T(8,128)(2,1)S(1)}, u32[]{:S(2)}, u32[]{:S(2)}) collective-permute-start(bf16[2,2,8,5120]{3,2,1,0:T(8,128)(2,1)S(1)} %get-tuple-element.30), channel_id=1, source_target_pairs={{0,1},{1,0},{2,3},{3,2},{4,5},{5,4},{6,7},{7,6},{8,9},{9,8},{10,11... | collective-permute-start | bytes 983048 | tf_op jit(solution)/shard_map/ppermute | solution.py:23
  33.2 0.1 collective-permute-start.7
  33.3 1.2 %collective-permute-done.10 = bf16[2,2,8,5120]{3,2,1,0:T(8,128)(2,1)S(1)} collective-permute-done((bf16[2,2,8,5120]{3,2,1,0:T(8,128)(2,1)S(1)}, bf16[2,2,8,5120]{3,2,1,0:T(8,128)(2,1)S(1)}, u32[]{:S(2)}, u32[]{:S(2)}) %collective-permute-start.10) | collective-permute-done | bytes 327712 | tf_op jit(solution)/shard_map/ppermute | solution.py:23
  34.5 0.1 convert_add_fusion.far_ref
  34.6 1.5 %collective-permute-start.11 = (bf16[2,8,5120]{2,1,0:T(8,128)(2,1)S(1)}, bf16[2,8,5120]{2,1,0:T(8,128)(2,1)S(1)}, u32[]{:S(2)}, u32[]{:S(2)}) collective-permute-start(bf16[2,8,5120]{2,1,0:T(8,128)(2,1)S(1)} %fusion.2), channel_id=1, source_target_pairs={{0,2},{1,3},{2,0},{3,1},{4,6},{5,7},{6,4},{7,5},{8,10},{9,11},{10,... | collective-permute-start | bytes 491528 | tf_op jit(solution)/shard_map/ppermute | solution.py:23
  36.0 0.1 convert_add_fusion.1
  36.1 0.7 %collective-permute-start.8 = (bf16[2,8,5120]{2,1,0:T(8,128)(2,1)S(1)}, bf16[2,8,5120]{2,1,0:T(8,128)(2,1)S(1)}, u32[]{:S(2)}, u32[]{:S(2)}) collective-permute-start(bf16[2,8,5120]{2,1,0:T(8,128)(2,1)S(1)} %fusion.1), channel_id=1, source_target_pairs={{0,2},{1,3},{2,0},{3,1},{4,6},{5,7},{6,4},{7,5},{8,10},{9,11},{10,... | collective-permute-start | bytes 491528 | tf_op jit(solution)/shard_map/ppermute | solution.py:23
  36.9 4.8 %collective-permute-done.11.refs_0_ = bf16[2,8,5120]{2,1,0:T(8,128)(2,1)S(1)} collective-permute-done((bf16[2,8,5120]{2,1,0:T(8,128)(2,1)S(1)}, bf16[2,8,5120]{2,1,0:T(8,128)(2,1)S(1)}, u32[]{:S(2)}, u32[]{:S(2)}) %collective-permute-start.11) | collective-permute-done | bytes 163872 | tf_op jit(solution)/shard_map/ppermute | solution.py:23
  41.7 3.1 %collective-permute-start.12 = (bf16[8,5120]{1,0:T(8,128)(2,1)S(1)}, bf16[8,5120]{1,0:T(8,128)(2,1)S(1)}, u32[]{:S(2)}, u32[]{:S(2)}) collective-permute-start(bf16[8,5120]{1,0:T(8,128)(2,1)S(1)} %get-tuple-element.31), channel_id=1, source_target_pairs={{0,8},{4,12},{8,0},{12,4},{1,9},{5,13},{9,1},{13,5},{2,10},{6,14},... | collective-permute-start | bytes 245768 | tf_op jit(solution)/shard_map/ppermute | solution.py:23
  44.8 1.5 %collective-permute-start.13 = (bf16[8,5120]{1,0:T(8,128)(2,1)S(1)}, bf16[8,5120]{1,0:T(8,128)(2,1)S(1)}, u32[]{:S(2)}, u32[]{:S(2)}) collective-permute-start(bf16[8,5120]{1,0:T(8,128)(2,1)S(1)} %get-tuple-element.32), channel_id=1, source_target_pairs={{0,12},{4,8},{8,4},{12,0},{1,13},{5,9},{9,5},{13,1},{2,14},{6,10},... | collective-permute-start | bytes 245768 | tf_op jit(solution)/shard_map/ppermute | solution.py:23
  46.3 0.6 %collective-permute-start.9 = (bf16[8,5120]{1,0:T(8,128)(2,1)S(1)}, bf16[8,5120]{1,0:T(8,128)(2,1)S(1)}, u32[]{:S(2)}, u32[]{:S(2)}) collective-permute-start(bf16[8,5120]{1,0:T(8,128)(2,1)S(1)} %fusion.8), channel_id=1, source_target_pairs={{0,4},{4,0},{8,12},{12,8},{1,5},{5,1},{9,13},{13,9},{2,6},{6,2},{1... | collective-permute-start | bytes 245768 | tf_op jit(solution)/shard_map/ppermute | solution.py:23
  46.9 3.1 %collective-permute-done.12 = bf16[8,5120]{1,0:T(8,128)(2,1)S(1)} collective-permute-done((bf16[8,5120]{1,0:T(8,128)(2,1)S(1)}, bf16[8,5120]{1,0:T(8,128)(2,1)S(1)}, u32[]{:S(2)}, u32[]{:S(2)}) %collective-permute-start.12) | collective-permute-done | bytes 81952 | tf_op jit(solution)/shard_map/ppermute | solution.py:23
  49.9 1.5 %collective-permute-done.13 = bf16[8,5120]{1,0:T(8,128)(2,1)S(1)} collective-permute-done((bf16[8,5120]{1,0:T(8,128)(2,1)S(1)}, bf16[8,5120]{1,0:T(8,128)(2,1)S(1)}, u32[]{:S(2)}, u32[]{:S(2)}) %collective-permute-start.13) | collective-permute-done | bytes 81952 | tf_op jit(solution)/shard_map/ppermute | solution.py:23
  51.5 0.2 collective-permute-done.9
  51.7 0.7 %fusion.7 = bf16[8,5120]{1,0:T(8,128)(2,1)} fusion(f32[8,5120]{1,0:T(8,128)S(1)} %bitcast.58, f32[2,8,5120]{2,1,0:T(8,128)S(1)} %fusion, bf16[8,5120]{1,0:T(8,128)(2,1)S(1)} %collective-permute-done.13, bf16[8,5120]{1,0:T(8,128)(2,1)S(1)} %collective-permute-done.12, bf16[8,5120]{1,0:T(8,128)(2,1)S(1)} %collective-permute-done.9), kind=kLoop, calls=%fused_computation.15 | loop fusion | flops 327680 | bytes 655360 | tf_op jit(solution)/shard_map/convert_element_type | solution.py:490
  (31 shorter events, 0.4 us)
Async XLA Ops:
  1.0 7.5 %collective-permute-start = (bf16[32,1408]{1,0:T(8,128)(2,1)S(1)}, bf16[32,1408]{1,0:T(8,128)(2,1)S(1)}, u32[]{:S(2)}, u32[]{:S(2)}) collective-permute-start(bf16[32,1408]{1,0:T(8,128)(2,1)S(1)} %get-tuple-element.19), channel_id=1, source_target_pairs={{0,4},{4,0},{8,12},{12,8},{1,5},{5,1},{9,13},{13,9},{2,6},{6,2},{1... | collective-permute-start | bytes 270344 | tf_op jit(solution)/shard_map/ppermute | solution.py:23
  4.1 9.8 %collective-permute-start.1 = (bf16[32,1408]{1,0:T(8,128)(2,1)S(1)}, bf16[32,1408]{1,0:T(8,128)(2,1)S(1)}, u32[]{:S(2)}, u32[]{:S(2)}) collective-permute-start(bf16[32,1408]{1,0:T(8,128)(2,1)S(1)} %get-tuple-element.19), channel_id=1, source_target_pairs={{0,8},{4,12},{8,0},{12,4},{1,9},{5,13},{9,1},{13,5},{2,10},{6,14},... | collective-permute-start | bytes 270344 | tf_op jit(solution)/shard_map/ppermute | solution.py:23
  6.7 7.2 %collective-permute-start.2 = (bf16[32,1408]{1,0:T(8,128)(2,1)S(1)}, bf16[32,1408]{1,0:T(8,128)(2,1)S(1)}, u32[]{:S(2)}, u32[]{:S(2)}) collective-permute-start(bf16[32,1408]{1,0:T(8,128)(2,1)S(1)} %get-tuple-element.19), channel_id=1, source_target_pairs={{0,12},{4,8},{8,4},{12,0},{1,13},{5,9},{9,5},{13,1},{2,14},{6,10},... | collective-permute-start | bytes 270344 | tf_op jit(solution)/shard_map/ppermute | solution.py:23
  6.7 9.0 %collective-permute-start.4 = (bf16[32,1408]{1,0:T(8,128)(2,1)S(1)}, bf16[32,1408]{1,0:T(8,128)(2,1)S(1)}, u32[]{:S(2)}, u32[]{:S(2)}) collective-permute-start(bf16[32,1408]{1,0:T(8,128)(2,1)S(1)} %get-tuple-element.19), channel_id=1, source_target_pairs={{0,2},{1,3},{2,0},{3,1},{4,6},{5,7},{6,4},{7,5},{8,10},{9,11},{10,... | collective-permute-start | bytes 270344 | tf_op jit(solution)/shard_map/ppermute | solution.py:23
  13.9 6.5 %collective-permute-start.5 = (bf16[96,1408]{1,0:T(8,128)(2,1)S(1)}, bf16[96,1408]{1,0:T(8,128)(2,1)S(1)}, u32[]{:S(2)}, u32[]{:S(2)}) collective-permute-start(bf16[96,1408]{1,0:T(8,128)(2,1)S(1)} %pad_maximum_fusion), channel_id=1, source_target_pairs={{0,2},{1,3},{2,0},{3,1},{4,6},{5,7},{6,4},{7,5},{8,10},{9,11},{10,... | collective-permute-start | bytes 811016 | tf_op jit(solution)/shard_map/ppermute | solution.py:23
  15.6 5.1 %collective-permute-start.3 = (bf16[128,1408]{1,0:T(8,128)(2,1)S(1)}, bf16[128,1408]{1,0:T(8,128)(2,1)S(1)}, u32[]{:S(2)}, u32[]{:S(2)}) collective-permute-start(bf16[128,1408]{1,0:T(8,128)(2,1)S(1)} %constant_dynamic-update-slice_fusion.chunk_ref.refs_0_), channel_id=1, source_target_pairs={{0,1},{1,0},{2,3},{3,2},{4,5},{5,4},{6,7},{7,6},{8,9},{9,8},{10,11... | collective-permute-start | bytes 1081352 | tf_op jit(solution)/shard_map/ppermute | solution.py:23
  15.7 8.4 %slice-start = ((s8[10485760]{0:T(1024)(128)(4,1)}), s8[4194304]{0:T(1024)(128)(4,1)S(1)}, s32[]{:S(2)}) async-start(s8[10485760]{0:T(1024)(128)(4,1)} %bitcast.53), calls=%async_computation | async-start | bytes 8388608
  15.7 8.4 %slice-start.1 = ((s8[10485760]{0:T(1024)(128)(4,1)}), s8[4194304]{0:T(1024)(128)(4,1)S(1)}, s32[]{:S(2)}) async-start(s8[10485760]{0:T(1024)(128)(4,1)} %bitcast.53), calls=%async_computation.1 | async-start | bytes 8388608
  20.5 3.6 %collective-permute-start.6 = (bf16[128,1408]{1,0:T(8,128)(2,1)S(1)}, bf16[128,1408]{1,0:T(8,128)(2,1)S(1)}, u32[]{:S(2)}, u32[]{:S(2)}) collective-permute-start(bf16[128,1408]{1,0:T(8,128)(2,1)S(1)} %join.1.refs_2_), channel_id=1, source_target_pairs={{0,1},{1,0},{2,3},{3,2},{4,5},{5,4},{6,7},{7,6},{8,9},{9,8},{10,11... | collective-permute-start | bytes 1081352 | tf_op jit(solution)/shard_map/ppermute | solution.py:23
  20.6 3.7 %slice-start.2 = ((s8[10485760]{0:T(1024)(128)(4,1)}), s8[2097152]{0:T(1024)(128)(4,1)S(1)}, s32[]{:S(2)}) async-start(s8[10485760]{0:T(1024)(128)(4,1)} %bitcast.53), calls=%async_computation.2 | async-start | bytes 4194304
  32.7 1.8 %collective-permute-start.10 = (bf16[2,2,8,5120]{3,2,1,0:T(8,128)(2,1)S(1)}, bf16[2,2,8,5120]{3,2,1,0:T(8,128)(2,1)S(1)}, u32[]{:S(2)}, u32[]{:S(2)}) collective-permute-start(bf16[2,2,8,5120]{3,2,1,0:T(8,128)(2,1)S(1)} %get-tuple-element.30), channel_id=1, source_target_pairs={{0,1},{1,0},{2,3},{3,2},{4,5},{5,4},{6,7},{7,6},{8,9},{9,8},{10,11... | collective-permute-start | bytes 983048 | tf_op jit(solution)/shard_map/ppermute | solution.py:23
  33.2 2.8 %collective-permute-start.7 = (bf16[2,2,8,5120]{3,2,1,0:T(8,128)(2,1)S(1)}, bf16[2,2,8,5120]{3,2,1,0:T(8,128)(2,1)S(1)}, u32[]{:S(2)}, u32[]{:S(2)}) collective-permute-start(bf16[2,2,8,5120]{3,2,1,0:T(8,128)(2,1)S(1)} %get-tuple-element.28), channel_id=1, source_target_pairs={{0,1},{1,0},{2,3},{3,2},{4,5},{5,4},{6,7},{7,6},{8,9},{9,8},{10,11... | collective-permute-start | bytes 983048 | tf_op jit(solution)/shard_map/ppermute | solution.py:23
  34.6 7.1 %collective-permute-start.11 = (bf16[2,8,5120]{2,1,0:T(8,128)(2,1)S(1)}, bf16[2,8,5120]{2,1,0:T(8,128)(2,1)S(1)}, u32[]{:S(2)}, u32[]{:S(2)}) collective-permute-start(bf16[2,8,5120]{2,1,0:T(8,128)(2,1)S(1)} %fusion.2), channel_id=1, source_target_pairs={{0,2},{1,3},{2,0},{3,1},{4,6},{5,7},{6,4},{7,5},{8,10},{9,11},{10,... | collective-permute-start | bytes 491528 | tf_op jit(solution)/shard_map/ppermute | solution.py:23
  36.1 10.1 %collective-permute-start.8 = (bf16[2,8,5120]{2,1,0:T(8,128)(2,1)S(1)}, bf16[2,8,5120]{2,1,0:T(8,128)(2,1)S(1)}, u32[]{:S(2)}, u32[]{:S(2)}) collective-permute-start(bf16[2,8,5120]{2,1,0:T(8,128)(2,1)S(1)} %fusion.1), channel_id=1, source_target_pairs={{0,2},{1,3},{2,0},{3,1},{4,6},{5,7},{6,4},{7,5},{8,10},{9,11},{10,... | collective-permute-start | bytes 491528 | tf_op jit(solution)/shard_map/ppermute | solution.py:23
  41.7 8.2 %collective-permute-start.12 = (bf16[8,5120]{1,0:T(8,128)(2,1)S(1)}, bf16[8,5120]{1,0:T(8,128)(2,1)S(1)}, u32[]{:S(2)}, u32[]{:S(2)}) collective-permute-start(bf16[8,5120]{1,0:T(8,128)(2,1)S(1)} %get-tuple-element.31), channel_id=1, source_target_pairs={{0,8},{4,12},{8,0},{12,4},{1,9},{5,13},{9,1},{13,5},{2,10},{6,14},... | collective-permute-start | bytes 245768 | tf_op jit(solution)/shard_map/ppermute | solution.py:23
  44.8 6.7 %collective-permute-start.13 = (bf16[8,5120]{1,0:T(8,128)(2,1)S(1)}, bf16[8,5120]{1,0:T(8,128)(2,1)S(1)}, u32[]{:S(2)}, u32[]{:S(2)}) collective-permute-start(bf16[8,5120]{1,0:T(8,128)(2,1)S(1)} %get-tuple-element.32), channel_id=1, source_target_pairs={{0,12},{4,8},{8,4},{12,0},{1,13},{5,9},{9,5},{13,1},{2,14},{6,10},... | collective-permute-start | bytes 245768 | tf_op jit(solution)/shard_map/ppermute | solution.py:23
  46.3 5.4 %collective-permute-start.9 = (bf16[8,5120]{1,0:T(8,128)(2,1)S(1)}, bf16[8,5120]{1,0:T(8,128)(2,1)S(1)}, u32[]{:S(2)}, u32[]{:S(2)}) collective-permute-start(bf16[8,5120]{1,0:T(8,128)(2,1)S(1)} %fusion.8), channel_id=1, source_target_pairs={{0,4},{4,0},{8,12},{12,8},{1,5},{5,1},{9,13},{13,9},{2,6},{6,2},{1... | collective-permute-start | bytes 245768 | tf_op jit(solution)/shard_map/ppermute | solution.py:23
